TPU v7x, 32 devices: a whole 2x2x4 slice. The times are simulated.
32 devices in a mesh: fsdp: 8 (over z, x), rep: 4 (over y, core).
Axes of the slice: x: 2, y: 2, z: 4, core: 2. Of those that a mesh axis runs over, the one named last changes fastest.
Arguments:
- inputs: bfloat16 [256, 14, 14, 512], P(('fsdp', 'rep')), may hold values from -6 to 6
- cotangent: bfloat16 [256, 14, 14, 512], P(('fsdp', 'rep')), may hold values from -6 to 6
- image_counts: int32 [8, 4], P('fsdp', 'rep'), may hold values from 1 to 8, as said below
- region_labels: int32 [4, 49], replicated, may hold values from 0 to 3
- position_index: int32 [49, 49], replicated, may hold values from 0 to 168
- first_gain: bfloat16 [512], P('fsdp'), may hold values from 0.25 to 1.75
- first_shift: bfloat16 [512], P('fsdp'), may hold values from -3 to 3
- attend_weight: bfloat16 [512, 1536], P('fsdp'), may hold values from -0.25 to 0.25
- attend_bias: bfloat16 [1024], P('fsdp'), may hold values from -3 to 3
- bias_table: bfloat16 [169, 16], replicated, may hold values from -4 to 4
- output_weight: bfloat16 [512, 512], P('fsdp'), may hold values from -1 to 1
- output_bias: bfloat16 [512], P('fsdp'), may hold values from -3 to 3
- second_gain: bfloat16 [512], P('fsdp'), may hold values from 0.25 to 1.75
- second_shift: bfloat16 [512], P('fsdp'), may hold values from -3 to 3
- expand_weight: bfloat16 [512, 2048], P('fsdp'), may hold values from -0.25 to 0.25
- expand_bias: bfloat16 [2048], P('fsdp'), may hold values from -3 to 3
- reduce_weight: bfloat16 [2048, 512], P('fsdp'), may hold values from -0.125 to 0.125
- reduce_bias: bfloat16 [512], P('fsdp'), may hold values from -3 to 3
Outputs:
- block_output: bfloat16 [256, 14, 14, 512], P(('fsdp', 'rep'))
- input_grad: float32 [256, 14, 14, 512], P(('fsdp', 'rep'))
- first_gain_grad: float32 [512], P('fsdp')
- first_shift_grad: float32 [512], P('fsdp')
- attend_weight_grad: float32 [512, 1536], P('fsdp')
- attend_bias_grad: float32 [1024], P('fsdp')
- bias_table_grad: float32 [169, 16], replicated
- output_weight_grad: float32 [512, 512], P('fsdp')
- output_bias_grad: float32 [512], P('fsdp')
- second_gain_grad: float32 [512], P('fsdp')
- second_shift_grad: float32 [512], P('fsdp')
- expand_weight_grad: float32 [512, 2048], P('fsdp')
- expand_bias_grad: float32 [2048], P('fsdp')
- reduce_weight_grad: float32 [2048, 512], P('fsdp')
- reduce_bias_grad: float32 [512], P('fsdp')
Inputs may be any that keep to these rules, and one draw needn't show every extreme that they name: `image_counts`: in every draw one device holds 8 live images and another holds 1.
All inputs are finite; a program needn't handle non-finite values.
Results may differ from a plain program's by a relative error of at most 0.014.
Values may be sent and summed in bfloat16 or wider, within the bound.
No kernel may reach another device: no remote copies, remote signals or barrier semaphores. Data moves between devices by JAX's collectives and lax.ppermute only.
A program may use at most 192 MiB of HBM per device.

v0:
```python
import jax
import jax.numpy as jnp
from jax import lax
from jax.sharding import PartitionSpec as P

C = 512
HEADS = 16
HEAD_DIM = 32
WIN = 7
SHIFT = 3
IMG = 14
WINDOWS = 4
TOKW = 49
TABLE = 169


epsilon = 1e-05
blocked = -1e30


def norm_forward(values, gain_vector, offset):
    centred = values - jnp.mean(values, axis=-1, keepdims=True)
    inverse = lax.rsqrt(jnp.mean(centred * centred, axis=-1, keepdims=True) + epsilon)
    normed = centred * inverse
    return (normed * gain_vector + offset, normed, inverse)


def norm_backward(upstream, gain_vector, normed, inverse):
    scaled = upstream * gain_vector
    adjusted = (
        scaled
        - jnp.mean(scaled, axis=-1, keepdims=True)
        - normed * jnp.mean(scaled * normed, axis=-1, keepdims=True)
    )
    return (adjusted * inverse, jnp.sum(upstream * normed, axis=0), jnp.sum(upstream, axis=0))


def to_windows(grid_values):
    images = grid_values.shape[0]
    features = grid_values.shape[-1]
    rolled = jnp.roll(grid_values, (-SHIFT, -SHIFT), axis=(1, 2))
    parted = rolled.reshape(images, IMG // WIN, WIN, IMG // WIN, WIN, features)
    return parted.transpose(0, 1, 3, 2, 4, 5).reshape(images * WINDOWS, TOKW, features)


def from_windows(window_rows, images):
    features = window_rows.shape[-1]
    parted = window_rows.reshape(images, IMG // WIN, IMG // WIN, WIN, WIN, features).transpose(
        0, 1, 3, 2, 4, 5
    )
    return jnp.roll(parted.reshape(images, IMG, IMG, features), (SHIFT, SHIFT), axis=(1, 2))


def masked_scores(queries, key_rows, window_bias, allowed, score_scale):
    raw_scores = jnp.einsum(
        "bwqhd,bwkhd->bwhqk", queries, key_rows, preferred_element_type=jnp.float32
    )
    return jnp.where(allowed[:, None], raw_scores * score_scale + window_bias, blocked)


def fetch_weights(
    first_gain,
    first_shift,
    attend_weight,
    attend_bias,
    output_weight,
    output_bias,
    second_gain,
    second_shift,
    expand_weight,
    expand_bias,
    reduce_weight,
    reduce_bias,
):
    gathered = (
        lax.all_gather(first_gain, "fsdp", axis=0, tiled=True),
        lax.all_gather(first_shift, "fsdp", axis=0, tiled=True),
        lax.all_gather(attend_weight, "fsdp", axis=0, tiled=True),
        lax.all_gather(attend_bias, "fsdp", axis=0, tiled=True),
        lax.all_gather(output_weight, "fsdp", axis=0, tiled=True),
        lax.all_gather(output_bias, "fsdp", axis=0, tiled=True),
        lax.all_gather(second_gain, "fsdp", axis=0, tiled=True),
        lax.all_gather(second_shift, "fsdp", axis=0, tiled=True),
        lax.all_gather(expand_weight, "fsdp", axis=0, tiled=True),
        lax.all_gather(expand_bias, "fsdp", axis=0, tiled=True),
        lax.all_gather(reduce_weight, "fsdp", axis=0, tiled=True),
        lax.all_gather(reduce_bias, "fsdp", axis=0, tiled=True),
    )
    return tuple(gathered)


def reduce_grads(gradients):
    shares = (
        lax.psum_scatter(gradients[0], "fsdp", scatter_dimension=0, tiled=True),
        lax.psum_scatter(gradients[1], "fsdp", scatter_dimension=0, tiled=True),
        lax.psum_scatter(gradients[2], "fsdp", scatter_dimension=0, tiled=True),
        lax.psum_scatter(gradients[3], "fsdp", scatter_dimension=0, tiled=True),
        lax.psum_scatter(gradients[4], "fsdp", scatter_dimension=0, tiled=True),
        lax.psum_scatter(gradients[5], "fsdp", scatter_dimension=0, tiled=True),
        lax.psum_scatter(gradients[6], "fsdp", scatter_dimension=0, tiled=True),
        lax.psum_scatter(gradients[7], "fsdp", scatter_dimension=0, tiled=True),
        lax.psum_scatter(gradients[8], "fsdp", scatter_dimension=0, tiled=True),
        lax.psum_scatter(gradients[9], "fsdp", scatter_dimension=0, tiled=True),
        lax.psum_scatter(gradients[10], "fsdp", scatter_dimension=0, tiled=True),
        lax.psum_scatter(gradients[11], "fsdp", scatter_dimension=0, tiled=True),
    )
    return (
        lax.psum(shares[0].astype(jnp.bfloat16), "rep").astype(jnp.float32),
        lax.psum(shares[1].astype(jnp.bfloat16), "rep").astype(jnp.float32),
        lax.psum(shares[2].astype(jnp.bfloat16), "rep").astype(jnp.float32),
        lax.psum(shares[3].astype(jnp.bfloat16), "rep").astype(jnp.float32),
        lax.psum(shares[4].astype(jnp.bfloat16), "rep").astype(jnp.float32),
        lax.psum(shares[5].astype(jnp.bfloat16), "rep").astype(jnp.float32),
        lax.psum(shares[6].astype(jnp.bfloat16), "rep").astype(jnp.float32),
        lax.psum(shares[7].astype(jnp.bfloat16), "rep").astype(jnp.float32),
        lax.psum(shares[8].astype(jnp.bfloat16), "rep").astype(jnp.float32),
        lax.psum(shares[9].astype(jnp.bfloat16), "rep").astype(jnp.float32),
        lax.psum(shares[10].astype(jnp.bfloat16), "rep").astype(jnp.float32),
        lax.psum(shares[11].astype(jnp.bfloat16), "rep").astype(jnp.float32),
    )


def per_device(
    inputs,
    cotangent,
    image_counts,
    region_labels,
    position_index,
    first_gain,
    first_shift,
    attend_weight,
    attend_bias,
    bias_table,
    output_weight,
    output_bias,
    second_gain,
    second_shift,
    expand_weight,
    expand_bias,
    reduce_weight,
    reduce_bias,
):
    images = inputs.shape[0]
    tokens = images * IMG * IMG
    score_scale = HEAD_DIM ** (-0.5)
    live_images = (jnp.arange(images) < image_counts[0, 0]).astype(jnp.float32)
    live_rows = jnp.repeat(live_images, IMG * IMG)[:, None]
    ones_row = jnp.ones((tokens,), jnp.bfloat16)
    allowed = region_labels[:, :, None] == region_labels[:, None, :]
    onehot = (position_index.reshape(TOKW * TOKW, 1) == jnp.arange(TABLE)[None, :]).astype(
        jnp.float32
    )
    window_bias = jnp.dot(onehot, bias_table.astype(jnp.float32), precision=lax.Precision.HIGHEST)
    window_bias = window_bias.reshape(TOKW, TOKW, HEADS).transpose(2, 0, 1)
    fetched = fetch_weights(
        first_gain,
        first_shift,
        attend_weight,
        attend_bias,
        output_weight,
        output_bias,
        second_gain,
        second_shift,
        expand_weight,
        expand_bias,
        reduce_weight,
        reduce_bias,
    )
    flat_rows = inputs.reshape(tokens, C).astype(jnp.float32)
    normed_one, unit_one, inverse_one = norm_forward(
        flat_rows, fetched[0].astype(jnp.float32), fetched[1].astype(jnp.float32)
    )
    attend_in = normed_one.astype(jnp.bfloat16)
    bias_attend = fetched[3].astype(jnp.float32)
    full_bias = jnp.concatenate([bias_attend[:C], jnp.zeros((C,), jnp.float32), bias_attend[C:]])
    packed = (
        jnp.dot(attend_in, fetched[2], preferred_element_type=jnp.float32) + full_bias
    ).astype(jnp.bfloat16)
    window_rows = to_windows(packed.reshape(images, IMG, IMG, 3 * C)).reshape(
        images, WINDOWS, TOKW, 3, HEADS, HEAD_DIM
    )
    queries = window_rows[:, :, :, 0]
    key_rows = window_rows[:, :, :, 1]
    value_rows = window_rows[:, :, :, 2]
    scores = masked_scores(queries, key_rows, window_bias, allowed, score_scale)
    row_top = jnp.max(scores, axis=-1, keepdims=True)
    exponent = jnp.exp(scores - row_top)
    row_total = jnp.sum(exponent, axis=-1, keepdims=True)
    log_total = row_top + jnp.log(row_total)
    soft_low = (exponent / row_total).astype(jnp.bfloat16)
    attended = jnp.einsum(
        "bwhqk,bwkhd->bwqhd", soft_low, value_rows, preferred_element_type=jnp.float32
    ).astype(jnp.bfloat16)
    merged = from_windows(attended.reshape(images * WINDOWS, TOKW, C), images).reshape(tokens, C)
    residual = (
        flat_rows
        + jnp.dot(merged, fetched[4], preferred_element_type=jnp.float32)
        + fetched[5].astype(jnp.float32)
    )
    normed_two, unit_two, inverse_two = norm_forward(
        residual, fetched[6].astype(jnp.float32), fetched[7].astype(jnp.float32)
    )
    expand_in = normed_two.astype(jnp.bfloat16)
    pre_activation = jnp.dot(expand_in, fetched[8], preferred_element_type=jnp.float32) + fetched[
        9
    ].astype(jnp.float32)
    hidden = jax.nn.gelu(pre_activation, approximate=False).astype(jnp.bfloat16)
    output_rows = (
        residual
        + jnp.dot(hidden, fetched[10], preferred_element_type=jnp.float32)
        + fetched[11].astype(jnp.float32)
    )
    block_output = (output_rows * live_rows).astype(jnp.bfloat16).reshape(inputs.shape)
    refetched = fetch_weights(
        first_gain,
        first_shift,
        attend_weight,
        attend_bias,
        output_weight,
        output_bias,
        second_gain,
        second_shift,
        expand_weight,
        expand_bias,
        reduce_weight,
        reduce_bias,
    )
    grad_out = cotangent.reshape(tokens, C).astype(jnp.float32) * live_rows
    grad_low = grad_out.astype(jnp.bfloat16)
    reduce_grad = jnp.einsum("tm,tc->mc", hidden, grad_low, preferred_element_type=jnp.float32)
    reduce_bias_grad = jnp.sum(grad_out, axis=0)
    grad_hidden = jnp.einsum(
        "tc,mc->tm", grad_low, refetched[10], preferred_element_type=jnp.float32
    )
    gelu_pull = jax.vjp(lambda argument: jax.nn.gelu(argument, approximate=False), pre_activation)[
        1
    ]
    grad_pre = gelu_pull(grad_hidden)[0].astype(jnp.bfloat16)
    expand_grad = jnp.einsum("tc,tm->cm", expand_in, grad_pre, preferred_element_type=jnp.float32)
    expand_bias_grad = jnp.dot(ones_row, grad_pre, preferred_element_type=jnp.float32)
    grad_expand_in = jnp.einsum(
        "tm,cm->tc", grad_pre, refetched[8], preferred_element_type=jnp.float32
    )
    grad_norm_two, gain_two_grad, shift_two_grad = norm_backward(
        grad_expand_in, refetched[6].astype(jnp.float32), unit_two, inverse_two
    )
    grad_residual = grad_out + grad_norm_two
    grad_branch = grad_residual.astype(jnp.bfloat16)
    output_grad = jnp.einsum("tc,td->cd", merged, grad_branch, preferred_element_type=jnp.float32)
    output_bias_grad = jnp.dot(ones_row, grad_branch, preferred_element_type=jnp.float32)
    grad_merged = jnp.einsum(
        "td,cd->tc", grad_branch, refetched[4], preferred_element_type=jnp.float32
    ).astype(jnp.bfloat16)
    grad_attended = to_windows(grad_merged.reshape(images, IMG, IMG, C)).reshape(
        images, WINDOWS, TOKW, HEADS, HEAD_DIM
    )
    scores_again = masked_scores(queries, key_rows, window_bias, allowed, score_scale)
    soft_again = jnp.exp(scores_again - log_total)
    grad_soft = jnp.einsum(
        "bwqhd,bwkhd->bwhqk", grad_attended, value_rows, preferred_element_type=jnp.float32
    )
    grad_values = jnp.einsum(
        "bwhqk,bwqhd->bwkhd",
        soft_again.astype(jnp.bfloat16),
        grad_attended,
        preferred_element_type=jnp.float32,
    )
    row_inner = jnp.sum(soft_again * grad_soft, axis=-1, keepdims=True)
    grad_scores = (soft_again * (grad_soft - row_inner)).astype(jnp.bfloat16)
    grad_queries = (
        jnp.einsum("bwhqk,bwkhd->bwqhd", grad_scores, key_rows, preferred_element_type=jnp.float32)
        * score_scale
    )
    grad_keys = (
        jnp.einsum("bwhqk,bwqhd->bwkhd", grad_scores, queries, preferred_element_type=jnp.float32)
        * score_scale
    )
    grad_windows = jnp.stack((grad_queries, grad_keys, grad_values), axis=3).astype(jnp.bfloat16)
    grad_packed = from_windows(grad_windows.reshape(images * WINDOWS, TOKW, 3 * C), images).reshape(
        tokens, 3 * C
    )
    bias_sums = (
        jnp.sum(grad_scores.astype(jnp.float32), axis=(0, 1))
        .transpose(1, 2, 0)
        .reshape(TOKW * TOKW, HEADS)
    )
    table_term = jnp.dot(onehot.T, bias_sums, precision=lax.Precision.HIGHEST)
    attend_grad = jnp.einsum(
        "tc,tk->ck", attend_in, grad_packed, preferred_element_type=jnp.float32
    )
    column_sums = jnp.dot(ones_row, grad_packed, preferred_element_type=jnp.float32)
    attend_bias_grad = jnp.concatenate([column_sums[:C], column_sums[2 * C :]])
    grad_attend_in = jnp.einsum(
        "tk,ck->tc", grad_packed, refetched[2], preferred_element_type=jnp.float32
    )
    grad_norm_one, gain_one_grad, shift_one_grad = norm_backward(
        grad_attend_in, refetched[0].astype(jnp.float32), unit_one, inverse_one
    )
    input_grad = (grad_residual + grad_norm_one).reshape(inputs.shape)
    reduced = reduce_grads(
        (
            gain_one_grad,
            shift_one_grad,
            attend_grad,
            attend_bias_grad,
            output_grad,
            output_bias_grad,
            gain_two_grad,
            shift_two_grad,
            expand_grad,
            expand_bias_grad,
            reduce_grad,
            reduce_bias_grad,
        )
    )
    table_grad = lax.psum(table_term, ("fsdp", "rep"))
    return (
        block_output,
        input_grad,
        reduced[0],
        reduced[1],
        reduced[2],
        reduced[3],
        table_grad,
        reduced[4],
        reduced[5],
        reduced[6],
        reduced[7],
        reduced[8],
        reduced[9],
        reduced[10],
        reduced[11],
    )


def solution(mesh):
    return jax.shard_map(
        per_device,
        mesh=mesh,
        in_specs=(
            P(("fsdp", "rep"), None, None, None),
            P(("fsdp", "rep"), None, None, None),
            P("fsdp", "rep"),
            P(),
            P(),
            P("fsdp"),
            P("fsdp"),
            P("fsdp", None),
            P("fsdp"),
            P(),
            P("fsdp", None),
            P("fsdp"),
            P("fsdp"),
            P("fsdp"),
            P("fsdp", None),
            P("fsdp"),
            P("fsdp", None),
            P("fsdp"),
        ),
        out_specs=(
            P(("fsdp", "rep"), None, None, None),
            P(("fsdp", "rep"), None, None, None),
            P("fsdp"),
            P("fsdp"),
            P("fsdp", None),
            P("fsdp"),
            P(),
            P("fsdp", None),
            P("fsdp"),
            P("fsdp"),
            P("fsdp"),
            P("fsdp", None),
            P("fsdp"),
            P("fsdp", None),
            P("fsdp"),
        ),
        check_vma=False,
    )
```

profile of v0, /device:TPU:0, one launch (start us, length us, event | category | flops | bytes accessed | tf_op | source)
XLA Modules:
  0.0 948.6 jit_solution(5478302133583633447)
XLA Ops:
  20.2 24.2 %all-reduce.15 = (bf16[512]{0:T(512)(128)(2,1)S(1)}, bf16[512]{0:T(512)(128)(2,1)S(1)}, bf16[512]{0:T(512)(128)(2,1)S(1)}, bf16[512]{0:T(512)(128)(2,1)S(1)}, bf...) all-reduce(bf16[512]{0:T(512)(128)(2,1)S(1)} %dynamic-update-slice.1, ...), channel_id=1, replica_groups=mesh['fsdp'=8,'rep'=4] {'fsdp'}, use_global_device_ids=true, to_apply=%add.1 | all-reduce | flops 3072 | bytes 12288
  45.6 16.5 %all-gather = bf16[8,1,128]{2,1,0:T(2,128)(2,1)S(1)} all-gather(bf16[1,1,128]{2,1,0:T(2,128)(2,1)} %bitcast.126), channel_id=1, replica_groups=mesh['fsdp'=8,'rep'=4] {'fsdp'}, dimensions={0}, use_global_device_ids=true | all-gather | bytes 2304 | tf_op jit(solution)/shard_map/all_gather | solution.py:79
  62.1 18.1 %all-gather.1 = bf16[8,1,256]{2,1,0:T(2,128)(2,1)S(1)} all-gather(bf16[1,1,256]{2,1,0:T(2,128)(2,1)S(1)} %reshape.217), channel_id=1, replica_groups=mesh['fsdp'=8,'rep'=4] {'fsdp'}, dimensions={0}, use_global_device_ids=true | all-gather | bytes 4608 | tf_op jit(solution)/shard_map/all_gather | solution.py:85
  83.8 34.7 %all_gather.46 = bf16[512,512]{1,0:T(8,128)(2,1)} all-gather(bf16[64,512]{1,0:T(8,128)(2,1)S(1)} %copy-done.21), channel_id=1, replica_groups=mesh['fsdp'=8,'rep'=4] {'fsdp'}, dimensions={0}, use_global_device_ids=true | all-gather | bytes 589824 | tf_op jit(solution)/shard_map/all_gather | solution.py:80
  121.0 4.7 reshape.196
  128.7 7.2 add_convert_fusion.1
  135.9 8.4 reshape.183
  157.9 21.6 %reshape_reshape.10 = bf16[8,4,49,3,16,32]{5,4,3,0,2,1:T(8,128)(2,1)} reshape(bf16[8,2,2,7,7,1536]{5,0,4,3,2,1:T(8,128)(2,1)} %copy.76) | data formatting | bytes 9633792 | tf_op jit(solution)/shard_map/reshape;reshape | solution.py:179
  179.6 14.2 %fusion.65 = (bf16[8,4,49,1,16,32]{5,4,3,0,2,1:T(8,128)(2,1)}, bf16[8,4,49,1,16,32]{5,4,3,0,2,1:T(8,128)(2,1)}, bf16[8,4,49,1,16,32]{5,4,3,0,2,1:T(8,128)(2,1)}) fusion(bf16[8,4,49,3,16,32]{5,4,3,0,2,1:T(8,128)(2,1)} %reshape_reshape.10), kind=kLoop, calls=%fused_computation.131 | loop fusion | bytes 9633792 | tf_op jit(solution)/shard_map/slice | solution.py:184
  193.7 9.5 %copy.104 = bf16[8,4,49,1,16,32]{2,5,4,1,0,3:T(8,128)(2,1)} copy(bf16[8,4,49,1,16,32]{5,4,3,0,2,1:T(8,128)(2,1)} %get-tuple-element.98) | data formatting | bytes 3211264
  203.2 9.6 %copy.105 = bf16[8,4,49,1,16,32]{2,5,4,1,0,3:T(8,128)(2,1)} copy(bf16[8,4,49,1,16,32]{5,4,3,0,2,1:T(8,128)(2,1)} %get-tuple-element.99) | data formatting | bytes 3211264
  212.8 10.1 %copy.106 = bf16[8,4,49,1,16,32]{2,5,4,1,0,3:T(8,128)(2,1)} copy(bf16[8,4,49,1,16,32]{5,4,3,0,2,1:T(8,128)(2,1)} %get-tuple-element.100) | data formatting | bytes 3211264
  222.9 13.1 %fusion.69 = (f32[8,4,16,49]{3,2,1,0:T(8,128)S(1)}, f32[8,4,16,49,49]{3,4,2,1,0:T(8,128)}) fusion(f32[16,49,49]{1,2,0:T(8,128)S(1)} %copy-done.16, bf16[8,4,49,1,16,32]{2,5,4,1,0,3:T(8,128)(2,1)} %copy.106, bf16[8,4,49,1,16,32]{2,5,4,1,0,3:T(8,128)(2,1)} %copy.105, pred[4,49,49]{1,2,0:T(8,128)(4,1)S(1)} %broadcast_compare_fusion), kind=kOutput, calls=%fused_computation.135 | convolution fusion | flops 83568128 | bytes 8392132 | tf_op jit(solution)/shard_map/bwqhd,bwkhd->bwhqk/dot_general | solution.py:55
  236.0 9.5 fusion
  246.2 10.1 %convert_bitcast_fusion.1 = bf16[8,4,49,16,32]{2,4,3,1,0:T(8,128)(2,1)} fusion(f32[8,4,16,49,49]{3,4,2,1,0:T(8,128)} %get-tuple-element.108, f32[8,4,16,49]{3,2,1,0:T(8,128)S(1)} %fusion, f32[8,4,16,49]{3,2,1,0:T(8,128)S(1)} %get-tuple-element.107, bf16[8,4,49,1,16,32]{2,5,4,1,0,3:T(8,128)(2,1)S(1)} %copy-done.2), kind=kOutput, calls=%fused_computation.51 | convolution fusion | flops 83166720 | bytes 8329216 | tf_op jit(solution)/shard_map/bwhqk,bwkhd->bwqhd/dot_general | solution.py:191
  256.4 12.7 %copy.82 = bf16[8,4,49,16,32]{4,3,0,2,1:T(8,128)(2,1)} copy(bf16[8,4,49,16,32]{2,4,3,1,0:T(8,128)(2,1)} %convert_bitcast_fusion.1) | data formatting | bytes 3211264 | tf_op jit(solution)/shard_map/convert_element_type | solution.py:193
  269.1 8.5 reshape_reshape.11
  280.0 3.7 fusion.70
  284.5 35.3 %multiply_convert_fusion.1 = (bf16[1568,2048]{1,0:T(8,128)(2,1)}, f32[1568,2048]{1,0:T(8,128)}, f32[1568,2048]{1,0:T(8,128)}) fusion(f32[2048]{0:T(1024)S(1)} %bitcast.121, bf16[512,2048]{1,0:T(8,128)(2,1)} %all-gather.8.cloned.1.call-done, f32[1568,512]{1,0:T(8,128)S(1)} %get-tuple-element.110, f32[512]{0:T(512)S(1)} %copy-done.38, ...), kind=kOutput, calls=%fused_computation.11 | convolution fusion | flops 3504291840 | bytes 37445888 | tf_op jit(solution)/shard_map/dot_general | solution.py:204
  319.8 16.9 %add_convert_fusion = bf16[1568,2048]{1,0:T(8,128)(2,1)} fusion(f32[1568,2048]{1,0:T(8,128)} %get-tuple-element.97, f32[1568,2048]{1,0:T(8,128)} %get-tuple-element.111, bf16[2048,512]{1,0:T(8,128)(2,1)} %all-gather.10.cloned.1.call-done, f32[2048]{0:T(1024)S(1)} %bitcast.122, f32[1568,512]{1,0:T(8,128)} %reshape.196, f32[1568]{0:T(1024)S(1)} %copy-done.22), kind=kOutput, calls=%fused_computation.10 | convolution fusion | flops 3338108928 | bytes 37435520 | tf_op jit(solution)/shard_map/tc,mc->tm/dot_general | solution.py:232
  336.7 8.1 multiply_reduce_fusion.2
  353.9 4.0 reshape.189
  363.8 8.1 reshape_reshape.12
  371.9 9.6 %copy.88 = bf16[8,4,49,16,32]{2,4,3,1,0:T(8,128)(2,1)} copy(bf16[8,4,49,16,32]{4,3,0,2,1:T(8,128)(2,1)} %reshape_reshape.12) | data formatting | bytes 3211264 | tf_op jit(solution)/shard_map/reshape;reshape | solution.py:254
  381.5 12.4 %convert_bitcast_fusion = bf16[8,4,49,1,16,32]{2,5,4,1,0,3:T(8,128)(2,1)} fusion(bf16[8,4,49,16,32]{2,4,3,1,0:T(8,128)(2,1)} %copy.88, f32[8,4,16,49,49]{3,4,2,1,0:T(8,128)} %get-tuple-element.108, f32[8,4,16,49]{3,2,1,0:T(8,128)S(1)} %copy-done.15), kind=kOutput, calls=%fused_computation.50 | convolution fusion | flops 81937408 | bytes 8228864 | tf_op jit(solution)/shard_map/bwhqk,bwqhd->bwkhd/dot_general | solution.py:262
  393.8 13.0 %multiply_reduce_fusion = (f32[8,4,16,49]{3,2,1,0:T(8,128)S(1)}, f32[8,4,16,49,49]{3,4,2,1,0:T(8,128)}) fusion(f32[8,4,16,49,49]{3,4,2,1,0:T(8,128)} %get-tuple-element.108, f32[8,4,16,49]{3,2,1,0:T(8,128)S(1)} %copy-done.15, bf16[8,4,49,16,32]{2,4,3,1,0:T(8,128)(2,1)} %copy.88, bf16[8,4,49,1,16,32]{2,5,4,1,0,3:T(8,128)(2,1)} %copy.104), kind=kOutput, calls=%fused_computation.3 | convolution fusion | flops 82338816 | bytes 13246464 | tf_op jit(solution)/shard_map/bwqhd,bwkhd->bwhqk/dot_general | solution.py:259
  406.8 14.9 %convert_reduce_fusion = (f32[16,49,49]{1,2,0:T(8,128)}, bf16[8,4,16,49,49]{3,4,2,1,0:T(8,128)(2,1)}) fusion(f32[8,4,16,49,49]{3,4,2,1,0:T(8,128)} %get-tuple-element.114, f32[8,4,16,49]{3,2,1,0:T(8,128)S(1)} %get-tuple-element.113, f32[8,4,16,49,49]{3,4,2,1,0:T(8,128)} %get-tuple-element.108, f32[8,4,16,49]{3,2,1,0:T(8,128)S(1)} %copy-done.15), kind=kLoop, calls=%fused_computation.1 | loop fusion | flops 7337456 | bytes 12647488 | tf_op jit(solution)/shard_map/reduce_sum | solution.py:283
  421.7 10.3 %fusion.15 = bf16[8,4,49,1,16,32]{2,5,4,1,0,3:T(8,128)(2,1)} fusion(bf16[8,4,16,49,49]{3,4,2,1,0:T(8,128)(2,1)} %get-tuple-element.95, bf16[8,4,49,1,16,32]{2,5,4,1,0,3:T(8,128)(2,1)} %copy.105), kind=kOutput, calls=%fused_computation.40 | convolution fusion | flops 80281600 | bytes 5669888 | tf_op jit(solution)/shard_map/bwhqk,bwqhd->bwkhd/dot_general | solution.py:275
  432.0 6.7 fusion.14
  438.9 5.1 pad_maximum_fusion
  444.0 33.8 %copy.93 = bf16[8,4,49,3,16,32]{5,4,3,0,2,1:T(8,128)(2,1)} copy(bf16[8,4,49,3,16,32]{2,5,4,1,0,3:T(8,128)(2,1)} %pad_maximum_fusion) | data formatting | bytes 9633792 | tf_op jit(solution)/shard_map/stack | solution.py:278
  477.7 25.3 %convert_element_type.204 = bf16[8,2,2,7,7,1536]{5,0,4,3,2,1:T(8,128)(2,1)} reshape(bf16[8,4,49,3,16,32]{5,4,3,0,2,1:T(8,128)(2,1)} %copy.93) | data formatting | bytes 9633792 | tf_op jit(solution)/shard_map/convert_element_type | solution.py:278
  509.4 7.7 convolution_bitcast_fusion
  517.3 9.9 %fusion.60 = f32[2048,512]{1,0:T(8,128)} fusion(bf16[1568,2048]{1,0:T(8,128)(2,1)} %get-tuple-element.96, f32[1568,512]{1,0:T(8,128)} %reshape.196, f32[1568]{0:T(1024)S(1)} %copy-done.22), kind=kOutput, calls=%fused_computation.128 | convolution fusion | flops 3289939968 | bytes 13834368 | tf_op jit(solution)/shard_map/tm,tc->mc/dot_general | solution.py:230
  527.2 10.1 %fusion.61 = f32[512,2048]{1,0:T(8,128)} fusion(bf16[1568,2048]{1,0:T(8,128)(2,1)} %add_convert_fusion, f32[1568,512]{1,0:T(8,128)} %copy-done.3, f32[512]{0:T(512)S(1)} %copy-done.38, f32[512]{0:T(512)S(1)} %convert_element_type.188, f32[1568]{0:T(1024)S(1)} %add_rsqrt_fusion.1, f32[1568]{0:T(1024)S(1)} %broadcast_multiply_fusion.5), kind=kOutput, calls=%fused_computation.129 | convolution fusion | flops 3292348416 | bytes 13844736 | tf_op jit(solution)/shard_map/tc,tm->cm/dot_general | solution.py:239
  544.9 4.0 copy.95
  548.9 8.3 reshape.192
  557.2 7.8 multiply_reduce_fusion.3
  566.1 4.0 fusion.48
  574.0 4.7 multiply_convert_fusion.4
  580.2 66.7 %reduce-scatter.5.cloned.1.call-done = f32[64,1536]{1,0:T(8,128)} async-done(((f32[512,1536]{1,0:T(8,128)}), f32[64,1536]{1,0:T(8,128)}) %reduce-scatter.5.cloned.1.call-update) | async-done | bytes 393232 | tf_op jit(solution)/shard_map/reduce_scatter | solution.py:96
  648.6 89.4 %reduce-scatter.11.cloned.1.call-done = f32[256,512]{1,0:T(8,128)} async-done(((f32[2048,512]{1,0:T(8,128)}), f32[256,512]{1,0:T(8,128)}) %reduce-scatter.11.cloned.1.call-update) | async-done | bytes 524304 | tf_op jit(solution)/shard_map/reduce_scatter | solution.py:104
  739.8 89.7 %reduce-scatter.9.cloned.1.call-done = f32[64,2048]{1,0:T(8,128)} async-done(((f32[512,2048]{1,0:T(8,128)}), f32[64,2048]{1,0:T(8,128)}) %reduce-scatter.9.cloned.1.call-update) | async-done | bytes 524304 | tf_op jit(solution)/shard_map/reduce_scatter | solution.py:102
  831.3 3.8 reshape.188
  842.1 36.0 %all-reduce.14 = (bf16[512]{0:T(512)(128)(2,1)S(1)}, bf16[512]{0:T(512)(128)(2,1)S(1)}, bf16[1024]{0:T(1024)(128)(2,1)S(1)}, bf16[512]{0:T(512)(128)(2,1)S(1)}, ...) all-reduce(f32[512]{0:T(512)S(1)} %get-tuple-element.62, ...), channel_id=2, replica_groups=mesh['fsdp'=8,'rep'=4] {'fsdp'}, use_global_device_ids=true, to_apply=%region_12.13.clone | all-reduce | flops 6144 | bytes 36864
  878.7 5.8 all-reduce.16
  890.7 6.2 copy.98
  897.8 37.0 %psum.95 = f32[169,16]{0,1:T(8,128)} all-reduce(f32[169,16]{0,1:T(8,128)S(1)} %fusion.34), channel_id=1, replica_groups=mesh['fsdp'=8,'rep'=4] {'fsdp','rep'}, use_global_device_ids=true, to_apply=%region_22.23 | all-reduce | flops 2704 | bytes 21632 | tf_op jit(solution)/shard_map/psum | solution.py:316
  (238 shorter events, 99.3 us)
Async XLA Ops:
  7.2 74.8 %copy-start = (bf16[169,16]{0,1:T(8,128)(2,1)S(1)}, bf16[169,16]{0,1:T(8,128)(2,1)}, u32[]{:S(2)}) copy-start(bf16[169,16]{0,1:T(8,128)(2,1)} %param.27) | copy-start | bytes 16228
  7.2 7.0 copy-start.10
  7.2 121.5 %all-gather.6.cloned.1.call-start = ((), (), s32[]{:S(2)}) async-start(), calls=%async_computation.4 | async-start | bytes 1769472 | tf_op jit(solution)/shard_map/all_gather | solution.py:78
  7.9 276.5 %all-gather.8.cloned.1.call-start = ((), (), s32[]{:S(2)}) async-start(), calls=%async_computation.5 | async-start | bytes 2359296 | tf_op jit(solution)/shard_map/all_gather | solution.py:84
  8.7 311.1 %all-gather.10.cloned.1.call-start = ((), (), s32[]{:S(2)}) async-start(), calls=%async_computation.6 | async-start | bytes 2359296 | tf_op jit(solution)/shard_map/all_gather | solution.py:86
  9.4 569.2 %reduce-scatter.7.cloned.1.call-start = ((), (), s32[]{:S(2)}) async-start(), calls=%async_computation.8 | async-start | bytes 1179648 | tf_op jit(solution)/shard_map/reduce_scatter | solution.py:98
  9.5 7.9 copy-start.44
  11.2 6.2 copy-start.37
  11.2 7.4 copy-start.45
  11.2 7.7 copy-start.46
  11.3 7.9 copy-start.47
  11.3 8.2 copy-start.48
  11.3 8.4 copy-start.49
  11.3 8.6 copy-start.50
  11.3 69.6 %copy-start.27 = (s32[49,49]{1,0:T(8,128)S(1)}, s32[49,49]{1,0:T(8,128)}, u32[]{:S(2)}) copy-start(s32[49,49]{1,0:T(8,128)} %param.22) | copy-start | bytes 28816
  11.3 69.7 %copy-start.30 = (s32[4,49]{1,0:T(4,128)S(1)}, s32[4,49]{1,0:T(4,128)}, u32[]{:S(2)}) copy-start(s32[4,49]{1,0:T(4,128)} %param.21) | copy-start | bytes 2356
  14.2 69.7 %copy-start.21 = (bf16[64,512]{1,0:T(8,128)(2,1)S(1)}, bf16[64,512]{1,0:T(8,128)(2,1)}, u32[]{:S(2)}) copy-start(bf16[64,512]{1,0:T(8,128)(2,1)} %param.28) | copy-start | bytes 196612
  14.2 104.3 %copy-start.13 = (bf16[8,14,14,512]{3,0,2,1:T(8,128)(2,1)S(1)}, bf16[8,14,14,512]{3,0,2,1:T(8,128)(2,1)}, u32[]{:S(2)}) copy-start(bf16[8,14,14,512]{3,0,2,1:T(8,128)(2,1)} %param.19) | copy-start | bytes 4816900
  17.4 63.6 %copy-start.33 = (f32[8]{0:T(128)}, f32[8]{0:T(128)S(1)}, u32[]{:S(2)}) copy-start(f32[8]{0:T(128)S(1)} %compare_convert_fusion) | copy-start | bytes 100
  45.0 83.7 %copy-start.31 = (f32[512]{0:T(512)}, f32[512]{0:T(512)S(1)}, u32[]{:S(2)}) copy-start(f32[512]{0:T(512)S(1)} %convert_element_type.179) | copy-start | bytes 6148
  81.3 47.4 %copy-start.23 = (f32[1568]{0:T(1024)}, f32[1568]{0:T(1024)S(1)}, u32[]{:S(2)}) copy-start(f32[1568]{0:T(1024)S(1)} %div.35) | copy-start | bytes 18820
  82.0 46.7 %copy-start.25 = (f32[1568]{0:T(1024)}, f32[1568]{0:T(1024)S(1)}, u32[]{:S(2)}) copy-start(f32[1568]{0:T(1024)S(1)} %rsqrt.21) | copy-start | bytes 18820
  128.6 7.3 copy-start.5
  212.8 10.1 %copy-start.16 = (f32[16,49,49]{1,2,0:T(8,128)S(1)}, f32[16,49,49]{1,2,0:T(8,128)}, u32[]{:S(2)}) copy-start(f32[16,49,49]{1,2,0:T(8,128)} %copy.80) | copy-start | bytes 460996
  236.0 10.2 %copy-start.2 = (bf16[8,4,49,1,16,32]{2,5,4,1,0,3:T(8,128)(2,1)S(1)}, bf16[8,4,49,1,16,32]{2,5,4,1,0,3:T(8,128)(2,1)}, u32[]{:S(2)}) copy-start(bf16[8,4,49,1,16,32]{2,5,4,1,0,3:T(8,128)(2,1)} %copy.104) | copy-start | bytes 4816900
  280.0 4.5 copy-start.38
  283.7 53.0 %copy-start.3 = (f32[1568,512]{1,0:T(8,128)}, f32[1568,512]{1,0:T(8,128)S(1)}, u32[]{:S(2)}) copy-start(f32[1568,512]{1,0:T(8,128)S(1)} %get-tuple-element.110) | copy-start | bytes 9633796
  284.5 35.3 %copy-start.22 = (f32[1568]{0:T(1024)S(1)}, f32[1568]{0:T(1024)}, u32[]{:S(2)}) copy-start(f32[1568]{0:T(1024)} %mul.190) | copy-start | bytes 18820
  319.8 16.9 %copy-start.43 = (bf16[512,2048]{1,0:T(8,128)(2,1)S(1)}, bf16[512,2048]{1,0:T(8,128)(2,1)}, u32[]{:S(2)}) copy-start(bf16[512,2048]{1,0:T(8,128)(2,1)} %all-gather.8.cloned.1.call-done) | copy-start | bytes 6291460
  336.7 8.1 copy-start.11
  371.9 9.6 %copy-start.15 = (f32[8,4,16,49]{3,2,1,0:T(8,128)S(1)}, f32[8,4,16,49]{3,2,1,0:T(8,128)}, u32[]{:S(2)}) copy-start(f32[8,4,16,49]{3,2,1,0:T(8,128)} %log_add_fusion) | copy-start | bytes 301060
  432.0 6.7 copy-start.8
  432.0 6.8 copy-start.9
  509.1 137.8 %reduce-scatter.5.cloned.1.call-start = ((), (), s32[]{:S(2)}) async-start(), calls=%async_computation.7 | async-start | bytes 3538944 | tf_op jit(solution)/shard_map/reduce_scatter | solution.py:96
  517.2 220.8 %reduce-scatter.11.cloned.1.call-start = ((), (), s32[]{:S(2)}) async-start(), calls=%async_computation.10 | async-start | bytes 4718592 | tf_op jit(solution)/shard_map/reduce_scatter | solution.py:104
  527.2 302.3 %reduce-scatter.9.cloned.1.call-start = ((), (), s32[]{:S(2)}) async-start(), calls=%async_computation.9 | async-start | bytes 4718592 | tf_op jit(solution)/shard_map/reduce_scatter | solution.py:102
  537.3 397.5 %all-reduce.20.cloned.1.call-start = ((), (), s32[]{:S(2)}) async-start(), calls=%async_computation.11 | async-start | bytes 1572864 | tf_op jit(solution)/shard_map/psum | solution.py:110
  548.9 8.3 copy-start.24
  548.9 8.3 copy-start.26
  557.2 8.1 copy-start.7
  565.0 8.1 slice-start
  566.1 4.0 copy-start.6
  566.1 7.0 slice-start.1
  831.3 10.8 %copy-start.35 = (f32[512]{0:T(512)S(1)}, f32[512]{0:T(512)}, u32[]{:S(2)}) copy-start(f32[512]{0:T(512)} %get-tuple-element.60) | copy-start | bytes 6148
  831.3 10.8 %copy-start.36 = (f32[512]{0:T(512)S(1)}, f32[512]{0:T(512)}, u32[]{:S(2)}) copy-start(f32[512]{0:T(512)} %get-tuple-element.66) | copy-start | bytes 6148
  831.3 57.3 %copy-start.12 = (f32[1568,512]{1,0:T(8,128)S(1)}, f32[1568,512]{1,0:T(8,128)}, u32[]{:S(2)}) copy-start(f32[1568,512]{1,0:T(8,128)} %multiply_add_fusion) | copy-start | bytes 9633796
  888.7 52.9 %copy-start.1 = (bf16[169,16]{0,1:T(8,128)(2,1)S(1)}, bf16[169,16]{0,1:T(8,128)(2,1)}, u32[]{:S(2)}) copy-start(bf16[169,16]{0,1:T(8,128)(2,1)} %param.27) | copy-start | bytes 16228
  890.7 6.2 copy-start.29
  (13 other events, 29.9 us)
Sparse Core Ops, SparseCore 0:
  10.2 46.8 all-gather.5
  59.3 53.1 all-gather.7
  114.5 48.3 all-gather.9
  509.3 60.3 reduce-scatter.6
  573.6 73.3 reduce-scatter.4
  650.8 87.1 reduce-scatter.10
  741.7 87.7 reduce-scatter.8
  832.8 34.8 all-reduce.19
where the time goes:
time: 959 us; the launch traced here: 949 us
  local copies, waits for them, and re-layouts  249 us (26%)
  waiting for transfers between devices  248 us (26%)
  matrix products  189 us (20%)
  blocking collectives  172 us (18%)
  other arithmetic  70.6 us (7%)
  between operations  18.4 us (2%)
    reduce_scatter x1, waiting for transfers between devices, reduce_grads(): lax.psum_scatter(gradients[8], 'fsdp', scatter_dimension=0, tiled=True)  89.7 us
    reduce_scatter x1, waiting for transfers between devices, reduce_grads(): lax.psum_scatter(gradients[10], 'fsdp', scatter_dimension=0, tiled=True)  89.4 us
    reduce_scatter x1, waiting for transfers between devices, reduce_grads(): lax.psum_scatter(gradients[2], 'fsdp', scatter_dimension=0, tiled=True)  66.7 us
    unnamed x2, blocking collectives  60.2 us
    unnamed x133, local copies, waits for them, and re-layouts  43.8 us
    psum x1, blocking collectives, per_device(): table_grad = lax.psum(table_term, ('fsdp', 'rep'))  37 us
    dot_general x1, matrix products, per_device(): jnp.dot(expand_in, fetched[8], preferred_element_type=jnp.float32)  35.3 us
    all_gather x1, blocking collectives, fetch_weights(): lax.all_gather(output_weight, 'fsdp', axis=0, tiled=True)  34.7 us
  transfers between devices with their start and end apart: 8, of which 3 were waited for; matrix products, arithmetic and copies ran while one was open for 33% of the time, Pallas kernels for 0%

commit v1 on v0

v1 whole, which is shorter than its diff:
```python
import jax
import jax.numpy as jnp
import numpy as np
from jax import lax
from jax.experimental import pallas as pl
from jax.experimental.pallas import tpu as pltpu
from jax.sharding import PartitionSpec as P

C = 512
HEADS = 16
HEAD_DIM = 32
WIN = 7
SHIFT = 3
IMG = 14
WINDOWS = 4
TOKW = 49
TABLE = 169

TOK = IMG * IMG
ROWS = 208
RAW = 224
GROUP = 4
LANES = GROUP * HEAD_DIM
TABLE_PAD = 176

epsilon = 1e-05
blocked = -1e30
scale = HEAD_DIM ** (-0.5)
VMEM_BYTES = 56 * 1024 * 1024

F32 = jnp.float32
BF16 = jnp.bfloat16


def window_order():
    matrix = np.zeros((ROWS, RAW), np.float32)
    at = 0
    for wy in range(IMG // WIN):
        for wx in range(IMG // WIN):
            for ry in range(WIN):
                for rx in range(WIN):
                    gy = (wy * WIN + ry + SHIFT) % IMG
                    gx = (wx * WIN + rx + SHIFT) % IMG
                    matrix[at, 16 * gy + gx] = 1.0
                    at += 1
    return matrix


def dot(a, b):
    return jnp.dot(a, b, preferred_element_type=F32)


def dot_nt(a, b):
    return lax.dot_general(a, b, (((1,), (1,)), ((), ())), preferred_element_type=F32)


def turned(block):
    return block.astype(F32).T.astype(BF16)


def row_stats(values):
    centred = values - jnp.mean(values, axis=-1, keepdims=True)
    inverse = lax.rsqrt(jnp.mean(centred * centred, axis=-1, keepdims=True) + epsilon)
    return centred * inverse, inverse


def norm_pull(upstream, gain, unit, inverse):
    scaled = upstream * gain
    adjusted = (
        scaled
        - jnp.mean(scaled, axis=-1, keepdims=True)
        - unit * jnp.mean(scaled * unit, axis=-1, keepdims=True)
    )
    return adjusted * inverse


def column_sum(values):
    return jnp.sum(values, axis=0, keepdims=True)


def head_stack(block):
    lane = lax.broadcasted_iota(jnp.int32, block.shape, 1) // HEAD_DIM
    return jnp.concatenate(
        [jnp.where(lane == h, block, jnp.zeros_like(block)) for h in range(GROUP)], axis=0
    )


def head_pick(stacked):
    lane = lax.broadcasted_iota(jnp.int32, (ROWS, LANES), 1) // HEAD_DIM
    picked = stacked[:ROWS]
    for h in range(1, GROUP):
        picked = jnp.where(lane == h, stacked[h * ROWS : (h + 1) * ROWS], picked)
    return picked


def load_grid(grid_ref, rows_ref):
    @pl.when(pl.program_id(0) == 0)
    def _():
        rows_ref[...] = jnp.zeros_like(rows_ref)

    for r in range(IMG):
        rows_ref[16 * r : 16 * r + IMG, :] = grid_ref[0, r]


def bias_kernel(code_ref, codes_ref, index_ref, table_ref, out_ref):
    out_ref[...] = jnp.full(out_ref.shape, blocked, F32)
    entry = lax.broadcasted_iota(jnp.int32, (TABLE_PAD, ROWS), 0)
    codes = codes_ref[...]
    table = table_ref[...]
    for j in range(TOKW):
        hot = (entry == index_ref[j : j + 1, :]).astype(F32).astype(BF16)
        found = dot(table, hot)
        for w in range(WINDOWS):
            row = TOKW * w + j
            out_ref[:, row, :] = jnp.where(codes == code_ref[row], found, blocked)


def table_kernel(sums_ref, index_ref, out_ref):
    entry = lax.broadcasted_iota(jnp.int32, (TABLE_PAD, ROWS), 0)
    total = jnp.zeros((HEADS, TABLE_PAD), F32)
    for j in range(TOKW):
        part = sums_ref[:, j, :]
        for w in range(1, WINDOWS):
            part = part + sums_ref[:, TOKW * w + j, :]
        hot = (entry == index_ref[j : j + 1, :]).astype(F32).astype(BF16)
        high = part.astype(BF16)
        low = (part - high.astype(F32)).astype(BF16)
        total = total + dot_nt(high, hot) + dot_nt(low, hot)
    out_ref[...] = total


def attend_kernel(
    grid_ref, order_ref, gain_ref, shift_ref, weight_ref, bias_ref, pair_ref,
    win_ref, in_ref, packed_ref, soft_ref, merged_ref, rows_ref,
):
    load_grid(grid_ref, rows_ref)
    values = dot(order_ref[...], rows_ref[...])
    win_ref[...] = values.astype(BF16)
    unit, _ = row_stats(values)
    attend_in = (unit * gain_ref[...] + shift_ref[...]).astype(BF16)
    in_ref[...] = attend_in
    packed_ref[...] = (dot(attend_in, weight_ref[...]) + bias_ref[...]).astype(BF16)
    for g in range(HEADS // GROUP):
        at = LANES * g
        q = packed_ref[:, at : at + LANES]
        k = packed_ref[:, C + at : C + at + LANES]
        v_turned = turned(packed_ref[:, 2 * C + at : 2 * C + at + LANES])
        raw = dot_nt(head_stack(k), q)
        parts = []
        for h in range(GROUP):
            s = raw[h * ROWS : (h + 1) * ROWS] * scale + pair_ref[g * GROUP + h]
            e = jnp.exp(s - jnp.max(s, axis=0, keepdims=True))
            p = (e * (1.0 / column_sum(e))).astype(BF16)
            soft_ref[0, g * GROUP + h] = p
            parts.append(dot(v_turned[h * HEAD_DIM : (h + 1) * HEAD_DIM], p))
        merged_ref[:, at : at + LANES] = jnp.concatenate(parts, axis=0).T.astype(BF16)


def mlp_kernel(
    count_ref, win_ref, merged_ref, grid_ref, order_ref, back_ref, out_w_ref, out_b_ref,
    gain_ref, shift_ref, exp_w_ref, exp_b_ref, red_w_ref, red_b_ref,
    block_ref, hidden_ref, d_pre_ref, in_ref, grad_ref, d_res_ref, d_branch_ref, d_att_ref,
    sums_ref, wide_ref, rows_ref,
):
    image = pl.program_id(0)

    @pl.when(image == 0)
    def _():
        sums_ref[...] = jnp.zeros_like(sums_ref)
        wide_ref[...] = jnp.zeros_like(wide_ref)

    live = (image < count_ref[0]).astype(F32)
    load_grid(grid_ref, rows_ref)
    grad = dot(order_ref[...], rows_ref[...]) * live
    grad_low = grad.astype(BF16)
    grad_ref[...] = grad_low
    residual = win_ref[...].astype(F32) + dot(merged_ref[...], out_w_ref[...]) + out_b_ref[...]
    unit, inverse = row_stats(residual)
    expand_in = (unit * gain_ref[...] + shift_ref[...]).astype(BF16)
    in_ref[...] = expand_in
    mlp = exp_w_ref.shape[1]
    step = 512
    out = residual + red_b_ref[...]
    d_in = jnp.zeros((ROWS, C), F32)
    for m in range(0, mlp, step):
        cols = slice(m, m + step)
        pre = dot(expand_in, exp_w_ref[:, cols]) + exp_b_ref[:, cols]
        bell = jnp.exp(pre * pre * -0.5)
        t = 1.0 / (1.0 + jnp.abs(pre) * (0.3275911 * 0.7071067811865476))
        tail = (
            t
            * bell
            * (
                0.127414796
                + t * (-0.142248368 + t * (0.7107068705 + t * (-0.7265760135 + t * 0.5307027145)))
            )
        )
        cdf = jnp.where(pre >= 0, 1.0 - tail, tail)
        hidden = (pre * cdf).astype(BF16)
        hidden_ref[:, cols] = hidden
        d_hidden = dot_nt(grad_low, red_w_ref[cols, :])
        d_pre = (d_hidden * (cdf + pre * bell * 0.3989422804014327)).astype(BF16)
        d_pre_ref[:, cols] = d_pre
        wide_ref[:, cols] += column_sum(d_pre.astype(F32))
        out = out + dot(hidden, red_w_ref[cols, :])
        d_in = d_in + dot_nt(d_pre, exp_w_ref[:, cols])
    block = (out * live).astype(BF16)
    block_rows = dot(back_ref[...], block).astype(BF16)
    for r in range(IMG):
        block_ref[0, r] = block_rows[16 * r : 16 * r + IMG]
    d_res = grad + norm_pull(d_in, gain_ref[...], unit, inverse)
    d_res_ref[...] = d_res
    d_branch = d_res.astype(BF16)
    d_branch_ref[...] = d_branch
    d_att_ref[...] = dot_nt(d_branch, out_w_ref[...]).astype(BF16)
    sums_ref[0:1, :] += column_sum(d_in * unit)
    sums_ref[1:2, :] += column_sum(d_in)
    sums_ref[2:3, :] += column_sum(d_branch.astype(F32))
    sums_ref[3:4, :] += column_sum(grad)


def attend_back_kernel(packed_ref, soft_ref, d_att_ref, d_packed_ref, pairs_ref):
    @pl.when(pl.program_id(0) == 0)
    def _():
        pairs_ref[...] = jnp.zeros_like(pairs_ref)

    for g in range(HEADS // GROUP):
        at = LANES * g
        q = packed_ref[:, at : at + LANES]
        k_turned = turned(packed_ref[:, C + at : C + at + LANES])
        v = packed_ref[:, 2 * C + at : 2 * C + at + LANES]
        d_att = d_att_ref[:, at : at + LANES]
        d_soft = dot_nt(head_stack(v), d_att)
        d_raw, d_q, soft = [], [], []
        for h in range(GROUP):
            head = g * GROUP + h
            low = soft_ref[0, head]
            soft.append(low)
            p = low.astype(F32)
            dp = d_soft[h * ROWS : (h + 1) * ROWS]
            ds = (p * (dp - column_sum(p * dp))).astype(BF16)
            pairs_ref[head] += ds.astype(F32)
            d_raw.append(ds)
            d_q.append(dot(k_turned[h * HEAD_DIM : (h + 1) * HEAD_DIM], ds))
        d_k = head_pick(dot(jnp.concatenate(d_raw, axis=0), q))
        d_v = head_pick(dot(jnp.concatenate(soft, axis=0), d_att))
        d_packed_ref[:, at : at + LANES] = (jnp.concatenate(d_q, axis=0) * scale).T.astype(BF16)
        d_packed_ref[:, C + at : C + at + LANES] = (d_k * scale).astype(BF16)
        d_packed_ref[:, 2 * C + at : 2 * C + at + LANES] = d_v.astype(BF16)


def input_kernel(
    d_packed_ref, win_ref, d_res_ref, gain_ref, weight_ref, back_ref,
    grad_ref, sums_ref, wide_ref,
):
    @pl.when(pl.program_id(0) == 0)
    def _():
        sums_ref[...] = jnp.zeros_like(sums_ref)
        wide_ref[...] = jnp.zeros_like(wide_ref)

    d_packed = d_packed_ref[...]
    d_in = dot_nt(d_packed, weight_ref[...])
    unit, inverse = row_stats(win_ref[...].astype(F32))
    total = d_res_ref[...] + norm_pull(d_in, gain_ref[...], unit, inverse)
    sums_ref[0:1, :] += column_sum(d_in * unit)
    sums_ref[1:2, :] += column_sum(d_in)
    wide_ref[...] += column_sum(d_packed.astype(F32))
    high = total.astype(BF16)
    low = (total - high.astype(F32)).astype(BF16)
    rows = dot(back_ref[...], high) + dot(back_ref[...], low)
    for r in range(IMG):
        grad_ref[0, r] = rows[16 * r : 16 * r + IMG]


def whole(shape):
    return pl.BlockSpec(shape, lambda *_: (0,) * len(shape))


def per_image(width):
    return pl.BlockSpec((ROWS, width), lambda i: (i, 0))


GRID_SPEC = pl.BlockSpec((1, IMG, IMG, C), lambda i: (i, 0, 0, 0))
SMEM_SPEC = pl.BlockSpec(memory_space=pltpu.SMEM)


def params():
    return pltpu.CompilerParams(vmem_limit_bytes=VMEM_BYTES)


def cost(flops, moved, special=0):
    return pl.CostEstimate(flops=int(flops), bytes_accessed=int(moved), transcendentals=int(special))


def struct(shape, dtype):
    return jax.ShapeDtypeStruct(shape, dtype)


def run_bias(codes, index_rows, table):
    return pl.pallas_call(
        bias_kernel,
        out_shape=struct((HEADS, ROWS, ROWS), F32),
        in_specs=[SMEM_SPEC] + [pl.BlockSpec(memory_space=pltpu.VMEM)] * 3,
        out_specs=pl.BlockSpec(memory_space=pltpu.VMEM),
        compiler_params=params(),
        cost_estimate=cost(2e9, 4e6),
    )(codes, codes[None, :], index_rows, table)


def run_table(pairs, index_rows):
    return pl.pallas_call(
        table_kernel,
        out_shape=struct((HEADS, TABLE_PAD), F32),
        in_specs=[pl.BlockSpec(memory_space=pltpu.VMEM)] * 2,
        out_specs=pl.BlockSpec(memory_space=pltpu.VMEM),
        compiler_params=params(),
        cost_estimate=cost(2e9, 4e6),
    )(pairs, index_rows)


def run_attend(inputs, order, gain, shift, weight, bias, pair):
    images = inputs.shape[0]
    rows = images * ROWS
    return pl.pallas_call(
        attend_kernel,
        grid=(images,),
        out_shape=(
            struct((rows, C), BF16),
            struct((rows, C), BF16),
            struct((rows, 3 * C), BF16),
            struct((images, HEADS, ROWS, ROWS), BF16),
            struct((rows, C), BF16),
        ),
        in_specs=[
            GRID_SPEC,
            whole((ROWS, RAW)),
            whole((1, C)),
            whole((1, C)),
            whole((C, 3 * C)),
            whole((1, 3 * C)),
            whole((HEADS, ROWS, ROWS)),
        ],
        out_specs=(
            per_image(C),
            per_image(C),
            per_image(3 * C),
            pl.BlockSpec((1, HEADS, ROWS, ROWS), lambda i: (i, 0, 0, 0)),
            per_image(C),
        ),
        scratch_shapes=[pltpu.VMEM((RAW, C), BF16)],
        compiler_params=params(),
        cost_estimate=cost(images * 5e9, images * 6e6),
    )(inputs, order, gain, shift, weight, bias, pair)


def run_mlp(count, win, merged, cotangent, order, back, weights):
    images = cotangent.shape[0]
    rows = images * ROWS
    mlp = weights[4].shape[1]
    return pl.pallas_call(
        mlp_kernel,
        grid=(images,),
        out_shape=(
            struct(cotangent.shape, BF16),
            struct((rows, mlp), BF16),
            struct((rows, mlp), BF16),
            struct((rows, C), BF16),
            struct((rows, C), BF16),
            struct((rows, C), F32),
            struct((rows, C), BF16),
            struct((rows, C), BF16),
            struct((8, C), F32),
            struct((1, mlp), F32),
        ),
        in_specs=[
            SMEM_SPEC,
            per_image(C),
            per_image(C),
            GRID_SPEC,
            whole((ROWS, RAW)),
            whole((RAW, ROWS)),
            whole((C, C)),
            whole((1, C)),
            whole((1, C)),
            whole((1, C)),
            whole((C, mlp)),
            whole((1, mlp)),
            whole((mlp, C)),
            whole((1, C)),
        ],
        out_specs=(
            GRID_SPEC,
            per_image(mlp),
            per_image(mlp),
            per_image(C),
            per_image(C),
            per_image(C),
            per_image(C),
            per_image(C),
            whole((8, C)),
            whole((1, mlp)),
        ),
        scratch_shapes=[pltpu.VMEM((RAW, C), BF16)],
        compiler_params=params(),
        cost_estimate=cost(images * 6e9, images * 4e6),
    )(count, win, merged, cotangent, order, back, *weights)


def run_attend_back(packed, soft, d_att):
    images = soft.shape[0]
    return pl.pallas_call(
        attend_back_kernel,
        grid=(images,),
        out_shape=(struct(packed.shape, BF16), struct((HEADS, ROWS, ROWS), F32)),
        in_specs=[
            per_image(3 * C),
            pl.BlockSpec((1, HEADS, ROWS, ROWS), lambda i: (i, 0, 0, 0)),
            per_image(C),
        ],
        out_specs=(per_image(3 * C), whole((HEADS, ROWS, ROWS))),
        compiler_params=params(),
        cost_estimate=cost(images * 6e9, images * 6e6),
    )(packed, soft, d_att)


def run_input(d_packed, win, d_res, gain, weight, back, shape):
    return pl.pallas_call(
        input_kernel,
        grid=(shape[0],),
        out_shape=(struct(shape, F32), struct((8, C), F32), struct((1, 3 * C), F32)),
        in_specs=[
            per_image(3 * C),
            per_image(C),
            per_image(C),
            whole((1, C)),
            whole((C, 3 * C)),
            whole((RAW, ROWS)),
        ],
        out_specs=(GRID_SPEC, whole((8, C)), whole((1, 3 * C))),
        compiler_params=params(),
        cost_estimate=cost(shape[0] * 1e9, shape[0] * 2e6),
    )(d_packed, win, d_res, gain, weight, back)


def weight_grad(rows_in, rows_out):
    return lax.dot_general(
        rows_in, rows_out, (((0,), (0,)), ((), ())), preferred_element_type=F32
    ).astype(BF16)


def gather(shard):
    return lax.all_gather(shard, "fsdp", axis=0, tiled=True)


def reduce_weight_grad(partial):
    share = lax.psum_scatter(partial, "fsdp", scatter_dimension=0, tiled=True)
    return lax.psum(share, "rep").astype(F32)


def per_device(
    inputs,
    cotangent,
    image_counts,
    region_labels,
    position_index,
    first_gain,
    first_shift,
    attend_weight,
    attend_bias,
    bias_table,
    output_weight,
    output_bias,
    second_gain,
    second_shift,
    expand_weight,
    expand_bias,
    reduce_weight,
    reduce_bias,
):
    order_host = window_order()
    order = jnp.asarray(order_host, BF16)
    back = jnp.asarray(order_host.T, BF16)
    shards = lax.axis_size("fsdp")
    mine = lax.axis_index("fsdp")

    window_of = jnp.arange(WINDOWS, dtype=jnp.int32)[:, None]
    codes = jnp.pad(
        (region_labels + 4 * window_of).reshape(-1), (0, ROWS - TOK), constant_values=-1
    )
    index_rows = jnp.pad(jnp.tile(position_index.T, (1, WINDOWS)), ((0, 0), (0, ROWS - TOK)))
    table = jnp.pad(bias_table.T, ((0, 0), (0, TABLE_PAD - TABLE)))
    pair = run_bias(codes, index_rows, table)

    vectors = (
        first_gain, first_shift, attend_bias, output_bias,
        second_gain, second_shift, expand_bias, reduce_bias,
    )
    sizes = [v.shape[0] for v in vectors]
    joined = gather(jnp.concatenate(vectors)).reshape(shards, sum(sizes)).astype(F32)
    cuts = np.cumsum([0] + sizes)
    full = [
        joined[:, cuts[i] : cuts[i + 1]].reshape(1, shards * sizes[i]) for i in range(len(sizes))
    ]
    gain_one, shift_one, bias_one, bias_out, gain_two, shift_two, bias_exp, bias_red = full
    bias_packed = jnp.concatenate(
        [bias_one[:, :C], jnp.zeros((1, C), F32), bias_one[:, C:]], axis=1
    )
    weight_one = gather(attend_weight)
    weight_out = gather(output_weight)
    weight_exp = gather(expand_weight)
    weight_red = gather(reduce_weight)

    win, attend_in, packed, soft, merged = run_attend(
        inputs, order, gain_one, shift_one, weight_one, bias_packed, pair
    )
    (
        block_output, hidden, d_pre, expand_in, grad_low, d_res, d_branch, d_att, sums_two, d_exp_bias,
    ) = run_mlp(
        image_counts.reshape(1), win, merged, cotangent, order, back,
        (weight_out, bias_out, gain_two, shift_two, weight_exp, bias_exp, weight_red, bias_red),
    )
    reduce_grad = reduce_weight_grad(weight_grad(hidden, grad_low))
    expand_grad = reduce_weight_grad(weight_grad(expand_in, d_pre))
    output_grad = reduce_weight_grad(weight_grad(merged, d_branch))
    d_packed, pairs = run_attend_back(packed, soft, d_att)
    attend_grad = reduce_weight_grad(weight_grad(attend_in, d_packed))
    input_grad, sums_one, d_packed_bias = run_input(
        d_packed, win, d_res, gain_one, weight_one, back, inputs.shape
    )
    table_part = run_table(pairs, index_rows)
    small = (
        sums_one[0], sums_one[1], d_packed_bias[0, :C], d_packed_bias[0, 2 * C :],
        sums_two[2], sums_two[0], sums_two[1], d_exp_bias[0], sums_two[3], table_part.reshape(-1),
    )
    small_sizes = np.cumsum([0] + [s.shape[0] for s in small])
    summed = lax.psum(jnp.concatenate(small), ("fsdp", "rep"))
    parts = [summed[small_sizes[i] : small_sizes[i + 1]] for i in range(len(small))]
    parts = parts[:2] + [jnp.concatenate(parts[2:4])] + parts[4:]

    def own(vector):
        size = vector.shape[0] // shards
        return lax.dynamic_slice(vector, (mine * size,), (size,))

    table_grad = parts[8].reshape(HEADS, TABLE_PAD)[:, :TABLE].T
    return (
        block_output,
        input_grad,
        own(parts[0]),
        own(parts[1]),
        attend_grad,
        own(parts[2]),
        table_grad,
        output_grad,
        own(parts[3]),
        own(parts[4]),
        own(parts[5]),
        expand_grad,
        own(parts[6]),
        reduce_grad,
        own(parts[7]),
    )


def solution(mesh):
    images = P(("fsdp", "rep"), None, None, None)
    rows, vector = P("fsdp", None), P("fsdp")
    return jax.shard_map(
        per_device,
        mesh=mesh,
        in_specs=(
            images, images, P("fsdp", "rep"), P(), P(), vector, vector, rows, vector, P(),
            rows, vector, vector, vector, rows, vector, rows, vector,
        ),
        out_specs=(
            images, images, vector, vector, rows, vector, P(), rows, vector, vector, vector,
            rows, vector, rows, vector,
        ),
        check_vma=False,
    )
```

time: 959 us -> 523 us (0.55)
  local copies, waits for them, and re-layouts: 249 us -> 35.1 us
  matrix products: 189 us -> 26.5 us
  Pallas kernels: 0 us -> 119 us
  blocking collectives: 172 us -> 106 us
  other arithmetic: 70.6 us -> 7.43 us
  waiting for transfers between devices: 248 us -> 212 us
    dot_general x23 -> x4, matrix products: 189 us -> 26.5 us  [weight_grad(): lax.dot_general(rows_in, rows_out, (((0,), (0,)), ((), ())), preferred_el...]
    pallas_call x0 -> x6, Pallas kernels: none -> 119 us  [the longest x1 39.2 us: run_mlp(): pl.pallas_call(mlp_kernel, grid=(images,), out_shape=(struct(cotangent.sh...]
    reduce_scatter x4, waiting for transfers between devices: 246 us -> 157 us  [reduce_weight_grad(): share = lax.psum_scatter(partial, 'fsdp', scatter_dimension=0, tiled=True)]
    another operation x5 -> x2, local copies, waits for them, and re-layouts: 81.5 us -> 0.12 us  [per_device(): jnp.tile(position_index.T, (1, WINDOWS))]
    unnamed x2 -> x0, blocking collectives: 60.2 us -> none
    convert_element_type x6 -> x0, local copies, waits for them, and re-layouts: 50.6 us -> none  [the longest x1 25.3 us: per_device(): jnp.stack((grad_queries, grad_keys, grad_values), axis=3)]
    reduce_sum x6 -> x0, other arithmetic: 30.8 us -> none  [the longest x1 14.9 us: per_device(): jnp.sum(grad_scores.astype(jnp.float32), axis=(0, 1)).transpose(1, 2, 0)]
    all_gather x3, waiting for transfers between devices: 0.04 us -> 29.4 us  [gather(): return lax.all_gather(shard, 'fsdp', axis=0, tiled=True)]
  transfers between devices with their start and end apart: 8 -> 8, of which waited for: 3 -> 5; matrix products, arithmetic and copies ran while one was open for 33% -> 11% of each run, Pallas kernels for 0% -> 15%
where the time goes in v1:
time: 523 us; the launch traced here: 522 us
  waiting for transfers between devices  212 us (41%)
  Pallas kernels  119 us (23%)
  blocking collectives  106 us (20%)
  local copies, waits for them, and re-layouts  35.1 us (7%)
  matrix products  26.5 us (5%)
  between operations  15.1 us (3%)
  other arithmetic  7.43 us (1%)
    reduce_scatter x4, waiting for transfers between devices, reduce_weight_grad(): share = lax.psum_scatter(partial, 'fsdp', scatter_dimension=0, tiled=True)  157 us
    all_gather x2, blocking collectives, gather(): return lax.all_gather(shard, 'fsdp', axis=0, tiled=True)  66.5 us
    psum x1, blocking collectives, per_device(): summed = lax.psum(jnp.concatenate(small), ('fsdp', 'rep'))  39.7 us
    pallas_call x1, Pallas kernels, run_mlp(): pl.pallas_call(mlp_kernel, grid=(images,), out_shape=(struct(cotangent.sh...  39.2 us
    pallas_call x1, Pallas kernels, run_attend(): pl.pallas_call(attend_kernel, grid=(images,), out_shape=(struct((rows, C)...  29.6 us
    all_gather x3, waiting for transfers between devices, gather(): return lax.all_gather(shard, 'fsdp', axis=0, tiled=True)  29.4 us
    dot_general x4, matrix products, weight_grad(): lax.dot_general(rows_in, rows_out, (((0,), (0,)), ((), ())), preferred_el...  26.5 us
    pallas_call x1, Pallas kernels, run_attend_back(): pl.pallas_call(attend_back_kernel, grid=(images,), out_shape=(struct(pack...  25.7 us
  transfers between devices with their start and end apart: 8, of which 5 were waited for; matrix products, arithmetic and copies ran while one was open for 11% of the time, Pallas kernels for 15%

profile of v1, /device:TPU:0, one launch (start us, length us, event | category | flops | bytes accessed | tf_op | source)
XLA Modules:
  0.0 521.8 jit_solution(14882759878058897238)
XLA Ops:
  7.2 0.7 all-gather.5.cloned.1.call-update
  8.0 0.7 all-gather.7.cloned.1.call-update
  8.7 0.7 all-gather.9.cloned.1.call-update
  9.4 5.4 %concatenate.12 = bf16[768]{0:T(1024)(128)(2,1)S(1)} concatenate(bf16[64]{0:T(256)(128)(2,1)} %param.25, bf16[64]{0:T(256)(128)(2,1)} %param.26, bf16[128]{0:T(256)(128)(2,1)} %param.28, bf16[64]{0:T(256)(128)(2,1)} %param.31, bf16[64]{0:T(256)(128)(2,1)} %param.32, bf16[64]{0:T(256)(128)(2,1)} %param.33, bf16[256]{0:T(256)(128)(2,1)} %param.35, bf16[64]{0:T(256)(128)(2,1)} %param.37), dimensions={0} | concatenate | bytes 3072 | tf_op jit(solution)/shard_map/concatenate | solution.py:499
  14.9 32.2 %all-gather = bf16[8,1,768]{2,1,0:T(2,128)(2,1)S(1)} all-gather(bf16[1,1,768]{2,1,0:T(2,128)(2,1)S(1)} %reshape.91), channel_id=1, replica_groups=mesh['fsdp'=8,'rep'=4] {'fsdp'}, dimensions={0}, use_global_device_ids=true | all-gather | bytes 13824 | tf_op jit(solution)/shard_map/all_gather | solution.py:452
  47.3 0.7 reshape.79.gain_ref
  47.9 0.7 reshape.80.shift_ref
  48.6 0.8 copy.40
  49.6 0.9 broadcast_add_fusion
  50.5 3.2 copy.41.grid_ref
  53.7 0.7 reshape.83.out_b_ref
  54.4 0.7 reshape.84.gain_ref
  55.0 0.7 reshape.85.shift_ref
  55.7 0.7 reshape.87.red_b_ref
  56.4 0.6 copy.46
  57.0 1.8 copy.42.grid_ref
  58.8 34.2 %all_gather.17.out_w_ref = bf16[512,512]{1,0:T(8,128)(2,1)} all-gather(bf16[64,512]{1,0:T(8,128)(2,1)S(1)} %copy-done.4), channel_id=1, replica_groups=mesh['fsdp'=8,'rep'=4] {'fsdp'}, dimensions={0}, use_global_device_ids=true | all-gather | bytes 589824 | tf_op jit(solution)/shard_map/all_gather | solution.py:452
  93.7 0.6 pad.13.index_ref
  94.9 0.6 pad.14.table_ref
  95.5 0.6 fusion.bias_ref
  96.1 4.8 shard_map.307.pair_ref
  100.9 29.6 %shard_map.308 = (bf16[1664,512]{1,0:T(8,128)(2,1)}, bf16[1664,512]{1,0:T(8,128)(2,1)}, bf16[1664,1536]{1,0:T(8,128)(2,1)}, bf16[8,16,208,208]{3,2,1,0:T(8,128)(2,1)}, bf16[1664,512]{1,0:T(8,128)(2,1)}) custom-call(bf16[8,14,14,512]{3,2,1,0:T(8,128)(2,1)} %copy.41.grid_ref, bf16[208,224]{1,0:T(8,128)(2,1)} %constant.32.clone.order_ref, ...), custom_call_target="tpu_custom_call" | custom-call | flops 40000000000 | bytes 48000000 | tf_op jit(solution)/shard_map/pallas_call | solution.py:324
  130.5 29.4 %all-gather.9.cloned.1.call-done.red_w_ref = bf16[2048,512]{1,0:T(8,128)(2,1)} async-done(((bf16[256,512]{1,0:T(8,128)(2,1)}), bf16[2048,512]{1,0:T(8,128)(2,1)}) %all-gather.9.cloned.1.call-update) | async-done | bytes 2097168 | tf_op jit(solution)/shard_map/all_gather | solution.py:452
  159.8 39.2 %shard_map.309 = (bf16[8,14,14,512]{3,2,1,0:T(8,128)(2,1)}, bf16[1664,2048]{1,0:T(8,128)(2,1)}, bf16[1664,2048]{1,0:T(8,128)(2,1)}, bf16[1664,512]{1,0:T(8,128)(...) custom-call(s32[1]{0:T(128)} %bitcast.31.count_ref, ...), custom_call_target="tpu_custom_call" | custom-call | flops 48000000000 | bytes 32000000 | tf_op jit(solution)/shard_map/pallas_call | solution.py:360
  199.0 3.4 convolution_convert_fusion.3
  202.7 25.7 %shard_map.310 = (bf16[1664,1536]{1,0:T(8,128)(2,1)}, f32[16,208,208]{2,1,0:T(8,128)}) custom-call(bf16[1664,1536]{1,0:T(8,128)(2,1)} %get-tuple-element.38.packed_ref, bf16[8,16,208,208]{3,2,1,0:T(8,128)(2,1)} %get-tuple-element.39.soft_ref, bf16[1664,512]{1,0:T(8,128)(2,1)} %get-tuple-element.40.d_att_ref), custom_call_target="tpu_custom_call" | custom-call | flops 48000000000 | bytes 48000000 | tf_op jit(solution)/shard_map/pallas_call | solution.py:411
  228.4 6.7 %convolution_convert_fusion.2 = bf16[512,1536]{1,0:T(8,128)(2,1)} fusion(bf16[1664,512]{1,0:T(8,128)(2,1)S(1)} %copy-done.9, bf16[1664,1536]{1,0:T(8,128)(2,1)} %get-tuple-element.41.d_packed_ref), kind=kOutput, calls=%fused_computation.2 | convolution fusion | flops 2618032128 | bytes 8388608 | tf_op jit(solution)/shard_map/dot_general | solution.py:446
  235.2 8.3 %convolution_convert_fusion = bf16[2048,512]{1,0:T(8,128)(2,1)} fusion(bf16[1664,2048]{1,0:T(8,128)(2,1)} %get-tuple-element.53, bf16[1664,512]{1,0:T(8,128)(2,1)S(1)} %copy-done.11), kind=kOutput, calls=%fused_computation | convolution fusion | flops 3490709504 | bytes 10616832 | tf_op jit(solution)/shard_map/dot_general | solution.py:446
  243.6 1.4 copy-done.10
  244.9 8.1 %convolution_convert_fusion.1 = bf16[512,2048]{1,0:T(8,128)(2,1)} fusion(bf16[1664,512]{1,0:T(8,128)(2,1)S(1)} %copy-done.10, bf16[1664,2048]{1,0:T(8,128)(2,1)} %get-tuple-element.52), kind=kOutput, calls=%fused_computation.1 | convolution fusion | flops 3490709504 | bytes 10616832 | tf_op jit(solution)/shard_map/dot_general | solution.py:446
  253.4 7.2 %shard_map.312 = f32[16,176]{1,0:T(8,128)} custom-call(f32[16,208,208]{2,1,0:T(8,128)} %get-tuple-element.48.sums_ref, s32[49,208]{1,0:T(8,128)} %pad.13.index_ref), custom_call_target="tpu_custom_call" | custom-call | flops 2000000000 | bytes 4000000 | tf_op jit(solution)/shard_map/pallas_call | solution.py:311
  260.6 0.8 reshape.88
  261.4 12.8 %shard_map.311 = (f32[8,14,14,512]{3,2,1,0:T(8,128)}, f32[8,512]{1,0:T(8,128)}, f32[1,1536]{1,0:T(1,128)}) custom-call(bf16[1664,1536]{1,0:T(8,128)(2,1)} %get-tuple-element.41.d_packed_ref, bf16[1664,512]{1,0:T(8,128)(2,1)} %get-tuple-element.35.win_ref, f32[1664,512]{1,0:T(8,128)} %get-tuple-element.42.d_res_ref, f32[1,512]{1,0:T(1,128)} %reshape.79.gain_ref, ...), custom_call_target="tpu_custom_call" | custom-call | flops 8000000000 | bytes 16000000 | tf_op jit(solution)/shard_map/pallas_call | solution.py:427
  274.2 0.8 fusion.4
  275.2 39.7 %psum.35 = f32[8960]{0:T(1024)S(1)} all-reduce(f32[8960]{0:T(1024)S(1)} %constant_dynamic-update-slice_fusion), channel_id=1, replica_groups=mesh['fsdp'=8,'rep'=4] {'fsdp','rep'}, use_global_device_ids=true, to_apply=%region_0.1 | all-reduce | flops 8960 | bytes 71680 | tf_op jit(solution)/shard_map/psum | solution.py:536
  315.0 16.2 %reduce-scatter.5.cloned.1.call-done = bf16[64,1536]{1,0:T(8,128)(2,1)} async-done(((bf16[512,1536]{1,0:T(8,128)(2,1)}), bf16[64,1536]{1,0:T(8,128)(2,1)}) %reduce-scatter.5.cloned.1.call-update) | async-done | bytes 196624 | tf_op jit(solution)/shard_map/reduce_scatter | solution.py:456
  331.2 70.0 %reduce-scatter.11.cloned.1.call-done = bf16[256,512]{1,0:T(8,128)(2,1)} async-done(((bf16[2048,512]{1,0:T(8,128)(2,1)}), bf16[256,512]{1,0:T(8,128)(2,1)}) %reduce-scatter.11.cloned.1.call-update) | async-done | bytes 262160 | tf_op jit(solution)/shard_map/reduce_scatter | solution.py:456
  401.2 71.0 %reduce-scatter.9.cloned.1.call-done = bf16[64,2048]{1,0:T(8,128)(2,1)} async-done(((bf16[512,2048]{1,0:T(8,128)(2,1)}), bf16[64,2048]{1,0:T(8,128)(2,1)}) %reduce-scatter.9.cloned.1.call-update) | async-done | bytes 262160 | tf_op jit(solution)/shard_map/reduce_scatter | solution.py:456
  472.3 0.6 dynamic_slice.27
  475.8 6.4 %copy.44 = f32[8,14,14,512]{3,0,2,1:T(8,128)} copy(f32[8,14,14,512]{3,2,1,0:T(8,128)} %get-tuple-element.71) | data formatting | bytes 6422528
  482.2 2.2 copy.43
  484.4 0.6 dynamic_slice.30
  485.6 0.6 slice_bitcast_fusion
  486.2 22.8 %all-reduce.6.cloned.1.call-done = (bf16[64,1536]{1,0:T(8,128)(2,1)}, bf16[64,512]{1,0:T(8,128)(2,1)}, bf16[64,2048]{1,0:T(8,128)(2,1)}, bf16[256,512]{1,0:T(8,128)(2,1)}) async-done(((bf16[64,1536]{1,0:T(8,128)(2,1)}, bf16[64,512]{1,0:T(8,128)(2,1)}, bf16[64,2048]{1,0:T(8,128)(2,1)}, bf16[256,512]{1,0:T(8,128)(2,1)}), (bf16[64,1536]{1,0:T(8,128)(2,1)}, bf16[64,512]{1,0:T(8,128)(2,1)}, ...) | async-done | bytes 786448 | tf_op jit(solution)/shard_map/psum | solution.py:457
  509.0 1.8 convert_element_type.39
  510.8 1.8 convert_element_type.41
  512.6 1.7 convert_element_type.35
  514.3 0.7 convert_element_type.37
  (76 shorter events, 5.5 us)
Async XLA Ops:
  7.2 93.7 %all-gather.5.cloned.1.call-start = ((), (), s32[]{:S(2)}) async-start(), calls=%async_computation.4 | async-start | bytes 1769472 | tf_op jit(solution)/shard_map/all_gather | solution.py:452
  7.9 122.5 %all-gather.7.cloned.1.call-start = ((), (), s32[]{:S(2)}) async-start(), calls=%async_computation.5 | async-start | bytes 2359296 | tf_op jit(solution)/shard_map/all_gather | solution.py:452
  8.7 151.2 %all-gather.9.cloned.1.call-start = ((), (), s32[]{:S(2)}) async-start(), calls=%async_computation.6 | async-start | bytes 2359296 | tf_op jit(solution)/shard_map/all_gather | solution.py:452
  9.4 305.6 %reduce-scatter.7.cloned.1.call-start = ((), (), s32[]{:S(2)}) async-start(), calls=%async_computation.8 | async-start | bytes 589824 | tf_op jit(solution)/shard_map/reduce_scatter | solution.py:456
  49.5 7.5 %copy-start.2 = (bf16[8,14,14,512]{3,0,2,1:T(8,128)(2,1)S(1)}, bf16[8,14,14,512]{3,0,2,1:T(8,128)(2,1)}, u32[]{:S(2)}) copy-start(bf16[8,14,14,512]{3,0,2,1:T(8,128)(2,1)} %param.21) | copy-start | bytes 4816900
  53.7 5.1 copy-start.4
  57.0 37.9 %copy-start.6 = (bf16[169,16]{0,1:T(8,128)(2,1)S(1)}, bf16[169,16]{0,1:T(8,128)(2,1)}, u32[]{:S(2)}) copy-start(bf16[169,16]{0,1:T(8,128)(2,1)} %param.29) | copy-start | bytes 16228
  159.8 39.2 %copy-start.1 = (bf16[1664,512]{1,0:T(8,128)(2,1)S(1)}, bf16[1664,512]{1,0:T(8,128)(2,1)}, u32[]{:S(2)}) copy-start(bf16[1664,512]{1,0:T(8,128)(2,1)} %get-tuple-element.36.merged_ref) | copy-start | bytes 5111812
  202.5 128.7 %reduce-scatter.5.cloned.1.call-start = ((), (), s32[]{:S(2)}) async-start(), calls=%async_computation.7 | async-start | bytes 1769472 | tf_op jit(solution)/shard_map/reduce_scatter | solution.py:456
  202.7 25.7 %copy-start.9 = (bf16[1664,512]{1,0:T(8,128)(2,1)S(1)}, bf16[1664,512]{1,0:T(8,128)(2,1)}, u32[]{:S(2)}) copy-start(bf16[1664,512]{1,0:T(8,128)(2,1)} %get-tuple-element.49) | copy-start | bytes 5111812
  228.4 6.8 %copy-start.11 = (bf16[1664,512]{1,0:T(8,128)(2,1)S(1)}, bf16[1664,512]{1,0:T(8,128)(2,1)}, u32[]{:S(2)}) copy-start(bf16[1664,512]{1,0:T(8,128)(2,1)} %get-tuple-element.54) | copy-start | bytes 5111812
  235.1 166.1 %reduce-scatter.11.cloned.1.call-start = ((), (), s32[]{:S(2)}) async-start(), calls=%async_computation.10 | async-start | bytes 2359296 | tf_op jit(solution)/shard_map/reduce_scatter | solution.py:456
  243.5 1.5 copy-start.10
  243.5 228.7 %reduce-scatter.9.cloned.1.call-start = ((), (), s32[]{:S(2)}) async-start(), calls=%async_computation.9 | async-start | bytes 2359296 | tf_op jit(solution)/shard_map/reduce_scatter | solution.py:456
  253.1 255.9 %all-reduce.6.cloned.1.call-start = ((), (), s32[]{:S(2)}) async-start(), calls=%async_computation.11 | async-start | bytes 1572864 | tf_op jit(solution)/shard_map/psum | solution.py:457
  261.4 13.7 %copy-start.8 = (f32[8,512]{1,0:T(8,128)S(1)}, f32[8,512]{1,0:T(8,128)}, u32[]{:S(2)}) copy-start(f32[8,512]{1,0:T(8,128)} %get-tuple-element.46) | copy-start | bytes 49156
  261.4 13.7 %copy-start.7 = (f32[1,2048]{1,0:T(1,128)S(1)}, f32[1,2048]{1,0:T(1,128)}, u32[]{:S(2)}) copy-start(f32[1,2048]{1,0:T(1,128)} %get-tuple-element.47) | copy-start | bytes 24580
  314.9 167.3 %copy-start.3 = (f32[8960]{0:T(1024)}, f32[8960]{0:T(1024)S(1)}, u32[]{:S(2)}) copy-start(f32[8960]{0:T(1024)S(1)} %psum.35) | copy-start | bytes 107524
  475.8 6.4 %copy-start = (bf16[8,14,14,512]{3,2,1,0:T(8,128)(2,1)S(1)}, bf16[8,14,14,512]{3,2,1,0:T(8,128)(2,1)}, u32[]{:S(2)}) copy-start(bf16[8,14,14,512]{3,2,1,0:T(8,128)(2,1)} %get-tuple-element.70) | copy-start | bytes 4816900
  482.2 2.8 slice-start
  509.0 5.3 %copy-start.5 = (bf16[64,512]{1,0:T(8,128)(2,1)S(1)}, bf16[64,512]{1,0:T(8,128)(2,1)}, u32[]{:S(2)}) copy-start(bf16[64,512]{1,0:T(8,128)(2,1)} %get-tuple-element.86) | copy-start | bytes 196612
Sparse Core Ops, SparseCore 0:
  10.2 47.9 all-gather.4
  60.3 48.4 all-gather.6
  110.9 48.8 all-gather.8
  202.6 60.2 reduce-scatter.6
  267.1 64.0 reduce-scatter.4
  334.6 66.6 reduce-scatter.10
  405.4 66.8 reduce-scatter.8
  474.9 34.0 all-reduce.5

commit v2 on v1

--- a/solution.py
+++ b/solution.py
@@ -115,24 +115,37 @@
             out_ref[:, row, :] = jnp.where(codes == code_ref[row], found, blocked)
 
 
-def table_kernel(sums_ref, index_ref, out_ref):
+def table_kernel(sums_ref, index_ref, out_ref, window_ref):
+    for h in range(HEADS):
+        part = sums_ref[h, :TOKW, :]
+        for w in range(1, WINDOWS):
+            part = part + sums_ref[h, TOKW * w : TOKW * (w + 1), :]
+        window_ref[h, :TOKW, :] = part
     entry = lax.broadcasted_iota(jnp.int32, (TABLE_PAD, ROWS), 0)
-    total = jnp.zeros((HEADS, TABLE_PAD), F32)
+    total = jnp.zeros((2 * HEADS, TABLE_PAD), F32)
     for j in range(TOKW):
-        part = sums_ref[:, j, :]
-        for w in range(1, WINDOWS):
-            part = part + sums_ref[:, TOKW * w + j, :]
+        part = window_ref[:, j, :]
         hot = (entry == index_ref[j : j + 1, :]).astype(F32).astype(BF16)
         high = part.astype(BF16)
         low = (part - high.astype(F32)).astype(BF16)
-        total = total + dot_nt(high, hot) + dot_nt(low, hot)
-    out_ref[...] = total
-
-
-def attend_kernel(
-    grid_ref, order_ref, gain_ref, shift_ref, weight_ref, bias_ref, pair_ref,
-    win_ref, in_ref, packed_ref, soft_ref, merged_ref, rows_ref,
-):
+        total = total + dot_nt(jnp.concatenate([high, low], axis=0), hot)
+    out_ref[...] = total[:HEADS] + total[HEADS:]
+
+
+def attend_kernel(starts_ref, grid_ref, order_ref, gain_ref, shift_ref, bias_ref, pair_ref, *rest):
+    pieces = rest[:-7]
+    win_ref, in_ref, packed_ref, soft_ref, merged_ref, weight_ref, rows_ref = rest[-7:]
+
+    @pl.when(pl.program_id(0) == 0)
+    def _():
+        rows = weight_ref.shape[0] // starts_ref.shape[0]
+        at = 0
+        for piece in pieces:
+            for r in range(0, piece.shape[0], rows):
+                start = pl.multiple_of(starts_ref[at], rows)
+                weight_ref[pl.ds(start, rows), :] = piece[r : r + rows, :]
+                at += 1
+
     load_grid(grid_ref, rows_ref)
     values = dot(order_ref[...], rows_ref[...])
     win_ref[...] = values.astype(BF16)
@@ -157,17 +170,31 @@
 
 
 def mlp_kernel(
-    count_ref, win_ref, merged_ref, grid_ref, order_ref, back_ref, out_w_ref, out_b_ref,
-    gain_ref, shift_ref, exp_w_ref, exp_b_ref, red_w_ref, red_b_ref,
+    count_ref, win_ref, merged_ref, grid_ref, order_ref, back_ref, out_b_ref,
+    gain_ref, shift_ref, exp_b_ref, red_b_ref, joined_ref,
     block_ref, hidden_ref, d_pre_ref, in_ref, grad_ref, d_res_ref, d_branch_ref, d_att_ref,
-    sums_ref, wide_ref, rows_ref,
+    sums_ref, wide_ref, rows_ref, red_w_ref, red_t_ref, exp_t_ref, out_t_ref,
 ):
     image = pl.program_id(0)
+    mlp = exp_b_ref.shape[1]
+    blocks = mlp // C
+    out_w_ref = joined_ref.at[:, :C]
+    exp_w_ref = joined_ref.at[:, C : C + mlp]
 
     @pl.when(image == 0)
     def _():
         sums_ref[...] = jnp.zeros_like(sums_ref)
         wide_ref[...] = jnp.zeros_like(wide_ref)
+        for at in range(0, C, 16):
+            for b in range(blocks):
+                cols = C + mlp + b * C
+                red_w_ref[blocks * at + 16 * b : blocks * at + 16 * (b + 1), :] = joined_ref[
+                    at : at + 16, cols : cols + C
+                ]
+        out_t_ref[...] = turned(out_w_ref[...])
+        for m in range(0, mlp, C):
+            red_t_ref[:, m : m + C] = turned(red_w_ref[m : m + C, :])
+            exp_t_ref[m : m + C, :] = turned(exp_w_ref[:, m : m + C])
 
     live = (image < count_ref[0]).astype(F32)
     load_grid(grid_ref, rows_ref)
@@ -178,7 +205,6 @@
     unit, inverse = row_stats(residual)
     expand_in = (unit * gain_ref[...] + shift_ref[...]).astype(BF16)
     in_ref[...] = expand_in
-    mlp = exp_w_ref.shape[1]
     step = 512
     out = residual + red_b_ref[...]
     d_in = jnp.zeros((ROWS, C), F32)
@@ -198,12 +224,12 @@
         cdf = jnp.where(pre >= 0, 1.0 - tail, tail)
         hidden = (pre * cdf).astype(BF16)
         hidden_ref[:, cols] = hidden
-        d_hidden = dot_nt(grad_low, red_w_ref[cols, :])
+        d_hidden = dot(grad_low, red_t_ref[:, cols])
         d_pre = (d_hidden * (cdf + pre * bell * 0.3989422804014327)).astype(BF16)
         d_pre_ref[:, cols] = d_pre
         wide_ref[:, cols] += column_sum(d_pre.astype(F32))
         out = out + dot(hidden, red_w_ref[cols, :])
-        d_in = d_in + dot_nt(d_pre, exp_w_ref[:, cols])
+        d_in = d_in + dot(d_pre, exp_t_ref[cols, :])
     block = (out * live).astype(BF16)
     block_rows = dot(back_ref[...], block).astype(BF16)
     for r in range(IMG):
@@ -212,7 +238,7 @@
     d_res_ref[...] = d_res
     d_branch = d_res.astype(BF16)
     d_branch_ref[...] = d_branch
-    d_att_ref[...] = dot_nt(d_branch, out_w_ref[...]).astype(BF16)
+    d_att_ref[...] = dot(d_branch, out_t_ref[...]).astype(BF16)
     sums_ref[0:1, :] += column_sum(d_in * unit)
     sums_ref[1:2, :] += column_sum(d_in)
     sums_ref[2:3, :] += column_sum(d_branch.astype(F32))
@@ -251,15 +277,17 @@
 
 def input_kernel(
     d_packed_ref, win_ref, d_res_ref, gain_ref, weight_ref, back_ref,
-    grad_ref, sums_ref, wide_ref,
+    grad_ref, sums_ref, wide_ref, turned_ref,
 ):
     @pl.when(pl.program_id(0) == 0)
     def _():
+        for m in range(0, 3 * C, C):
+            turned_ref[m : m + C, :] = turned(weight_ref[:, m : m + C])
         sums_ref[...] = jnp.zeros_like(sums_ref)
         wide_ref[...] = jnp.zeros_like(wide_ref)
 
     d_packed = d_packed_ref[...]
-    d_in = dot_nt(d_packed, weight_ref[...])
+    d_in = dot(d_packed, turned_ref[...])
     unit, inverse = row_stats(win_ref[...].astype(F32))
     total = d_res_ref[...] + norm_pull(d_in, gain_ref[...], unit, inverse)
     sums_ref[0:1, :] += column_sum(d_in * unit)
@@ -313,12 +341,13 @@
         out_shape=struct((HEADS, TABLE_PAD), F32),
         in_specs=[pl.BlockSpec(memory_space=pltpu.VMEM)] * 2,
         out_specs=pl.BlockSpec(memory_space=pltpu.VMEM),
+        scratch_shapes=[pltpu.VMEM((HEADS, 56, ROWS), F32)],
         compiler_params=params(),
         cost_estimate=cost(2e9, 4e6),
     )(pairs, index_rows)
 
 
-def run_attend(inputs, order, gain, shift, weight, bias, pair):
+def run_attend(inputs, order, gain, shift, starts, pieces, bias, pair):
     images = inputs.shape[0]
     rows = images * ROWS
     return pl.pallas_call(
@@ -330,33 +359,36 @@
             struct((rows, 3 * C), BF16),
             struct((images, HEADS, ROWS, ROWS), BF16),
             struct((rows, C), BF16),
+            struct((C, 3 * C), BF16),
         ),
         in_specs=[
+            SMEM_SPEC,
             GRID_SPEC,
             whole((ROWS, RAW)),
             whole((1, C)),
             whole((1, C)),
-            whole((C, 3 * C)),
             whole((1, 3 * C)),
             whole((HEADS, ROWS, ROWS)),
-        ],
+        ]
+        + [whole(piece.shape) for piece in pieces],
         out_specs=(
             per_image(C),
             per_image(C),
             per_image(3 * C),
             pl.BlockSpec((1, HEADS, ROWS, ROWS), lambda i: (i, 0, 0, 0)),
             per_image(C),
+            whole((C, 3 * C)),
         ),
         scratch_shapes=[pltpu.VMEM((RAW, C), BF16)],
         compiler_params=params(),
         cost_estimate=cost(images * 5e9, images * 6e6),
-    )(inputs, order, gain, shift, weight, bias, pair)
+    )(starts, inputs, order, gain, shift, bias, pair, *pieces)
 
 
 def run_mlp(count, win, merged, cotangent, order, back, weights):
     images = cotangent.shape[0]
     rows = images * ROWS
-    mlp = weights[4].shape[1]
+    mlp = weights[3].shape[1]
     return pl.pallas_call(
         mlp_kernel,
         grid=(images,),
@@ -379,14 +411,12 @@
             GRID_SPEC,
             whole((ROWS, RAW)),
             whole((RAW, ROWS)),
-            whole((C, C)),
             whole((1, C)),
             whole((1, C)),
             whole((1, C)),
-            whole((C, mlp)),
             whole((1, mlp)),
-            whole((mlp, C)),
             whole((1, C)),
+            whole((C, C + 2 * mlp)),
         ],
         out_specs=(
             GRID_SPEC,
@@ -400,7 +430,13 @@
             whole((8, C)),
             whole((1, mlp)),
         ),
-        scratch_shapes=[pltpu.VMEM((RAW, C), BF16)],
+        scratch_shapes=[
+            pltpu.VMEM((RAW, C), BF16),
+            pltpu.VMEM((mlp, C), BF16),
+            pltpu.VMEM((C, mlp), BF16),
+            pltpu.VMEM((mlp, C), BF16),
+            pltpu.VMEM((C, C), BF16),
+        ],
         compiler_params=params(),
         cost_estimate=cost(images * 6e9, images * 4e6),
     )(count, win, merged, cotangent, order, back, *weights)
@@ -437,6 +473,7 @@
             whole((RAW, ROWS)),
         ],
         out_specs=(GRID_SPEC, whole((8, C)), whole((1, 3 * C))),
+        scratch_shapes=[pltpu.VMEM((3 * C, C), BF16)],
         compiler_params=params(),
         cost_estimate=cost(shape[0] * 1e9, shape[0] * 2e6),
     )(d_packed, win, d_res, gain, weight, back)
@@ -450,6 +487,144 @@
 
 def gather(shard):
     return lax.all_gather(shard, "fsdp", axis=0, tiled=True)
+
+
+def swap(value, axis, bits):
+    return lax.ppermute(value, axis, [(i, i ^ bits) for i in range(lax.axis_size(axis))])
+
+
+def pick(value, index, axis):
+    return lax.dynamic_index_in_dim(value, index, axis, keepdims=False)
+
+
+def gather_line(shard):
+    half = shard.shape[0] // 2
+    own = lax.dynamic_slice_in_dim(shard, lax.axis_index("rep") % 2 * half, half, 0)
+    return jnp.concatenate([own] + [swap(own, "fsdp", d) for d in (2, 4, 6)], axis=0)
+
+
+def gather_pieces(line, rows):
+    mine, core = lax.axis_index("fsdp"), lax.axis_index("rep") % 2
+    across = swap(line, "fsdp", 1)
+    pieces = [line, swap(line, "rep", 1), across, swap(across, "rep", 1)]
+    starts = []
+    for side in (0, 1):
+        for other in (0, 1):
+            for d in (0, 2, 4, 6):
+                starts.append((mine ^ d ^ side) * rows + (core ^ other) * (rows // 2))
+    return jnp.stack(starts).astype(jnp.int32), pieces
+
+
+def gather_vector(line):
+    mine, owners = lax.axis_index("fsdp"), lax.axis_size("fsdp")
+    held = jnp.concatenate([line, swap(line, "fsdp", 1)], axis=0)
+    stacked = held.reshape(owners, -1).astype(F32)
+    order = jnp.asarray((0, 4, 2, 6, 1, 5, 3, 7))
+    chosen = (jnp.arange(owners)[:, None] ^ order[None, :]) == mine
+    return jnp.sum(jnp.where(chosen[:, :, None], stacked[None], 0.0), axis=1)
+
+
+def gather_joined(weight_out, weight_exp, weight_red):
+    replica, replicas = lax.axis_index("rep"), lax.axis_size("rep")
+    rows = weight_out.shape[0] // replicas
+    blocks = weight_red.shape[0] // weight_out.shape[0]
+
+    def quarter(shard):
+        size = shard.shape[0] // replicas
+        return lax.dynamic_slice_in_dim(shard, replica * size, size, 0)
+
+    red = quarter(weight_red).reshape(blocks, rows, C).transpose(1, 0, 2).reshape(rows, blocks * C)
+    joined = jnp.concatenate([quarter(weight_out), quarter(weight_exp), red], axis=1)
+    return lax.all_gather(joined, ("fsdp", "rep"), axis=0, tiled=True)
+
+
+def halves(block, bit, axis):
+    return pick(block, bit, axis), pick(block, 1 - bit, axis)
+
+
+def added(a, b):
+    return (a.astype(F32) + b.astype(F32)).astype(BF16)
+
+
+def scatter_parts(partials):
+    joined = []
+    for partial in partials:
+        cols = partial.shape[1]
+        blocks = partial.shape[0] // (32 * 16)
+        quarters = partial.reshape(32, blocks, 16, cols).transpose(0, 2, 1, 3)
+        joined.append(quarters.reshape(2, 2, 2, 2, 2, 16, blocks * cols))
+    return jnp.concatenate(joined, axis=-1)
+
+
+def scatter_bits():
+    mine, replica = lax.axis_index("fsdp"), lax.axis_index("rep")
+    return mine // 4, mine // 2 % 2, mine % 2, replica // 2, replica % 2
+
+
+def scatter_step(kept, got, bit, axis):
+    keep, away = halves(kept, bit, axis)
+    got_keep, got_away = halves(got, bit, axis)
+    return added(keep, got_keep), added(away, got_away)
+
+
+def join_kernel(id_ref, *refs):
+    groups = refs[: len(refs) - 4]
+    outs = refs[len(refs) - 4 :]
+    at = 0
+    for g in range(0, len(groups), 2):
+        col = 0
+        while col < groups[g].shape[2]:
+            out = outs[at]
+            at += 1
+            rows, cols = out.shape
+            rows = rows // 4
+            for e in range(4):
+                start = pl.multiple_of((id_ref[0] ^ e) * rows, rows)
+                for b in range(rows // 16):
+                    block = groups[g + e // 2][e % 2, :, col + b * cols : col + (b + 1) * cols]
+                    out[pl.ds(start + 16 * b, 16), :] = block.astype(F32)
+            col += rows // 16 * cols
+
+
+def run_join(pieces, shapes):
+    moved = sum(6 * a * b for a, b in shapes)
+    return pl.pallas_call(
+        join_kernel,
+        out_shape=[struct(shape, F32) for shape in shapes],
+        in_specs=[SMEM_SPEC] + [pl.BlockSpec(memory_space=pltpu.VMEM)] * len(pieces),
+        out_specs=[pl.BlockSpec(memory_space=pltpu.VMEM)] * len(shapes),
+        compiler_params=params(),
+        cost_estimate=cost(moved, moved),
+    )(lax.axis_index("rep").astype(jnp.int32)[None], *pieces)
+
+
+def finish(kept_mlp, away_mlp, kept, away, vector):
+    far, near, side, row, _ = scatter_bits()
+    kept_mlp, away_mlp = scatter_step(kept_mlp, away_mlp, near, 0)
+    kept, away = scatter_step(kept, away, side, 2)
+    size = vector.shape[0]
+    rows = jnp.pad(vector, (0, -size % 1024)).reshape(-1, 128)
+    tie = lax.optimization_barrier
+
+    away_mlp, away, rows = tie((away_mlp, away, rows))
+    total_mlp = added(kept_mlp, swap(away_mlp, "fsdp", 2))
+    kept, away = scatter_step(kept, swap(away, "fsdp", 1), far, 0)
+    rows = rows + swap(rows, "rep", 1)
+    total_mlp, away, rows = tie((total_mlp, away, rows))
+    both_mlp = jnp.stack([total_mlp, swap(total_mlp, "rep", 1)])
+    kept, away = scatter_step(kept, swap(away, "fsdp", 4), near, 0)
+    rows = rows + swap(rows, "rep", 2)
+    both_mlp, away, rows = tie((both_mlp, away, rows))
+    rest_mlp = swap(both_mlp, "rep", 2)
+    total = added(kept, swap(away, "fsdp", 2))
+    rows = rows + swap(rows, "fsdp", 1)
+    rest_mlp, total, rows = tie((rest_mlp, total, rows))
+    both = jnp.stack([total, swap(total, "rep", 1)])
+    rows = rows + swap(rows, "fsdp", 4)
+    both, rows = tie((both, rows))
+    rest = swap(both, "rep", 2)
+    rows = rows + swap(rows, "fsdp", 2)
+    return [both_mlp, rest_mlp, both, rest], rows.reshape(-1)[:size]
 
 
 def reduce_weight_grad(partial):
@@ -482,6 +657,7 @@
     back = jnp.asarray(order_host.T, BF16)
     shards = lax.axis_size("fsdp")
     mine = lax.axis_index("fsdp")
+    paired = shards == 8 and lax.axis_size("rep") == 4
 
     window_of = jnp.arange(WINDOWS, dtype=jnp.int32)[:, None]
     codes = jnp.pad(
@@ -496,7 +672,19 @@
         second_gain, second_shift, expand_bias, reduce_bias,
     )
     sizes = [v.shape[0] for v in vectors]
-    joined = gather(jnp.concatenate(vectors)).reshape(shards, sum(sizes)).astype(F32)
+    if paired:
+        joined_weights = gather_joined(output_weight, expand_weight, reduce_weight)
+        line = gather_line(attend_weight)
+        own = jnp.concatenate(vectors).reshape(1, -1, 128)
+        vector_line = own
+        for bits in (4, 2):
+            vector_line = jnp.concatenate([vector_line, swap(vector_line, "fsdp", bits)], axis=0)
+        line, vector_line, pair = lax.optimization_barrier((line, vector_line, pair))
+        joined = gather_vector(vector_line)
+        starts, pieces = gather_pieces(line, attend_weight.shape[0])
+        inputs, cotangent, _ = lax.optimization_barrier((inputs, cotangent, line))
+    else:
+        joined = gather(jnp.concatenate(vectors)).reshape(shards, sum(sizes)).astype(F32)
     cuts = np.cumsum([0] + sizes)
     full = [
         joined[:, cuts[i] : cuts[i + 1]].reshape(1, shards * sizes[i]) for i in range(len(sizes))
@@ -505,35 +693,67 @@
     bias_packed = jnp.concatenate(
         [bias_one[:, :C], jnp.zeros((1, C), F32), bias_one[:, C:]], axis=1
     )
-    weight_one = gather(attend_weight)
-    weight_out = gather(output_weight)
-    weight_exp = gather(expand_weight)
-    weight_red = gather(reduce_weight)
-
-    win, attend_in, packed, soft, merged = run_attend(
-        inputs, order, gain_one, shift_one, weight_one, bias_packed, pair
+    if not paired:
+        starts, pieces = jnp.zeros((1,), jnp.int32), [gather(attend_weight)]
+        red = gather(reduce_weight).reshape(C // 16, -1, 16, C).transpose(0, 2, 1, 3).reshape(C, -1)
+        joined_weights = jnp.concatenate([gather(output_weight), gather(expand_weight), red], axis=1)
+
+    win, attend_in, packed, soft, merged, weight_one = run_attend(
+        inputs, order, gain_one, shift_one, starts, pieces, bias_packed, pair
     )
     (
         block_output, hidden, d_pre, expand_in, grad_low, d_res, d_branch, d_att, sums_two, d_exp_bias,
     ) = run_mlp(
         image_counts.reshape(1), win, merged, cotangent, order, back,
-        (weight_out, bias_out, gain_two, shift_two, weight_exp, bias_exp, weight_red, bias_red),
-    )
-    reduce_grad = reduce_weight_grad(weight_grad(hidden, grad_low))
-    expand_grad = reduce_weight_grad(weight_grad(expand_in, d_pre))
-    output_grad = reduce_weight_grad(weight_grad(merged, d_branch))
+        (bias_out, gain_two, shift_two, bias_exp, bias_red, joined_weights),
+    )
+    reduce_part = weight_grad(hidden, grad_low)
+    expand_part = weight_grad(expand_in, d_pre)
+    output_part = weight_grad(merged, d_branch)
+    if paired:
+        far, _, side, row, core = scatter_bits()
+        kept_mlp, away = halves(scatter_parts([output_part, expand_part, reduce_part]), core, 4)
+        kept_mlp, away = scatter_step(kept_mlp, swap(away, "rep", 1), row, 3)
+        d_att, away = lax.optimization_barrier((d_att, away))
+        got = swap(away, "rep", 2)
     d_packed, pairs = run_attend_back(packed, soft, d_att)
-    attend_grad = reduce_weight_grad(weight_grad(attend_in, d_packed))
+    if paired:
+        kept_mlp, away_mlp = scatter_step(kept_mlp, got, side, 2)
+        d_packed, pairs, away_mlp = lax.optimization_barrier((d_packed, pairs, away_mlp))
+        got_mlp = swap(away_mlp, "fsdp", 1)
+    attend_part = weight_grad(attend_in, d_packed)
+    if paired:
+        kept, away = halves(scatter_parts([attend_part]), core, 4)
+        pairs, away = lax.optimization_barrier((pairs, away))
+        got = swap(away, "rep", 1)
+    table_part = run_table(pairs, index_rows)
+    if paired:
+        kept, away = scatter_step(kept, got, row, 3)
+        kept_mlp, away_mlp = scatter_step(kept_mlp, got_mlp, far, 0)
+        d_packed, away, away_mlp, table_part = lax.optimization_barrier(
+            (d_packed, away, away_mlp, table_part)
+        )
+        got, got_mlp = swap(away, "rep", 2), swap(away_mlp, "fsdp", 4)
     input_grad, sums_one, d_packed_bias = run_input(
         d_packed, win, d_res, gain_one, weight_one, back, inputs.shape
     )
-    table_part = run_table(pairs, index_rows)
     small = (
         sums_one[0], sums_one[1], d_packed_bias[0, :C], d_packed_bias[0, 2 * C :],
         sums_two[2], sums_two[0], sums_two[1], d_exp_bias[0], sums_two[3], table_part.reshape(-1),
     )
     small_sizes = np.cumsum([0] + [s.shape[0] for s in small])
-    summed = lax.psum(jnp.concatenate(small), ("fsdp", "rep"))
+    if paired:
+        pieces, summed = finish(kept_mlp, got_mlp, kept, got, jnp.concatenate(small))
+        output_grad, expand_grad, reduce_grad, attend_grad = run_join(
+            pieces,
+            [w.shape for w in (output_weight, expand_weight, reduce_weight, attend_weight)],
+        )
+    else:
+        output_grad, expand_grad, attend_grad, reduce_grad = (
+            reduce_weight_grad(part)
+            for part in (output_part, expand_part, attend_part, reduce_part)
+        )
+        summed = lax.psum(jnp.concatenate(small), ("fsdp", "rep"))
     parts = [summed[small_sizes[i] : small_sizes[i + 1]] for i in range(len(small))]
     parts = parts[:2] + [jnp.concatenate(parts[2:4])] + parts[4:]
 

time: 523 us -> 277 us (0.53)
  waiting for transfers between devices: 212 us -> 32.6 us
  blocking collectives: 106 us -> 0 us
  starting transfers between devices: 0.72 us -> 26.9 us
  local copies, waits for them, and re-layouts: 35.1 us -> 46.6 us
    reduce_scatter x4 -> x0, waiting for transfers between devices: 157 us -> none  [reduce_weight_grad(): share = lax.psum_scatter(partial, 'fsdp', scatter_dimension=0, tiled=True)]
    all_gather x2 -> x0, blocking collectives: 66.5 us -> none  [gather(): return lax.all_gather(shard, 'fsdp', axis=0, tiled=True)]
    psum x1 -> x0, blocking collectives: 39.7 us -> none  [per_device(): summed = lax.psum(jnp.concatenate(small), ('fsdp', 'rep'))]
    ppermute x0 -> x28, waiting for transfers between devices: none -> 32.6 us  [swap(): lax.ppermute(value, axis, [(i, i ^ bits) for i in range(lax.axis_size(axi...]
    all_gather x3 -> x1, waiting for transfers between devices: 29.4 us -> 0.01 us  [gather_joined(): return lax.all_gather(joined, ('fsdp', 'rep'), axis=0, tiled=True)]
    ppermute x0 -> x28, starting transfers between devices: none -> 26.9 us  [swap(): lax.ppermute(value, axis, [(i, i ^ bits) for i in range(lax.axis_size(axi...]
    psum x1 -> x0, waiting for transfers between devices: 22.8 us -> none  [reduce_weight_grad(): return lax.psum(share, 'rep').astype(F32)]
    unnamed x41 -> x52, local copies, waits for them, and re-layouts: 15.7 us -> 13.8 us
  transfers between devices with their start and end apart: 8 -> 29, of which waited for: 5 -> 13; matrix products, arithmetic and copies ran while one was open for 11% -> 16% of each run, Pallas kernels for 15% -> 30%
where the time goes in v2:
time: 277 us; the launch traced here: 272 us
  Pallas kernels  120 us (43%)
  local copies, waits for them, and re-layouts  46.6 us (17%)
  waiting for transfers between devices  32.6 us (12%)
  starting transfers between devices  26.9 us (10%)
  matrix products  23.3 us (8%)
  between operations  15.6 us (6%)
  other arithmetic  6.72 us (2%)
    pallas_call x1, Pallas kernels, run_mlp(): pl.pallas_call(mlp_kernel, grid=(images,), out_shape=(struct(cotangent.sh...  37.7 us
    ppermute x28, waiting for transfers between devices, swap(): lax.ppermute(value, axis, [(i, i ^ bits) for i in range(lax.axis_size(axi...  32.6 us
    pallas_call x1, Pallas kernels, run_attend(): pl.pallas_call(attend_kernel, grid=(images,), out_shape=(struct((rows, C)...  30.6 us
    ppermute x28, starting transfers between devices, swap(): lax.ppermute(value, axis, [(i, i ^ bits) for i in range(lax.axis_size(axi...  26.9 us
    pallas_call x1, Pallas kernels, run_attend_back(): pl.pallas_call(attend_back_kernel, grid=(images,), out_shape=(struct(pack...  25.6 us
    dot_general x4, matrix products, weight_grad(): lax.dot_general(rows_in, rows_out, (((0,), (0,)), ((), ())), preferred_el...  23.3 us
    unnamed x52, local copies, waits for them, and re-layouts  13.8 us
    pallas_call x1, Pallas kernels, run_input(): pl.pallas_call(input_kernel, grid=(shape[0],), out_shape=(struct(shape, F...  12.8 us
  transfers between devices with their start and end apart: 29, of which 13 were waited for; matrix products, arithmetic and copies ran while one was open for 16% of the time, Pallas kernels for 30%

profile of v2, /device:TPU:0, one launch (start us, length us, event | category | flops | bytes accessed | tf_op | source)
XLA Modules:
  0.0 272.1 jit_solution(17277360849129673171)
XLA Ops:
  7.2 0.9 copy-done
  8.9 0.8 constant_dynamic-slice_fusion.6
  10.4 0.9 constant_dynamic-slice_fusion.9
  11.3 3.0 %collective-permute-start = (bf16[32,1536]{1,0:T(8,128)(2,1)S(1)}, bf16[32,1536]{1,0:T(8,128)(2,1)S(1)}, u32[]{:S(2)}, u32[]{:S(2)}) collective-permute-start(bf16[32,1536]{1,0:T(8,128)(2,1)S(1)} %constant_dynamic-slice_fusion.9), channel_id=1, source_target_pairs={{0,8},{4,12},{8,0},{12,4},{16,24},{20,28},{24,16},{28,20},{1,9},{5... | collective-permute-start | bytes 294920 | tf_op jit(solution)/shard_map/ppermute | solution.py:493
  14.4 2.6 collective-permute-start.1
  17.0 5.4 %concatenate.32 = bf16[768]{0:T(1024)(128)(2,1)S(1)} concatenate(bf16[64]{0:T(256)(128)(2,1)} %param.26, bf16[64]{0:T(256)(128)(2,1)} %param.27, bf16[128]{0:T(256)(128)(2,1)} %param.29, bf16[64]{0:T(256)(128)(2,1)} %param.32, bf16[64]{0:T(256)(128)(2,1)} %param.33, bf16[64]{0:T(256)(128)(2,1)} %param.34, bf16[256]{0:T(256)(128)(2,1)} %param.36, bf16[64]{0:T(256)(128)(2,1)} %param.38), dimensions={0} | concatenate | bytes 3072 | tf_op jit(solution)/shard_map/concatenate | solution.py:678
  22.4 1.9 collective-permute-start.3
  25.0 0.8 copy.67
  27.3 1.3 pad.18.table_ref
  28.6 2.5 collective-permute-start.4
  31.2 5.0 %shard_map.316.pair_ref = f32[16,208,208]{2,1,0:T(8,128)} custom-call(s32[208]{0:T(256)} %pad.16.code_ref, s32[1,208]{1,0:T(1,128)} %bitcast.199, s32[49,208]{1,0:T(8,128)} %pad.17.index_ref, bf16[16,176]{1,0:T(8,128)(2,1)} %pad.18.table_ref), custom_call_target="tpu_custom_call" | custom-call | flops 2000000000 | bytes 4000000 | tf_op jit(solution)/shard_map/pallas_call | solution.py:328
  36.9 1.5 collective-permute-start.5
  40.3 1.8 copy.68.grid_ref
  42.1 1.8 copy.70.grid_ref
  48.8 4.7 %collective-permute-done.7.rest_2_ = bf16[128,1536]{1,0:T(8,128)(2,1)} collective-permute-done((bf16[128,1536]{1,0:T(8,128)(2,1)}, bf16[128,1536]{1,0:T(8,128)(2,1)}, u32[]{:S(2)}, u32[]{:S(2)}) %collective-permute-start.7) | collective-permute-done | bytes 393248 | tf_op jit(solution)/shard_map/ppermute | solution.py:493
  54.1 1.3 collective-permute-done.8.rest_3_
  56.2 30.6 %shard_map.317 = (bf16[1664,512]{1,0:T(8,128)(2,1)}, bf16[1664,512]{1,0:T(8,128)(2,1)}, bf16[1664,1536]{1,0:T(8,128)(2,1)}, bf16[8,16,208,208]{3,2,1,0:T(8,128)(...) custom-call(s32[16]{0:T(128)} %stack.85.starts_ref, bf16[8,14,14,512]{3,2,1,0:T(8,128)(2,1)} %copy.68.grid_ref, ...), custom_call_target="tpu_custom_call" | custom-call | flops 40000000000 | bytes 48000000 | tf_op jit(solution)/shard_map/pallas_call | solution.py:353
  86.8 37.7 %shard_map.318 = (bf16[8,14,14,512]{3,2,1,0:T(8,128)(2,1)}, bf16[1664,2048]{1,0:T(8,128)(2,1)}, bf16[1664,2048]{1,0:T(8,128)(2,1)}, bf16[1664,512]{1,0:T(8,128)(...) custom-call(s32[1]{0:T(128)} %bitcast.169.count_ref, ...), custom_call_target="tpu_custom_call" | custom-call | flops 48000000000 | bytes 32000000 | tf_op jit(solution)/shard_map/pallas_call | solution.py:392
  124.6 2.7 convolution_convert_fusion.3
  127.3 7.4 %convolution_convert_fusion = bf16[2048,512]{1,0:T(8,128)(2,1)S(1)} fusion(bf16[1664,2048]{1,0:T(8,128)(2,1)} %get-tuple-element.84, bf16[1664,512]{1,0:T(8,128)(2,1)S(1)} %copy-done.18), kind=kOutput, calls=%fused_computation.1 | convolution fusion | flops 3490709504 | bytes 10616832 | tf_op jit(solution)/shard_map/dot_general | solution.py:483
  134.7 2.0 copy.105
  136.7 2.8 %reshape.247 = bf16[2,2,2,2,2,16,2048]{6,5,4,3,2,1,0:T(8,128)(2,1)} reshape(bf16[32,16,4,512]{3,2,1,0:T(4,128)(2,1)S(1)} %bitcast.170) | data formatting | bytes 4194304 | tf_op jit(solution)/shard_map/reshape | solution.py:555
  139.5 7.6 %convolution_convert_fusion.1 = bf16[512,2048]{1,0:T(8,128)(2,1)S(1)} fusion(bf16[1664,512]{1,0:T(8,128)(2,1)} %get-tuple-element.82, bf16[1664,2048]{1,0:T(8,128)(2,1)} %get-tuple-element.83), kind=kOutput, calls=%fused_computation.2 | convolution fusion | flops 3490709504 | bytes 10616832 | tf_op jit(solution)/shard_map/dot_general | solution.py:483
  147.7 1.9 copy-done.2
  149.8 1.8 constant_dynamic-slice_fusion.3
  151.6 2.7 collective-permute-done.9
  154.3 2.4 fusion
  156.7 1.6 collective-permute-start.10
  158.2 25.6 %shard_map.319 = (bf16[1664,1536]{1,0:T(8,128)(2,1)}, f32[16,208,208]{2,1,0:T(8,128)}) custom-call(bf16[1664,1536]{1,0:T(8,128)(2,1)} %get-tuple-element.78.packed_ref, bf16[8,16,208,208]{3,2,1,0:T(8,128)(2,1)} %get-tuple-element.79.soft_ref, bf16[1664,512]{1,0:T(8,128)(2,1)} %get-tuple-element.86.d_att_ref), custom_call_target="tpu_custom_call" | custom-call | flops 48000000000 | bytes 48000000 | tf_op jit(solution)/shard_map/pallas_call | solution.py:447
  185.8 5.5 %convolution_convert_fusion.2 = bf16[512,1536]{1,0:T(8,128)(2,1)S(1)} fusion(bf16[1664,512]{1,0:T(8,128)(2,1)S(1)} %copy-done.17, bf16[1664,1536]{1,0:T(8,128)(2,1)} %get-tuple-element.96.d_packed_ref), kind=kOutput, calls=%fused_computation.3 | convolution fusion | flops 2618032128 | bytes 8388608 | tf_op jit(solution)/shard_map/dot_general | solution.py:483
  191.6 6.4 %shard_map.320 = f32[16,176]{1,0:T(8,128)} custom-call(f32[16,208,208]{2,1,0:T(8,128)} %get-tuple-element.95.sums_ref, s32[49,208]{1,0:T(8,128)} %pad.17.index_ref), custom_call_target="tpu_custom_call" | custom-call | flops 2000000000 | bytes 4000000 | tf_op jit(solution)/shard_map/pallas_call | solution.py:339
  198.0 1.6 collective-permute-done.12
  200.4 1.6 collective-permute-start.14
  202.3 12.8 %shard_map.321 = (f32[8,14,14,512]{3,2,1,0:T(8,128)}, f32[8,512]{1,0:T(8,128)}, f32[1,1536]{1,0:T(1,128)}) custom-call(bf16[1664,1536]{1,0:T(8,128)(2,1)} %get-tuple-element.96.d_packed_ref, bf16[1664,512]{1,0:T(8,128)(2,1)} %get-tuple-element.74.win_ref, f32[1664,512]{1,0:T(8,128)} %get-tuple-element.97.d_res_ref, f32[1,512]{1,0:T(1,128)} %reshape.236.gain_ref, ...), custom_call_target="tpu_custom_call" | custom-call | flops 8000000000 | bytes 16000000 | tf_op jit(solution)/shard_map/pallas_call | solution.py:463
  216.8 1.3 collective-permute-start.16
  218.1 4.3 %collective-permute-done.15 = bf16[16,4608]{1,0:T(8,128)(2,1)S(1)} collective-permute-done((bf16[16,4608]{1,0:T(8,128)(2,1)S(1)}, bf16[16,4608]{1,0:T(8,128)(2,1)S(1)}, u32[]{:S(2)}, u32[]{:S(2)}) %collective-permute-start.15) | collective-permute-done | bytes 147488 | tf_op jit(solution)/shard_map/ppermute | solution.py:493
  222.5 1.6 collective-permute-done.16
  224.2 2.5 collective-permute-start.19
  227.2 3.4 %collective-permute-done.20 = f32[72,128]{1,0:T(8,128)S(1)} collective-permute-done((f32[72,128]{1,0:T(8,128)S(1)}, f32[72,128]{1,0:T(8,128)S(1)}, u32[]{:S(2)}, u32[]{:S(2)}) %collective-permute-start.20) | collective-permute-done | bytes 36896 | tf_op jit(solution)/shard_map/ppermute | solution.py:493
  230.6 1.3 collective-permute-done.19
  232.5 0.8 collective-permute-start.23
  233.8 2.6 collective-permute-done.23
  236.5 4.9 %collective-permute-done.21.refs_1_ = bf16[2,16,4608]{2,1,0:T(8,128)(2,1)S(1)} collective-permute-done((bf16[2,16,4608]{2,1,0:T(8,128)(2,1)S(1)}, bf16[2,16,4608]{2,1,0:T(8,128)(2,1)S(1)}, u32[]{:S(2)}, u32[]{:S(2)}) %collective-permute-start.21) | collective-permute-done | bytes 294944 | tf_op jit(solution)/shard_map/ppermute | solution.py:493
  241.4 3.4 %collective-permute-start.25 = (f32[72,128]{1,0:T(8,128)S(1)}, f32[72,128]{1,0:T(8,128)S(1)}, u32[]{:S(2)}, u32[]{:S(2)}) collective-permute-start(f32[72,128]{1,0:T(8,128)S(1)} %add.338), channel_id=1, source_target_pairs={{0,16},{4,20},{8,24},{12,28},{16,0},{20,4},{24,8},{28,12},{1,17},{... | collective-permute-start | bytes 110600 | tf_op jit(solution)/shard_map/ppermute | solution.py:493
  244.8 2.7 %collective-permute-done.25 = f32[72,128]{1,0:T(8,128)S(1)} collective-permute-done((f32[72,128]{1,0:T(8,128)S(1)}, f32[72,128]{1,0:T(8,128)S(1)}, u32[]{:S(2)}, u32[]{:S(2)}) %collective-permute-start.25) | collective-permute-done | bytes 36896 | tf_op jit(solution)/shard_map/ppermute | solution.py:493
  247.6 2.2 copy.78
  249.8 6.3 %copy.79 = f32[8,14,14,512]{3,0,2,1:T(8,128)} copy(f32[8,14,14,512]{3,2,1,0:T(8,128)} %get-tuple-element.171) | data formatting | bytes 6422528
  262.7 2.3 shard_map.322
  (155 shorter events, 25.8 us)
Async XLA Ops:
  7.2 1.0 copy-start
  7.2 79.6 %all-gather.2.cloned.1.call-start = ((), (), s32[]{:S(2)}) async-start(), calls=%async_computation | async-start | bytes 4866048 | tf_op jit(solution)/shard_map/all_gather | solution.py:538
  11.3 24.8 %collective-permute-start = (bf16[32,1536]{1,0:T(8,128)(2,1)S(1)}, bf16[32,1536]{1,0:T(8,128)(2,1)S(1)}, u32[]{:S(2)}, u32[]{:S(2)}) collective-permute-start(bf16[32,1536]{1,0:T(8,128)(2,1)S(1)} %constant_dynamic-slice_fusion.9), channel_id=1, source_target_pairs={{0,8},{4,12},{8,0},{12,4},{16,24},{20,28},{24,16},{28,20},{1,9},{5... | collective-permute-start | bytes 294920 | tf_op jit(solution)/shard_map/ppermute | solution.py:493
  14.4 21.8 %collective-permute-start.1 = (bf16[32,1536]{1,0:T(8,128)(2,1)S(1)}, bf16[32,1536]{1,0:T(8,128)(2,1)S(1)}, u32[]{:S(2)}, u32[]{:S(2)}) collective-permute-start(bf16[32,1536]{1,0:T(8,128)(2,1)S(1)} %constant_dynamic-slice_fusion.9), channel_id=1, source_target_pairs={{0,16},{4,20},{8,24},{12,28},{16,0},{20,4},{24,8},{28,12},{1,17},{... | collective-permute-start | bytes 294920 | tf_op jit(solution)/shard_map/ppermute | solution.py:493
  16.9 19.2 %collective-permute-start.2 = (bf16[32,1536]{1,0:T(8,128)(2,1)S(1)}, bf16[32,1536]{1,0:T(8,128)(2,1)S(1)}, u32[]{:S(2)}, u32[]{:S(2)}) collective-permute-start(bf16[32,1536]{1,0:T(8,128)(2,1)S(1)} %constant_dynamic-slice_fusion.9), channel_id=1, source_target_pairs={{0,24},{4,28},{8,16},{12,20},{16,8},{20,12},{24,0},{28,4},{1,25},{... | collective-permute-start | bytes 294920 | tf_op jit(solution)/shard_map/ppermute | solution.py:493
  22.4 6.2 %collective-permute-start.3 = (bf16[1,6,128]{2,1,0:T(8,128)(2,1)S(1)}, bf16[1,6,128]{2,1,0:T(8,128)(2,1)S(1)}, u32[]{:S(2)}, u32[]{:S(2)}) collective-permute-start(bf16[1,6,128]{2,1,0:T(8,128)(2,1)S(1)} %bitcast.184), channel_id=1, source_target_pairs={{0,16},{4,20},{8,24},{12,28},{16,0},{20,4},{24,8},{28,12},{1,17},{... | collective-permute-start | bytes 4616 | tf_op jit(solution)/shard_map/ppermute | solution.py:493
  28.6 7.5 %collective-permute-start.4 = (bf16[2,6,128]{2,1,0:T(8,128)(2,1)S(1)}, bf16[2,6,128]{2,1,0:T(8,128)(2,1)S(1)}, u32[]{:S(2)}, u32[]{:S(2)}) collective-permute-start(bf16[2,6,128]{2,1,0:T(8,128)(2,1)S(1)} %pad_maximum_fusion.6), channel_id=1, source_target_pairs={{0,8},{4,12},{8,0},{12,4},{16,24},{20,28},{24,16},{28,20},{1,9},{5... | collective-permute-start | bytes 9224 | tf_op jit(solution)/shard_map/ppermute | solution.py:493
  31.1 7.3 %copy-start.15 = (s32[8]{0:T(128)S(1)}, s32[8]{0:T(128)}, u32[]{:S(2)}) copy-start(s32[8]{0:T(128)} %constant.336.clone) | copy-start | bytes 100
  31.2 9.2 %copy-start.6 = (bf16[8,14,14,512]{3,0,2,1:T(8,128)(2,1)S(1)}, bf16[8,14,14,512]{3,0,2,1:T(8,128)(2,1)}, u32[]{:S(2)}) copy-start(bf16[8,14,14,512]{3,0,2,1:T(8,128)(2,1)} %param.21) | copy-start | bytes 4816900
  36.9 5.2 %copy-start.7 = (bf16[8,14,14,512]{3,0,2,1:T(8,128)(2,1)S(1)}, bf16[8,14,14,512]{3,0,2,1:T(8,128)(2,1)}, u32[]{:S(2)}) copy-start(bf16[8,14,14,512]{3,0,2,1:T(8,128)(2,1)} %param.22) | copy-start | bytes 4816900
  36.9 7.0 %collective-permute-start.5 = (bf16[4,6,128]{2,1,0:T(8,128)(2,1)S(1)}, bf16[4,6,128]{2,1,0:T(8,128)(2,1)S(1)}, u32[]{:S(2)}, u32[]{:S(2)}) collective-permute-start(bf16[4,6,128]{2,1,0:T(8,128)(2,1)S(1)} %pad_maximum_fusion.5), channel_id=1, source_target_pairs={{0,4},{4,0},{8,12},{12,8},{16,20},{20,16},{24,28},{28,24},{1,5},{5... | collective-permute-start | bytes 18440 | tf_op jit(solution)/shard_map/ppermute | solution.py:493
  39.8 13.7 %collective-permute-start.7 = (bf16[128,1536]{1,0:T(8,128)(2,1)}, bf16[128,1536]{1,0:T(8,128)(2,1)}, u32[]{:S(2)}, u32[]{:S(2)}) collective-permute-start(bf16[128,1536]{1,0:T(8,128)(2,1)} %pad_maximum_fusion.1.rest_0_), channel_id=1, source_target_pairs={{0,4},{4,0},{8,12},{12,8},{16,20},{20,16},{24,28},{28,24},{1,5},{5... | collective-permute-start | bytes 1179656 | tf_op jit(solution)/shard_map/ppermute | solution.py:493
  40.3 13.8 %collective-permute-start.6 = (bf16[128,1536]{1,0:T(8,128)(2,1)}, bf16[128,1536]{1,0:T(8,128)(2,1)}, u32[]{:S(2)}, u32[]{:S(2)}) collective-permute-start(bf16[128,1536]{1,0:T(8,128)(2,1)} %pad_maximum_fusion.1.rest_0_), channel_id=1, source_target_pairs={{0,1},{1,0},{2,3},{3,2},{4,5},{5,4},{6,7},{7,6},{8,9},{9,8},{10,11... | collective-permute-start | bytes 1179656 | tf_op jit(solution)/shard_map/ppermute | solution.py:493
  53.5 1.9 collective-permute-start.8
  55.4 0.7 copy-start.16
  86.8 37.7 %copy-start.5 = (bf16[1664,512]{1,0:T(8,128)(2,1)S(1)}, bf16[1664,512]{1,0:T(8,128)(2,1)}, u32[]{:S(2)}) copy-start(bf16[1664,512]{1,0:T(8,128)(2,1)} %get-tuple-element.75.merged_ref) | copy-start | bytes 5111812
  124.6 2.7 %copy-start.18 = (bf16[1664,512]{1,0:T(8,128)(2,1)S(1)}, bf16[1664,512]{1,0:T(8,128)(2,1)}, u32[]{:S(2)}) copy-start(bf16[1664,512]{1,0:T(8,128)(2,1)} %get-tuple-element.85) | copy-start | bytes 5111812
  139.5 7.6 %copy-start.3 = (bf16[2,2,2,2,2,16,2048]{6,5,4,3,2,1,0:T(8,128)(2,1)S(1)}, bf16[2,2,2,2,2,16,2048]{6,5,4,3,2,1,0:T(8,128)(2,1)}, u32[]{:S(2)}) copy-start(bf16[2,2,2,2,2,16,2048]{6,5,4,3,2,1,0:T(8,128)(2,1)} %reshape.247) | copy-start | bytes 6291460
  147.5 2.1 copy-start.2
  147.5 2.3 copy-start.14
  149.6 4.7 %collective-permute-start.9 = (bf16[2,2,2,2,16,4608]{5,4,1,2,0,3:T(8,128)(2,1)S(1)}, bf16[2,2,2,2,16,4608]{5,4,1,2,0,3:T(8,128)(2,1)}, u32[]{:S(2)}, u32[]{:S(2)}) collective-permute-start(bf16[2,2,2,2,16,4608]{5,4,1,2,0,3:T(8,128)(2,1)S(1)} %copy_bitcast_fusion), channel_id=1, source_target_pairs={{0,1},{1,0},{2,3},{3,2},{4,5},{5,4},{6,7},{7,6},{8,9},{9,8},{10,11... | collective-permute-start | bytes 7077896 | tf_op jit(solution)/shard_map/ppermute | solution.py:493
  156.7 28.1 %collective-permute-start.10 = (bf16[2,2,2,16,4608]{4,3,1,2,0:T(8,128)(2,1)S(1)}, bf16[2,2,2,16,4608]{4,3,1,2,0:T(8,128)(2,1)S(1)}, u32[]{:S(2)}, u32[]{:S(2)}) collective-permute-start(bf16[2,2,2,16,4608]{4,3,1,2,0:T(8,128)(2,1)S(1)} %get-tuple-element.89), channel_id=1, source_target_pairs={{0,2},{1,3},{2,0},{3,1},{4,6},{5,7},{6,4},{7,5},{8,10},{9,11},{10,... | collective-permute-start | bytes 3538952 | tf_op jit(solution)/shard_map/ppermute | solution.py:493
  183.9 1.9 copy-start.17
  185.0 14.6 %collective-permute-start.12 = (bf16[2,2,16,4608]{3,2,1,0:T(8,128)(2,1)S(1)}, bf16[2,2,16,4608]{3,2,1,0:T(8,128)(2,1)S(1)}, u32[]{:S(2)}, u32[]{:S(2)}) collective-permute-start(bf16[2,2,16,4608]{3,2,1,0:T(8,128)(2,1)S(1)} %get-tuple-element.94), channel_id=1, source_target_pairs={{0,4},{4,0},{8,12},{12,8},{16,20},{20,16},{24,28},{28,24},{1,5},{5... | collective-permute-start | bytes 1769480 | tf_op jit(solution)/shard_map/ppermute | solution.py:493
  191.4 8.3 %collective-permute-start.11 = (bf16[2,2,2,2,16,1536]{5,4,1,2,0,3:T(8,128)(2,1)S(1)}, bf16[2,2,2,2,16,1536]{5,4,1,2,0,3:T(8,128)(2,1)S(1)}, u32[]{:S(2)}, u32[]{:S(2)}) collective-permute-start(bf16[2,2,2,2,16,1536]{5,4,1,2,0,3:T(8,128)(2,1)S(1)} %copy_bitcast_fusion.4), channel_id=1, source_target_pairs={{0,1},{1,0},{2,3},{3,2},{4,5},{5,4},{6,7},{7,6},{8,9},{9,8},{10,11... | collective-permute-start | bytes 2359304 | tf_op jit(solution)/shard_map/ppermute | solution.py:493
  199.6 0.7 copy-start.12
  200.4 16.1 %collective-permute-start.14 = (bf16[2,2,2,16,1536]{4,3,1,2,0:T(8,128)(2,1)S(1)}, bf16[2,2,2,16,1536]{4,3,1,2,0:T(8,128)(2,1)S(1)}, u32[]{:S(2)}, u32[]{:S(2)}) collective-permute-start(bf16[2,2,2,16,1536]{4,3,1,2,0:T(8,128)(2,1)S(1)} %get-tuple-element.101), channel_id=1, source_target_pairs={{0,2},{1,3},{2,0},{3,1},{4,6},{5,7},{6,4},{7,5},{8,10},{9,11},{10,... | collective-permute-start | bytes 1179656 | tf_op jit(solution)/shard_map/ppermute | solution.py:493
  202.0 14.5 %collective-permute-start.13 = (bf16[2,16,4608]{2,1,0:T(8,128)(2,1)S(1)}, bf16[2,16,4608]{2,1,0:T(8,128)(2,1)S(1)}, u32[]{:S(2)}, u32[]{:S(2)}) collective-permute-start(bf16[2,16,4608]{2,1,0:T(8,128)(2,1)S(1)} %get-tuple-element.100), channel_id=1, source_target_pairs={{0,16},{4,20},{8,24},{12,28},{16,0},{20,4},{24,8},{28,12},{1,17},{... | collective-permute-start | bytes 884744 | tf_op jit(solution)/shard_map/ppermute | solution.py:493
  202.3 13.7 %copy-start.13 = (f32[1,2048]{1,0:T(1,128)S(1)}, f32[1,2048]{1,0:T(1,128)}, u32[]{:S(2)}) copy-start(f32[1,2048]{1,0:T(1,128)} %get-tuple-element.105) | copy-start | bytes 24580
  216.5 31.1 %copy-start.4 = (bf16[8,14,14,512]{3,2,1,0:T(8,128)(2,1)S(1)}, bf16[8,14,14,512]{3,2,1,0:T(8,128)(2,1)}, u32[]{:S(2)}) copy-start(bf16[8,14,14,512]{3,2,1,0:T(8,128)(2,1)} %get-tuple-element.170) | copy-start | bytes 4816900
  216.6 5.8 %collective-permute-start.15 = (bf16[16,4608]{1,0:T(8,128)(2,1)S(1)}, bf16[16,4608]{1,0:T(8,128)(2,1)S(1)}, u32[]{:S(2)}, u32[]{:S(2)}) collective-permute-start(bf16[16,4608]{1,0:T(8,128)(2,1)S(1)} %fusion.15), channel_id=1, source_target_pairs={{0,8},{4,12},{8,0},{12,4},{16,24},{20,28},{24,16},{28,20},{1,9},{5... | collective-permute-start | bytes 442376 | tf_op jit(solution)/shard_map/ppermute | solution.py:493
  216.8 1.3 collective-permute-start.17
  216.8 7.3 %collective-permute-start.16 = (bf16[2,2,16,1536]{3,2,1,0:T(8,128)(2,1)S(1)}, bf16[2,2,16,1536]{3,2,1,0:T(8,128)(2,1)S(1)}, u32[]{:S(2)}, u32[]{:S(2)}) collective-permute-start(bf16[2,2,16,1536]{3,2,1,0:T(8,128)(2,1)S(1)} %get-tuple-element.108), channel_id=1, source_target_pairs={{0,4},{4,0},{8,12},{12,8},{16,20},{20,16},{24,28},{28,24},{1,5},{5... | collective-permute-start | bytes 589832 | tf_op jit(solution)/shard_map/ppermute | solution.py:493
  224.2 7.7 %collective-permute-start.19 = (bf16[2,16,1536]{2,1,0:T(8,128)(2,1)S(1)}, bf16[2,16,1536]{2,1,0:T(8,128)(2,1)S(1)}, u32[]{:S(2)}, u32[]{:S(2)}) collective-permute-start(bf16[2,16,1536]{2,1,0:T(8,128)(2,1)S(1)} %get-tuple-element.111), channel_id=1, source_target_pairs={{0,16},{4,20},{8,24},{12,28},{16,0},{20,4},{24,8},{28,12},{1,17},{... | collective-permute-start | bytes 294920 | tf_op jit(solution)/shard_map/ppermute | solution.py:493
  226.7 4.0 %collective-permute-start.20 = (f32[72,128]{1,0:T(8,128)S(1)}, f32[72,128]{1,0:T(8,128)S(1)}, u32[]{:S(2)}, u32[]{:S(2)}) collective-permute-start(f32[72,128]{1,0:T(8,128)S(1)} %add.332), channel_id=1, source_target_pairs={{0,2},{1,3},{2,0},{3,1},{4,6},{5,7},{6,4},{7,5},{8,10},{9,11},{10,... | collective-permute-start | bytes 110600 | tf_op jit(solution)/shard_map/ppermute | solution.py:493
  227.2 4.7 %collective-permute-start.18 = (bf16[16,4608]{1,0:T(8,128)(2,1)S(1)}, bf16[16,4608]{1,0:T(8,128)(2,1)S(1)}, u32[]{:S(2)}, u32[]{:S(2)}) collective-permute-start(bf16[16,4608]{1,0:T(8,128)(2,1)S(1)} %fusion.9), channel_id=1, source_target_pairs={{0,1},{1,0},{2,3},{3,2},{4,5},{5,4},{6,7},{7,6},{8,9},{9,8},{10,11... | collective-permute-start | bytes 442376 | tf_op jit(solution)/shard_map/ppermute | solution.py:493
  232.0 17.9 %copy-start.8 = (bf16[2,16,4608]{2,1,0:T(8,128)(2,1)}, bf16[2,16,4608]{2,1,0:T(8,128)(2,1)S(1)}, u32[]{:S(2)}) copy-start(bf16[2,16,4608]{2,1,0:T(8,128)(2,1)S(1)} %pad_maximum_fusion.2.refs_0_) | copy-start | bytes 884740
  232.0 4.5 %collective-permute-start.22 = (bf16[16,1536]{1,0:T(8,128)(2,1)S(1)}, bf16[16,1536]{1,0:T(8,128)(2,1)S(1)}, u32[]{:S(2)}, u32[]{:S(2)}) collective-permute-start(bf16[16,1536]{1,0:T(8,128)(2,1)S(1)} %fusion.20), channel_id=1, source_target_pairs={{0,8},{4,12},{8,0},{12,4},{16,24},{20,28},{24,16},{28,20},{1,9},{5... | collective-permute-start | bytes 147464 | tf_op jit(solution)/shard_map/ppermute | solution.py:493
  232.5 4.0 %collective-permute-start.23 = (f32[72,128]{1,0:T(8,128)S(1)}, f32[72,128]{1,0:T(8,128)S(1)}, u32[]{:S(2)}, u32[]{:S(2)}) collective-permute-start(f32[72,128]{1,0:T(8,128)S(1)} %add.335), channel_id=1, source_target_pairs={{0,4},{4,0},{8,12},{12,8},{16,20},{20,16},{24,28},{28,24},{1,5},{5... | collective-permute-start | bytes 110600 | tf_op jit(solution)/shard_map/ppermute | solution.py:493
  233.3 8.0 %collective-permute-start.21 = (bf16[2,16,4608]{2,1,0:T(8,128)(2,1)S(1)}, bf16[2,16,4608]{2,1,0:T(8,128)(2,1)S(1)}, u32[]{:S(2)}, u32[]{:S(2)}) collective-permute-start(bf16[2,16,4608]{2,1,0:T(8,128)(2,1)S(1)} %pad_maximum_fusion.2.refs_0_), channel_id=1, source_target_pairs={{0,2},{1,3},{2,0},{3,1},{4,6},{5,7},{6,4},{7,5},{8,10},{9,11},{10,... | collective-permute-start | bytes 884744 | tf_op jit(solution)/shard_map/ppermute | solution.py:493
  241.4 8.5 %copy-start.10 = (bf16[2,16,4608]{2,1,0:T(8,128)(2,1)}, bf16[2,16,4608]{2,1,0:T(8,128)(2,1)S(1)}, u32[]{:S(2)}) copy-start(bf16[2,16,4608]{2,1,0:T(8,128)(2,1)S(1)} %collective-permute-done.21.refs_1_) | copy-start | bytes 884740
  241.4 6.1 %collective-permute-start.24 = (bf16[16,1536]{1,0:T(8,128)(2,1)S(1)}, bf16[16,1536]{1,0:T(8,128)(2,1)S(1)}, u32[]{:S(2)}, u32[]{:S(2)}) collective-permute-start(bf16[16,1536]{1,0:T(8,128)(2,1)S(1)} %fusion.17), channel_id=1, source_target_pairs={{0,1},{1,0},{2,3},{3,2},{4,5},{5,4},{6,7},{7,6},{8,9},{9,8},{10,11... | collective-permute-start | bytes 147464 | tf_op jit(solution)/shard_map/ppermute | solution.py:493
  241.4 6.1 %collective-permute-start.25 = (f32[72,128]{1,0:T(8,128)S(1)}, f32[72,128]{1,0:T(8,128)S(1)}, u32[]{:S(2)}, u32[]{:S(2)}) collective-permute-start(f32[72,128]{1,0:T(8,128)S(1)} %add.338), channel_id=1, source_target_pairs={{0,16},{4,20},{8,24},{12,28},{16,0},{20,4},{24,8},{28,12},{1,17},{... | collective-permute-start | bytes 110600 | tf_op jit(solution)/shard_map/ppermute | solution.py:493
  247.5 8.6 %copy-start.9 = (bf16[2,16,1536]{2,1,0:T(8,128)(2,1)}, bf16[2,16,1536]{2,1,0:T(8,128)(2,1)S(1)}, u32[]{:S(2)}) copy-start(bf16[2,16,1536]{2,1,0:T(8,128)(2,1)S(1)} %pad_maximum_fusion.4.refs_2_) | copy-start | bytes 294916
  247.5 9.1 %collective-permute-start.26 = (f32[72,128]{1,0:T(8,128)S(1)}, f32[72,128]{1,0:T(8,128)S(1)}, u32[]{:S(2)}, u32[]{:S(2)}) collective-permute-start(f32[72,128]{1,0:T(8,128)S(1)} %add.339), channel_id=1, source_target_pairs={{0,8},{4,12},{8,0},{12,4},{16,24},{20,28},{24,16},{28,20},{1,9},{5... | collective-permute-start | bytes 110600 | tf_op jit(solution)/shard_map/ppermute | solution.py:493
  249.8 15.2 %copy-start.1 = (bf16[64,2048]{1,0:T(8,128)(2,1)S(1)}, bf16[64,2048]{1,0:T(8,128)(2,1)}, u32[]{:S(2)}) copy-start(bf16[64,2048]{1,0:T(8,128)(2,1)} %param.35) | copy-start | bytes 786436
  256.1 6.0 %collective-permute-start.27 = (bf16[2,16,1536]{2,1,0:T(8,128)(2,1)S(1)}, bf16[2,16,1536]{2,1,0:T(8,128)(2,1)S(1)}, u32[]{:S(2)}, u32[]{:S(2)}) collective-permute-start(bf16[2,16,1536]{2,1,0:T(8,128)(2,1)S(1)} %pad_maximum_fusion.4.refs_2_), channel_id=1, source_target_pairs={{0,2},{1,3},{2,0},{3,1},{4,6},{5,7},{6,4},{7,5},{8,10},{9,11},{10,... | collective-permute-start | bytes 294920 | tf_op jit(solution)/shard_map/ppermute | solution.py:493
  262.1 0.6 copy-start.11
Sparse Core Ops, SparseCore 0:
  11.5 68.5 all-gather.1

commit v3 on v2

v3 whole, which is shorter than its diff:
```python
import jax
import jax.numpy as jnp
import numpy as np
from jax import lax
from jax.experimental import pallas as pl
from jax.experimental.pallas import tpu as pltpu
from jax.sharding import PartitionSpec as P

C = 512
HEADS = 16
HEAD_DIM = 32
WIN = 7
SHIFT = 3
IMG = 14
WINDOWS = 4
TOKW = 49
TABLE = 169

TOK = IMG * IMG
ROWS = 208
RAW = 224
GROUP = 4
LANES = GROUP * HEAD_DIM
TABLE_PAD = 176

epsilon = 1e-05
blocked = -1e30
scale = HEAD_DIM ** (-0.5)
log2e = 1.4426950408889634
VMEM_BYTES = 56 * 1024 * 1024

F32 = jnp.float32
BF16 = jnp.bfloat16


def window_order():
    matrix = np.zeros((ROWS, RAW), np.float32)
    at = 0
    for wy in range(IMG // WIN):
        for wx in range(IMG // WIN):
            for ry in range(WIN):
                for rx in range(WIN):
                    gy = (wy * WIN + ry + SHIFT) % IMG
                    gx = (wx * WIN + rx + SHIFT) % IMG
                    matrix[at, 16 * gy + gx] = 1.0
                    at += 1
    return matrix


def dot(a, b):
    return jnp.dot(a, b, preferred_element_type=F32)


def dot_nt(a, b):
    return lax.dot_general(a, b, (((1,), (1,)), ((), ())), preferred_element_type=F32)


def turned(block):
    return block.astype(F32).T.astype(BF16)


def row_stats(values):
    centred = values - jnp.mean(values, axis=-1, keepdims=True)
    inverse = lax.rsqrt(jnp.mean(centred * centred, axis=-1, keepdims=True) + epsilon)
    return centred * inverse, inverse


def norm_pull(upstream, gain, unit, inverse):
    scaled = upstream * gain
    adjusted = (
        scaled
        - jnp.mean(scaled, axis=-1, keepdims=True)
        - unit * jnp.mean(scaled * unit, axis=-1, keepdims=True)
    )
    return adjusted * inverse


def column_sum(values):
    return jnp.sum(values, axis=0, keepdims=True)


def head_stack(block):
    lane = lax.broadcasted_iota(jnp.int32, block.shape, 1) // HEAD_DIM
    return jnp.concatenate(
        [jnp.where(lane == h, block, jnp.zeros_like(block)) for h in range(GROUP)], axis=0
    )


def head_pick(stacked):
    lane = lax.broadcasted_iota(jnp.int32, (ROWS, LANES), 1) // HEAD_DIM
    picked = stacked[:ROWS]
    for h in range(1, GROUP):
        picked = jnp.where(lane == h, stacked[h * ROWS : (h + 1) * ROWS], picked)
    return picked


def load_grid(grid_ref, rows_ref, order):
    @pl.when(pl.program_id(0) == 0)
    def _():
        rows_ref[...] = jnp.zeros_like(rows_ref)

    images = grid_ref.shape[0]
    for i in range(images):
        for r in range(IMG):
            at = RAW * i + 16 * r
            rows_ref[at : at + IMG, :] = grid_ref[i, r]
    return jnp.concatenate(
        [dot(order, rows_ref[RAW * i : RAW * (i + 1), :]) for i in range(images)], axis=0
    )


def chunk_place(j):
    return j % 2 * 8 + j // 2 % 2 * 4 + j // 8 * 2 + j // 4 % 2


def write_chunks(outs, core, sums_ref, col):
    cols = sums_ref.shape[1]
    for j in range(sums_ref.shape[0] // 32):
        for out, bit in zip(outs, (core, 1 - core)):
            start = pl.multiple_of(16 * (2 * j + bit), 16)
            out[chunk_place(j), :, col : col + cols] = sums_ref[pl.ds(start, 16), :].astype(BF16)


def bias_kernel(code_ref, codes_ref, index_ref, table_ref, out_ref):
    out_ref[...] = jnp.full(out_ref.shape, blocked, F32)
    entry = lax.broadcasted_iota(jnp.int32, (TABLE_PAD, ROWS), 0)
    codes = codes_ref[...]
    table = table_ref[...]
    for j in range(TOKW):
        hot = (entry == index_ref[j : j + 1, :]).astype(F32).astype(BF16)
        found = dot(table, hot) * log2e
        for w in range(WINDOWS):
            row = TOKW * w + j
            out_ref[:, row, :] = jnp.where(codes == code_ref[row], found, blocked)


def table_kernel(sums_ref, index_ref, out_ref, window_ref):
    for h in range(HEADS):
        part = sums_ref[h, :TOKW, :]
        for w in range(1, WINDOWS):
            part = part + sums_ref[h, TOKW * w : TOKW * (w + 1), :]
        window_ref[h, :TOKW, :] = part
    entry = lax.broadcasted_iota(jnp.int32, (TABLE_PAD, ROWS), 0)
    total = jnp.zeros((2 * HEADS, TABLE_PAD), F32)
    for j in range(TOKW):
        part = window_ref[:, j, :]
        hot = (entry == index_ref[j : j + 1, :]).astype(F32).astype(BF16)
        high = part.astype(BF16)
        low = (part - high.astype(F32)).astype(BF16)
        total = total + dot_nt(jnp.concatenate([high, low], axis=0), hot)
    out_ref[...] = total[:HEADS] + total[HEADS:]


def attend_kernel(starts_ref, grid_ref, order_ref, rows_in_ref, bias_ref, pair_ref, *rest):
    pieces = rest[:-7]
    win_ref, in_ref, packed_ref, soft_ref, merged_ref, weight_ref, rows_ref = rest[-7:]

    @pl.when(pl.program_id(0) == 0)
    def _():
        rows = weight_ref.shape[0] // starts_ref.shape[0]
        at = 0
        for piece in pieces:
            for r in range(0, piece.shape[0], rows):
                start = pl.multiple_of(starts_ref[at], rows)
                weight_ref[pl.ds(start, rows), :] = piece[r : r + rows, :]
                at += 1

    values = load_grid(grid_ref, rows_ref, order_ref[...])
    win_ref[...] = values.astype(BF16)
    unit, _ = row_stats(values)
    attend_in = (unit * rows_in_ref[0:1, :] + rows_in_ref[1:2, :]).astype(BF16)
    in_ref[...] = attend_in
    packed_ref[...] = (dot(attend_in, weight_ref[...]) + bias_ref[...]).astype(BF16)
    for g in range(HEADS // GROUP):
        at = LANES * g
        q = packed_ref[:, at : at + LANES]
        k = packed_ref[:, C + at : C + at + LANES]
        v_turned = turned(packed_ref[:, 2 * C + at : 2 * C + at + LANES])
        raw = dot_nt(head_stack(k), q)
        parts = []
        for h in range(GROUP):
            s = raw[h * ROWS : (h + 1) * ROWS] * (scale * log2e) + pair_ref[g * GROUP + h]
            e = jnp.exp2(s - jnp.max(s, axis=0, keepdims=True))
            p = (e * (1.0 / column_sum(e))).astype(BF16)
            soft_ref[0, g * GROUP + h] = p
            parts.append(dot(v_turned[h * HEAD_DIM : (h + 1) * HEAD_DIM], p))
        merged_ref[:, at : at + LANES] = jnp.concatenate(parts, axis=0).T.astype(BF16)


def mlp_kernel(
    count_ref, win_ref, merged_ref, grid_ref, order_ref, back_ref, six_ref, exp_b_ref, joined_ref,
    block_ref, d_res_ref, d_att_ref, kept_ref, away_ref,
    sums_ref, wide_ref, rows_ref, red_w_ref, out_sum_ref, exp_sum_ref, red_sum_ref,
):
    step_at = pl.program_id(0)
    images = grid_ref.shape[0]
    out_b, gain, shift, red_b = (six_ref[r : r + 1, :] for r in (2, 3, 4, 5))
    mlp = exp_b_ref.shape[1]
    blocks = mlp // C
    out_w_ref = joined_ref.at[:, :C]
    exp_w_ref = joined_ref.at[:, C : C + mlp]

    @pl.when(step_at == 0)
    def _():
        out_sum_ref[...] = jnp.zeros_like(out_sum_ref)
        exp_sum_ref[...] = jnp.zeros_like(exp_sum_ref)
        red_sum_ref[...] = jnp.zeros_like(red_sum_ref)
        sums_ref[...] = jnp.zeros_like(sums_ref)
        wide_ref[...] = jnp.zeros_like(wide_ref)
        for at in range(0, C, 16):
            for b in range(blocks):
                cols = C + mlp + b * C
                red_w_ref[blocks * at + 16 * b : blocks * at + 16 * (b + 1), :] = joined_ref[
                    at : at + 16, cols : cols + C
                ]

    row = lax.broadcasted_iota(jnp.int32, (images * ROWS, 1), 0)
    live = (row < (count_ref[0] - images * step_at) * ROWS).astype(F32)
    grad = load_grid(grid_ref, rows_ref, order_ref[...]) * live
    grad_low = grad.astype(BF16)
    grad_turned = turned(grad_low)
    residual = win_ref[...].astype(F32) + dot(merged_ref[...], out_w_ref[...]) + out_b
    unit, inverse = row_stats(residual)
    expand_in = (unit * gain + shift).astype(BF16)
    in_turned = turned(expand_in)
    step = 512
    out = residual + red_b
    d_in = jnp.zeros((images * ROWS, C), F32)
    for m in range(0, mlp, step):
        cols = slice(m, m + step)
        pre = dot(expand_in, exp_w_ref[:, cols]) + exp_b_ref[:, cols]
        bell = jnp.exp(pre * pre * -0.5)
        t = 1.0 / (1.0 + jnp.abs(pre) * (0.3275911 * 0.7071067811865476))
        tail = (
            t
            * bell
            * (
                0.127414796
                + t * (-0.142248368 + t * (0.7107068705 + t * (-0.7265760135 + t * 0.5307027145)))
            )
        )
        cdf = jnp.where(pre >= 0, 1.0 - tail, tail)
        hidden = (pre * cdf).astype(BF16)
        red_sum_ref[:, cols] += dot(grad_turned, hidden)
        d_hidden = dot_nt(grad_low, red_w_ref[cols, :])
        d_pre = (d_hidden * (cdf + pre * bell * 0.3989422804014327)).astype(BF16)
        exp_sum_ref[:, cols] += dot(in_turned, d_pre)
        wide_ref[:, cols] += column_sum(d_pre.astype(F32))
        out = out + dot(hidden, red_w_ref[cols, :])
        d_in = d_in + dot_nt(d_pre, exp_w_ref[:, cols])
    block = (out * live).astype(BF16)
    for i in range(images):
        block_rows = dot(back_ref[...], block[ROWS * i : ROWS * (i + 1)]).astype(BF16)
        for r in range(IMG):
            block_ref[i, r] = block_rows[16 * r : 16 * r + IMG]
    d_res = grad + norm_pull(d_in, gain, unit, inverse)
    d_res_ref[...] = d_res
    d_branch = d_res.astype(BF16)
    d_att_ref[...] = dot_nt(d_branch, out_w_ref[...]).astype(BF16)
    out_sum_ref[...] += dot(turned(merged_ref[...]), d_branch)
    sums_ref[0:1, :] += column_sum(d_in * unit)
    sums_ref[1:2, :] += column_sum(d_in)
    sums_ref[2:3, :] += column_sum(d_branch.astype(F32))
    sums_ref[3:4, :] += column_sum(grad)

    @pl.when(step_at == pl.num_programs(0) - 1)
    def _():
        core = count_ref[1]
        outs = (kept_ref, away_ref)
        write_chunks(outs, core, out_sum_ref, 0)
        write_chunks(outs, core, exp_sum_ref, C)
        for m in range(0, mlp, C):
            red_w_ref[m : m + C, :] = red_sum_ref[:, m : m + C].T.astype(BF16)
        for j in range(C // 32):
            for out, bit in zip(outs, (core, 1 - core)):
                for b in range(blocks):
                    start = pl.multiple_of(16 * (blocks * (2 * j + bit) + b), 16)
                    at = C + mlp + b * C
                    out[chunk_place(j), :, at : at + C] = red_w_ref[pl.ds(start, 16), :]


def attend_back_kernel(
    core_ref, packed_ref, soft_ref, d_att_ref, in_ref,
    d_packed_ref, pairs_ref, kept_ref, away_ref, sum_ref,
):
    @pl.when(pl.program_id(0) == 0)
    def _():
        pairs_ref[...] = jnp.zeros_like(pairs_ref)
        sum_ref[...] = jnp.zeros_like(sum_ref)

    for g in range(HEADS // GROUP):
        at = LANES * g
        q = packed_ref[:, at : at + LANES]
        k_turned = turned(packed_ref[:, C + at : C + at + LANES])
        v = packed_ref[:, 2 * C + at : 2 * C + at + LANES]
        d_att = d_att_ref[:, at : at + LANES]
        d_soft = dot_nt(head_stack(v), d_att)
        d_raw, d_q, soft = [], [], []
        for h in range(GROUP):
            head = g * GROUP + h
            low = soft_ref[0, head]
            soft.append(low)
            p = low.astype(F32)
            dp = d_soft[h * ROWS : (h + 1) * ROWS]
            ds = (p * (dp - column_sum(p * dp))).astype(BF16)
            pairs_ref[head] += ds.astype(F32)
            d_raw.append(ds)
            d_q.append(dot(k_turned[h * HEAD_DIM : (h + 1) * HEAD_DIM], ds))
        d_k = head_pick(dot(jnp.concatenate(d_raw, axis=0), q))
        d_v = head_pick(dot(jnp.concatenate(soft, axis=0), d_att))
        d_packed_ref[:, at : at + LANES] = (jnp.concatenate(d_q, axis=0) * scale).T.astype(BF16)
        d_packed_ref[:, C + at : C + at + LANES] = (d_k * scale).astype(BF16)
        d_packed_ref[:, 2 * C + at : 2 * C + at + LANES] = d_v.astype(BF16)
    in_turned = turned(in_ref[...])
    for m in range(0, 3 * C, C):
        sum_ref[:, m : m + C] += dot(in_turned, d_packed_ref[:, m : m + C])

    @pl.when(pl.program_id(0) == pl.num_programs(0) - 1)
    def _():
        write_chunks((kept_ref, away_ref), core_ref[0], sum_ref, 0)


def input_kernel(
    d_packed_ref, win_ref, d_res_ref, six_ref, weight_ref, back_ref,
    grad_ref, sums_ref, wide_ref, turned_ref,
):
    @pl.when(pl.program_id(0) == 0)
    def _():
        for m in range(0, 3 * C, C):
            turned_ref[m : m + C, :] = turned(weight_ref[:, m : m + C])
        sums_ref[...] = jnp.zeros_like(sums_ref)
        wide_ref[...] = jnp.zeros_like(wide_ref)

    d_packed = d_packed_ref[...]
    d_in = dot(d_packed, turned_ref[...])
    unit, inverse = row_stats(win_ref[...].astype(F32))
    total = d_res_ref[...] + norm_pull(d_in, six_ref[0:1, :], unit, inverse)
    sums_ref[0:1, :] += column_sum(d_in * unit)
    sums_ref[1:2, :] += column_sum(d_in)
    wide_ref[...] += column_sum(d_packed.astype(F32))
    high = total.astype(BF16)
    low = (total - high.astype(F32)).astype(BF16)
    rows = dot(back_ref[...], high) + dot(back_ref[...], low)
    for r in range(IMG):
        grad_ref[0, r] = rows[16 * r : 16 * r + IMG]


def whole(shape):
    return pl.BlockSpec(shape, lambda *_: (0,) * len(shape))


def per_image(width):
    return pl.BlockSpec((ROWS, width), lambda i: (i, 0))


GRID_SPEC = pl.BlockSpec((1, IMG, IMG, C), lambda i: (i, 0, 0, 0))
SMEM_SPEC = pl.BlockSpec(memory_space=pltpu.SMEM)


def params():
    return pltpu.CompilerParams(vmem_limit_bytes=VMEM_BYTES)


def cost(flops, moved, special=0):
    return pl.CostEstimate(flops=int(flops), bytes_accessed=int(moved), transcendentals=int(special))


def struct(shape, dtype):
    return jax.ShapeDtypeStruct(shape, dtype)


def run_bias(codes, index_rows, table):
    return pl.pallas_call(
        bias_kernel,
        out_shape=struct((HEADS, ROWS, ROWS), F32),
        in_specs=[SMEM_SPEC] + [pl.BlockSpec(memory_space=pltpu.VMEM)] * 3,
        out_specs=pl.BlockSpec(memory_space=pltpu.VMEM),
        compiler_params=params(),
        cost_estimate=cost(2e9, 4e6),
    )(codes, codes[None, :], index_rows, table)


def run_table(pairs, index_rows):
    return pl.pallas_call(
        table_kernel,
        out_shape=struct((HEADS, TABLE_PAD), F32),
        in_specs=[pl.BlockSpec(memory_space=pltpu.VMEM)] * 2,
        out_specs=pl.BlockSpec(memory_space=pltpu.VMEM),
        scratch_shapes=[pltpu.VMEM((HEADS, 56, ROWS), F32)],
        compiler_params=params(),
        cost_estimate=cost(2e9, 4e6),
    )(pairs, index_rows)


def run_attend(inputs, order, six, starts, pieces, bias, pair):
    images = inputs.shape[0]
    rows = images * ROWS
    return pl.pallas_call(
        attend_kernel,
        grid=(images,),
        out_shape=(
            struct((rows, C), BF16),
            struct((rows, C), BF16),
            struct((rows, 3 * C), BF16),
            struct((images, HEADS, ROWS, ROWS), BF16),
            struct((rows, C), BF16),
            struct((C, 3 * C), BF16),
        ),
        in_specs=[
            SMEM_SPEC,
            GRID_SPEC,
            whole((ROWS, RAW)),
            whole((6, C)),
            whole((1, 3 * C)),
            whole((HEADS, ROWS, ROWS)),
        ]
        + [whole(piece.shape) for piece in pieces],
        out_specs=(
            per_image(C),
            per_image(C),
            per_image(3 * C),
            pl.BlockSpec((1, HEADS, ROWS, ROWS), lambda i: (i, 0, 0, 0)),
            per_image(C),
            whole((C, 3 * C)),
        ),
        scratch_shapes=[pltpu.VMEM((RAW, C), BF16)],
        compiler_params=params(),
        cost_estimate=cost(images * 5e9, images * 6e6),
    )(starts, inputs, order, six, bias, pair, *pieces)


def run_mlp(count, win, merged, cotangent, order, back, weights):
    images = cotangent.shape[0]
    rows = images * ROWS
    mlp = weights[1].shape[1]
    per = 2 if images % 2 == 0 else 1
    some = pl.BlockSpec((per * ROWS, C), lambda i: (i, 0))
    grids = pl.BlockSpec((per, IMG, IMG, C), lambda i: (i, 0, 0, 0))
    half = (C // 32, 16, C + 2 * mlp)
    return pl.pallas_call(
        mlp_kernel,
        grid=(images // per,),
        out_shape=(
            struct(cotangent.shape, BF16),
            struct((rows, C), F32),
            struct((rows, C), BF16),
            struct(half, BF16),
            struct(half, BF16),
            struct((8, C), F32),
            struct((1, mlp), F32),
        ),
        in_specs=[
            SMEM_SPEC,
            some,
            some,
            grids,
            whole((ROWS, RAW)),
            whole((RAW, ROWS)),
            whole((6, C)),
            whole((1, mlp)),
            whole((C, C + 2 * mlp)),
        ],
        out_specs=(grids, some, some, whole(half), whole(half), whole((8, C)), whole((1, mlp))),
        scratch_shapes=[
            pltpu.VMEM((per * RAW, C), BF16),
            pltpu.VMEM((mlp, C), BF16),
            pltpu.VMEM((C, C), F32),
            pltpu.VMEM((C, mlp), F32),
            pltpu.VMEM((C, mlp), F32),
        ],
        compiler_params=params(),
        cost_estimate=cost(images * 6e9, images * 4e6),
    )(count, win, merged, cotangent, order, back, *weights)


def run_attend_back(core, packed, soft, d_att, attend_in):
    images = soft.shape[0]
    half = (C // 32, 16, 3 * C)
    return pl.pallas_call(
        attend_back_kernel,
        grid=(images,),
        out_shape=(
            struct(packed.shape, BF16),
            struct((HEADS, ROWS, ROWS), F32),
            struct(half, BF16),
            struct(half, BF16),
        ),
        in_specs=[
            SMEM_SPEC,
            per_image(3 * C),
            pl.BlockSpec((1, HEADS, ROWS, ROWS), lambda i: (i, 0, 0, 0)),
            per_image(C),
            per_image(C),
        ],
        out_specs=(per_image(3 * C), whole((HEADS, ROWS, ROWS)), whole(half), whole(half)),
        scratch_shapes=[pltpu.VMEM((C, 3 * C), F32)],
        compiler_params=params(),
        cost_estimate=cost(images * 6e9, images * 6e6),
    )(core, packed, soft, d_att, attend_in)


def run_input(d_packed, win, d_res, six, weight, back, shape):
    return pl.pallas_call(
        input_kernel,
        grid=(shape[0],),
        out_shape=(struct(shape, F32), struct((8, C), F32), struct((1, 3 * C), F32)),
        in_specs=[
            per_image(3 * C),
            per_image(C),
            per_image(C),
            whole((6, C)),
            whole((C, 3 * C)),
            whole((RAW, ROWS)),
        ],
        out_specs=(GRID_SPEC, whole((8, C)), whole((1, 3 * C))),
        scratch_shapes=[pltpu.VMEM((3 * C, C), BF16)],
        compiler_params=params(),
        cost_estimate=cost(shape[0] * 1e9, shape[0] * 2e6),
    )(d_packed, win, d_res, six, weight, back)


def gather(shard):
    return lax.all_gather(shard, "fsdp", axis=0, tiled=True)


def swap(value, axis, bits):
    return lax.ppermute(value, axis, [(i, i ^ bits) for i in range(lax.axis_size(axis))])


def pick(value, index, axis):
    return lax.dynamic_index_in_dim(value, index, axis, keepdims=False)


def gather_line(shard):
    half = shard.shape[0] // 2
    own = lax.dynamic_slice_in_dim(shard, lax.axis_index("rep") % 2 * half, half, 0)
    return jnp.concatenate([own] + [swap(own, "fsdp", d) for d in (2, 4, 6)], axis=0)


def gather_pieces(line, rows, vector_line):
    mine, core = lax.axis_index("fsdp"), lax.axis_index("rep") % 2
    across = swap(line, "fsdp", 1)
    vector = jnp.concatenate([vector_line, swap(vector_line, "fsdp", 1)], axis=0)
    across, vector = lax.optimization_barrier((across, vector))
    pieces = [line, swap(line, "rep", 1), across, swap(across, "rep", 1)]
    starts = []
    for side in (0, 1):
        for other in (0, 1):
            for d in (0, 2, 4, 6):
                starts.append((mine ^ d ^ side) * rows + (core ^ other) * (rows // 2))
    return jnp.stack(starts).astype(jnp.int32), pieces, gather_vector(vector)


def gather_vector(held):
    mine, owners = lax.axis_index("fsdp"), lax.axis_size("fsdp")
    stacked = held.reshape(owners, -1).astype(F32)
    order = jnp.asarray((0, 4, 2, 6, 1, 5, 3, 7))
    chosen = (jnp.arange(owners)[:, None] ^ order[None, :]) == mine
    return jnp.sum(jnp.where(chosen[:, :, None], stacked[None], 0.0), axis=1)


def gather_joined(weight_out, weight_exp, weight_red):
    replica, replicas = lax.axis_index("rep"), lax.axis_size("rep")
    rows = weight_out.shape[0] // replicas
    blocks = weight_red.shape[0] // weight_out.shape[0]

    def quarter(shard):
        size = shard.shape[0] // replicas
        return lax.dynamic_slice_in_dim(shard, replica * size, size, 0)

    red = quarter(weight_red).reshape(blocks, rows, C).transpose(1, 0, 2).reshape(rows, blocks * C)
    joined = jnp.concatenate([quarter(weight_out), quarter(weight_exp), red], axis=1)
    return lax.all_gather(joined, ("fsdp", "rep"), axis=0, tiled=True)


def halves(block, bit, axis):
    return pick(block, bit, axis), pick(block, 1 - bit, axis)


def added(a, b):
    return (a.astype(F32) + b.astype(F32)).astype(BF16)


def chunk_rows(kept, away):
    chunks = jnp.stack([kept, away]).reshape(2, 2, 2, 2, 2, 16, -1)
    return chunks.transpose(3, 4, 2, 1, 0, 5, 6).reshape(C, -1)


def scatter_bits():
    mine, replica = lax.axis_index("fsdp"), lax.axis_index("rep")
    return mine // 4, mine // 2 % 2, mine % 2, replica // 2, replica % 2


def scatter_step(kept, got, bit):
    keep, away = halves(kept, bit, 0)
    got_keep, got_away = halves(got, bit, 0)
    return added(keep, got_keep), added(away, got_away)


def join_kernel(ids_ref, both_ref, rest_ref, *refs):
    parts, rows_ref = refs[:4], refs[4]
    outs, vectors = refs[5:9], refs[9:]
    at = 0
    for out in outs:
        rows, cols = out.shape
        rows = rows // 4
        for e in range(4):
            start = pl.multiple_of((ids_ref[0] ^ e) * rows, rows)
            for b in range(rows // 16):
                if out is outs[3]:
                    block = parts[e][...]
                else:
                    block = (both_ref, rest_ref)[e // 2][e % 2, :, at + b * cols : at + (b + 1) * cols]
                out[pl.ds(start + 16 * b, 16), :] = block.astype(F32)
        at += rows // 16 * cols
    mine = ids_ref[1]
    base = 0
    for vector in vectors:
        if vector.shape[1] < 128:
            row = rows_ref[pl.ds(base + mine // 2, 1), :]
            moved = jnp.concatenate([row[:, 64:], row[:, :64]], axis=1)
            vector[...] = jnp.where(mine % 2 == 1, moved, row)[:, :64]
            base += 4
        else:
            count = vector.shape[0]
            for r in range(count):
                vector[r : r + 1, :] = rows_ref[pl.ds(base + count * mine + r, 1), :]
            base += 8 * count


def run_join(mlp, parts, rows, shapes, sizes):
    ids = jnp.stack([lax.axis_index("rep"), lax.axis_index("fsdp")]).astype(jnp.int32)
    moved = sum(6 * a * b for a, b in shapes)
    flat = [(max(size // 128, 1), min(size, 128)) for size in sizes]
    count = len(shapes) + len(sizes)
    outs = pl.pallas_call(
        join_kernel,
        out_shape=[struct(shape, F32) for shape in list(shapes) + flat],
        in_specs=[SMEM_SPEC] + [pl.BlockSpec(memory_space=pltpu.VMEM)] * 7,
        out_specs=[pl.BlockSpec(memory_space=pltpu.VMEM)] * count,
        compiler_params=params(),
        cost_estimate=cost(moved, moved),
    )(ids, *mlp, *parts, rows)
    return outs[:4], [out.reshape(-1) for out in outs[4:]]


def finish(kept_mlp, got_mlp, kept, got, vector, results):
    far, near, side, _, _ = scatter_bits()
    line = lax.axis_index("fsdp") // 2
    tie = lax.optimization_barrier
    kept_mlp, got_mlp, kept, got, vector = tie((kept_mlp, got_mlp, kept, got, vector))
    kept_mlp, away_mlp = scatter_step(kept_mlp, got_mlp, far)
    kept, away = scatter_step(kept, got, side)
    rows = jnp.pad(jnp.concatenate(vector), (0, -sum(v.shape[0] for v in vector) % 1024))
    rows = rows.reshape(-1, 128)

    away_mlp, away, rows = tie((away_mlp, away, rows))
    got_mlp = swap(away_mlp, "fsdp", 4)
    total = added(kept, swap(away, "fsdp", 1)).reshape(4, kept.shape[-2], kept.shape[-1])
    own = pick(total, line, 0)
    pieces = [pick(total, line ^ d, 0) for d in (1, 2, 3)]
    rows = rows + swap(rows, "rep", 1)

    own, pieces, rows, results = tie((own, pieces, rows, results))
    results = tuple(result.transpose(1, 2, 0, 3) for result in results)
    got_pieces = [swap(pieces[d - 1], "fsdp", 2 * d) for d in (1, 2, 3)]
    rows = rows + swap(rows, "rep", 2)

    got_mlp, kept_mlp, rows, results = tie((got_mlp, kept_mlp, rows, results))
    kept_mlp, away_mlp = scatter_step(kept_mlp, got_mlp, near)
    total_mlp = added(kept_mlp, swap(away_mlp, "fsdp", 2))
    rows = rows + swap(rows, "fsdp", 1)
    total = own.astype(F32)
    for piece in got_pieces:
        total = total + piece.astype(F32)
    total = total.astype(BF16)

    total, total_mlp, rows = tie((total, total_mlp, rows))
    parts = [total] + [swap(total, "rep", e) for e in (1, 2, 3)]
    both_mlp = jnp.stack([total_mlp, swap(total_mlp, "rep", 1)])
    rows = rows + swap(rows, "fsdp", 4)

    both_mlp, parts, rows = tie((both_mlp, parts, rows))
    rest_mlp = swap(both_mlp, "rep", 2)
    rows = rows + swap(rows, "fsdp", 2)
    results = tuple(result.transpose(2, 0, 1, 3) for result in results)
    return [both_mlp, rest_mlp], parts, rows, results


def reduce_weight_grad(partial):
    share = lax.psum_scatter(partial, "fsdp", scatter_dimension=0, tiled=True)
    return lax.psum(share, "rep").astype(F32)


def per_device(
    inputs,
    cotangent,
    image_counts,
    region_labels,
    position_index,
    first_gain,
    first_shift,
    attend_weight,
    attend_bias,
    bias_table,
    output_weight,
    output_bias,
    second_gain,
    second_shift,
    expand_weight,
    expand_bias,
    reduce_weight,
    reduce_bias,
):
    order_host = window_order()
    order = jnp.asarray(order_host, BF16)
    back = jnp.asarray(order_host.T, BF16)
    shards = lax.axis_size("fsdp")
    mine = lax.axis_index("fsdp")
    paired = shards == 8 and lax.axis_size("rep") == 4

    window_of = jnp.arange(WINDOWS, dtype=jnp.int32)[:, None]
    codes = jnp.pad(
        (region_labels + 4 * window_of).reshape(-1), (0, ROWS - TOK), constant_values=-1
    )
    index_rows = jnp.pad(jnp.tile(position_index.T, (1, WINDOWS)), ((0, 0), (0, ROWS - TOK)))
    table = jnp.pad(bias_table.T, ((0, 0), (0, TABLE_PAD - TABLE)))
    vectors = (
        first_gain, first_shift, output_bias, second_gain, second_shift, reduce_bias,
        attend_bias, expand_bias,
    )
    sizes = [v.shape[0] for v in vectors]
    if paired:
        joined_weights = gather_joined(output_weight, expand_weight, reduce_weight)
        line = gather_line(attend_weight)
        own = jnp.concatenate(vectors).reshape(1, -1, 128)
        vector_line = jnp.concatenate([own, swap(own, "fsdp", 4)], axis=0)
        line, vector_line, codes = lax.optimization_barrier((line, vector_line, codes))
        vector_line = jnp.concatenate([vector_line, swap(vector_line, "fsdp", 2)], axis=0)
        starts, pieces, joined = gather_pieces(line, attend_weight.shape[0], vector_line)
        inputs, cotangent, _ = lax.optimization_barrier((inputs, cotangent, line))
    else:
        joined = gather(jnp.concatenate(vectors)).reshape(shards, sum(sizes)).astype(F32)
    pair = run_bias(codes, index_rows, table)
    pair = run_bias(codes, index_rows, table)
    six = joined[:, : 6 * sizes[0]].reshape(shards, 6, sizes[0]).transpose(1, 0, 2).reshape(6, C)
    bias_one = joined[:, 6 * sizes[0] : 6 * sizes[0] + sizes[6]].reshape(1, 2 * C)
    bias_exp = joined[:, 6 * sizes[0] + sizes[6] :].reshape(1, shards * sizes[7])
    bias_packed = jnp.concatenate(
        [bias_one[:, :C], jnp.zeros((1, C), F32), bias_one[:, C:]], axis=1
    )
    if not paired:
        starts, pieces = jnp.zeros((1,), jnp.int32), [gather(attend_weight)]
        red = gather(reduce_weight).reshape(C // 16, -1, 16, C).transpose(0, 2, 1, 3).reshape(C, -1)
        joined_weights = jnp.concatenate([gather(output_weight), gather(expand_weight), red], axis=1)

    win, attend_in, packed, soft, merged, weight_one = run_attend(
        inputs, order, six, starts, pieces, bias_packed, pair
    )
    far, _, side, row, core = scatter_bits()
    core = core if paired else jnp.zeros((), jnp.int32)
    block_output, d_res, d_att, kept_mlp, away_mlp, sums_two, d_exp_bias = run_mlp(
        jnp.stack([image_counts[0, 0], core]), win, merged, cotangent, order, back,
        (six, bias_exp, joined_weights),
    )
    if paired:
        split = (2, 2, 2, 2, 16, -1)
        kept_mlp, away = kept_mlp.reshape(split), away_mlp.reshape(split)
        kept_mlp, away = scatter_step(kept_mlp, swap(away, "rep", 1), row)
        d_att, away = lax.optimization_barrier((d_att, away))
        got = swap(away, "rep", 2)
    d_packed, pairs, kept, away = run_attend_back(core[None], packed, soft, d_att, attend_in)
    if paired:
        kept_mlp, away_mlp = scatter_step(kept_mlp, got, side)
        pairs, away, away_mlp = lax.optimization_barrier((pairs, away, away_mlp))
        kept, away = kept.reshape(split), away.reshape(split)
        got, got_mlp = swap(away, "rep", 1), swap(away_mlp, "fsdp", 1)
    table_part = run_table(pairs, index_rows)
    if paired:
        kept, away = scatter_step(kept, got, row)
        d_packed, away, table_part = lax.optimization_barrier((d_packed, away, table_part))
        got = swap(away, "rep", 2)
    input_grad, sums_one, d_packed_bias = run_input(
        d_packed, win, d_res, six, weight_one, back, inputs.shape
    )
    small = (
        sums_one[0], sums_one[1], sums_two[2], sums_two[0], sums_two[1], sums_two[3],
        d_packed_bias[0, :C], d_packed_bias[0, 2 * C :], d_exp_bias[0], table_part.reshape(-1),
    )
    if paired:
        mlp_pieces, part_pieces, rows, (block_output, input_grad) = finish(
            kept_mlp, got_mlp, kept, got, small, (block_output, input_grad)
        )
        (output_grad, expand_grad, reduce_grad, attend_grad), owned = run_join(
            mlp_pieces, part_pieces, rows,
            [w.shape for w in (output_weight, expand_weight, reduce_weight, attend_weight)],
            sizes,
        )
        table_sum = rows.reshape(-1)[sum(sizes) * shards :][: HEADS * TABLE_PAD]
    else:
        parts = chunk_rows(kept_mlp, away_mlp)
        mlp = bias_exp.shape[1]
        reduce_part = parts[:, C + mlp :].reshape(C // 16, 16, -1, C).transpose(0, 2, 1, 3)
        output_grad, expand_grad, attend_grad, reduce_grad = (
            reduce_weight_grad(part)
            for part in (
                parts[:, :C], parts[:, C : C + mlp], chunk_rows(kept, away), reduce_part.reshape(mlp, C),
            )
        )
        summed = lax.psum(jnp.concatenate(small), ("fsdp", "rep"))
        ends = np.cumsum([0] + [size * shards for size in sizes])
        owned = [
            lax.dynamic_slice(summed[ends[i] : ends[i + 1]], (mine * sizes[i],), (sizes[i],))
            for i in range(len(sizes))
        ]
        table_sum = summed[ends[-1] :]
    table_grad = table_sum.reshape(HEADS, TABLE_PAD)[:, :TABLE].T
    return (
        block_output,
        input_grad,
        owned[0],
        owned[1],
        attend_grad,
        owned[6],
        table_grad,
        output_grad,
        owned[2],
        owned[3],
        owned[4],
        expand_grad,
        owned[7],
        reduce_grad,
        owned[5],
    )


def solution(mesh):
    images = P(("fsdp", "rep"), None, None, None)
    rows, vector = P("fsdp", None), P("fsdp")
    return jax.shard_map(
        per_device,
        mesh=mesh,
        in_specs=(
            images, images, P("fsdp", "rep"), P(), P(), vector, vector, rows, vector, P(),
            rows, vector, vector, vector, rows, vector, rows, vector,
        ),
        out_specs=(
            images, images, vector, vector, rows, vector, P(), rows, vector, vector, vector,
            rows, vector, rows, vector,
        ),
        check_vma=False,
    )
```

time: 277 us -> 246 us (0.89); the launches traced: 272 us -> 245 us
  matrix products: 23.3 us -> 0 us
  local copies, waits for them, and re-layouts: 46.6 us -> 29.3 us
  Pallas kernels: 120 us -> 136 us
  waiting for transfers between devices: 32.6 us -> 27 us
    dot_general x4 -> x0, matrix products: 23.3 us -> none  [weight_grad(): lax.dot_general(rows_in, rows_out, (((0,), (0,)), ((), ())), preferred_el...]
    pallas_call x2, Pallas kernels: 40 us -> 51.8 us  [the longest x1 49.5 us: run_mlp(): pl.pallas_call(mlp_kernel, grid=(images // per,), out_shape=(struct(cotan...]
    reshape x10 -> x4, local copies, waits for them, and re-layouts: 8.76 us -> 0.84 us  [the longest x2 0.76 us: per_device(): joined[:, :6 * sizes[0]].reshape(shards, 6, sizes[0]).transpose(1, 0, 2)]
    dynamic_slice x10 -> x0, local copies, waits for them, and re-layouts: 6.57 us -> none  [the longest x8 4.71 us: own(): return lax.dynamic_slice(vector, (mine * size,), (size,))]
    ppermute x28 -> x30, waiting for transfers between devices: 32.6 us -> 27 us  [swap(): lax.ppermute(value, axis, [(i, i ^ bits) for i in range(lax.axis_size(axi...]
    pallas_call x1, Pallas kernels: 25.6 us -> 30.9 us  [run_attend_back(): pl.pallas_call(attend_back_kernel, grid=(images,), out_shape=(struct(pack...]
    ppermute x28 -> x30, starting transfers between devices: 26.9 us -> 29.6 us  [swap(): lax.ppermute(value, axis, [(i, i ^ bits) for i in range(lax.axis_size(axi...]
    unnamed x52 -> x58, local copies, waits for them, and re-layouts: 13.8 us -> 12.7 us
  transfers between devices with their start and end apart: 29 -> 31, of which waited for: 13 -> 8; matrix products, arithmetic and copies ran while one was open for 16% -> 11% of each run, Pallas kernels for 30% -> 34%
where the time goes in v3:
time: 246 us; the launch traced here: 245 us
  Pallas kernels  136 us (55%)
  starting transfers between devices  29.6 us (12%)
  local copies, waits for them, and re-layouts  29.3 us (12%)
  waiting for transfers between devices  27 us (11%)
  between operations  15.4 us (6%)
  other arithmetic  7.43 us (3%)
    pallas_call x1, Pallas kernels, run_mlp(): pl.pallas_call(mlp_kernel, grid=(images // per,), out_shape=(struct(cotan...  49.5 us
    pallas_call x1, Pallas kernels, run_attend_back(): pl.pallas_call(attend_back_kernel, grid=(images,), out_shape=(struct(pack...  30.9 us
    ppermute x30, starting transfers between devices, swap(): lax.ppermute(value, axis, [(i, i ^ bits) for i in range(lax.axis_size(axi...  29.6 us
    pallas_call x1, Pallas kernels, run_attend(): pl.pallas_call(attend_kernel, grid=(images,), out_shape=(struct((rows, C)...  29.3 us
    ppermute x30, waiting for transfers between devices, swap(): lax.ppermute(value, axis, [(i, i ^ bits) for i in range(lax.axis_size(axi...  27 us
    unnamed x58, local copies, waits for them, and re-layouts  12.7 us
    pallas_call x1, Pallas kernels, run_input(): pl.pallas_call(input_kernel, grid=(shape[0],), out_shape=(struct(shape, F...  12.5 us
    pallas_call x1, Pallas kernels, run_table(): pl.pallas_call(table_kernel, out_shape=struct((HEADS, TABLE_PAD), F32), i...  6.38 us
  transfers between devices with their start and end apart: 31, of which 8 were waited for; matrix products, arithmetic and copies ran while one was open for 11% of the time, Pallas kernels for 34%

profile of v3, /device:TPU:0, one launch (start us, length us, event | category | flops | bytes accessed | tf_op | source)
XLA Modules:
  0.0 244.8 jit_solution(5490639012328251726)
XLA Ops:
  7.3 0.9 copy-done
  8.1 0.7 constant_dynamic-slice_fusion.2
  8.9 0.8 constant_dynamic-slice_fusion
  9.7 0.7 pad_maximum_fusion.2
  10.4 0.9 constant_dynamic-slice_fusion.3
  11.3 3.0 %collective-permute-start = (bf16[32,1536]{1,0:T(8,128)(2,1)S(1)}, bf16[32,1536]{1,0:T(8,128)(2,1)S(1)}, u32[]{:S(2)}, u32[]{:S(2)}) collective-permute-start(bf16[32,1536]{1,0:T(8,128)(2,1)S(1)} %constant_dynamic-slice_fusion.3), channel_id=1, source_target_pairs={{0,8},{4,12},{8,0},{12,4},{16,24},{20,28},{24,16},{28,20},{1,9},{5... | collective-permute-start | bytes 294920 | tf_op jit(solution)/shard_map/ppermute | solution.py:527
  14.3 2.6 %collective-permute-start.1 = (bf16[32,1536]{1,0:T(8,128)(2,1)S(1)}, bf16[32,1536]{1,0:T(8,128)(2,1)S(1)}, u32[]{:S(2)}, u32[]{:S(2)}) collective-permute-start(bf16[32,1536]{1,0:T(8,128)(2,1)S(1)} %constant_dynamic-slice_fusion.3), channel_id=1, source_target_pairs={{0,16},{4,20},{8,24},{12,28},{16,0},{20,4},{24,8},{28,12},{1,17},{... | collective-permute-start | bytes 294920 | tf_op jit(solution)/shard_map/ppermute | solution.py:527
  16.9 5.4 %concatenate.26 = bf16[768]{0:T(1024)(128)(2,1)S(1)} concatenate(bf16[64]{0:T(256)(128)(2,1)} %param.26, bf16[64]{0:T(256)(128)(2,1)} %param.27, bf16[64]{0:T(256)(128)(2,1)} %param.32, bf16[64]{0:T(256)(128)(2,1)} %param.33, bf16[64]{0:T(256)(128)(2,1)} %param.34, bf16[64]{0:T(256)(128)(2,1)} %param.38, bf16[128]{0:T(256)(128)(2,1)} %param.29, bf16[256]{0:T(256)(128)(2,1)} %param.36), dimensions={0} | concatenate | bytes 3072 | tf_op jit(solution)/shard_map/concatenate | solution.py:736
  22.4 1.9 collective-permute-start.3
  24.9 0.7 xor_compare_fusion
  25.6 0.8 broadcast_add_fusion
  27.7 2.5 %collective-permute-start.5 = (bf16[2,6,128]{2,1,0:T(8,128)(2,1)S(1)}, bf16[2,6,128]{2,1,0:T(8,128)(2,1)S(1)}, u32[]{:S(2)}, u32[]{:S(2)}) collective-permute-start(bf16[2,6,128]{2,1,0:T(8,128)(2,1)S(1)} %pad_maximum_fusion.5), channel_id=1, source_target_pairs={{0,8},{4,12},{8,0},{12,4},{16,24},{20,28},{24,16},{28,20},{1,9},{5... | collective-permute-start | bytes 9224 | tf_op jit(solution)/shard_map/ppermute | solution.py:527
  31.7 0.7 stack.93.starts_ref
  32.4 1.5 collective-permute-start.4
  34.5 5.1 %shard_map.316.pair_ref = f32[16,208,208]{2,1,0:T(8,128)} custom-call(s32[208]{0:T(256)} %pad.16.code_ref, s32[1,208]{1,0:T(1,128)} %bitcast.139, s32[49,208]{1,0:T(8,128)} %pad.17.index_ref, bf16[16,176]{1,0:T(8,128)(2,1)} %pad.18.table_ref), custom_call_target="tpu_custom_call" | custom-call | flops 2000000000 | bytes 4000000 | tf_op jit(solution)/shard_map/pallas_call | solution.py:373
  39.6 1.8 copy.57.grid_ref
  41.4 1.8 copy.59.grid_ref
  43.2 1.5 collective-permute-done.6
  45.1 0.7 reshape.203.rows_in_ref.six_ref
  47.0 0.7 copy-done.20
  47.8 0.7 copy-done.21
  48.5 29.3 %shard_map.317 = (bf16[1664,512]{1,0:T(8,128)(2,1)}, bf16[1664,512]{1,0:T(8,128)(2,1)}, bf16[1664,1536]{1,0:T(8,128)(2,1)}, bf16[8,16,208,208]{3,2,1,0:T(8,128)(...) custom-call(s32[16]{0:T(128)} %stack.93.starts_ref, bf16[8,14,14,512]{3,2,1,0:T(8,128)(2,1)} %copy.57.grid_ref, ...), custom_call_target="tpu_custom_call" | custom-call | flops 40000000000 | bytes 48000000 | tf_op jit(solution)/shard_map/pallas_call | solution.py:398
  77.8 49.5 %shard_map.318 = (bf16[8,14,14,512]{3,2,1,0:T(8,128)(2,1)}, f32[1664,512]{1,0:T(8,128)}, bf16[1664,512]{1,0:T(8,128)(2,1)}, bf16[16,16,4608]{2,1,0:T(8,128)(2,1)...) custom-call(s32[2]{0:T(128)} %pad_add_fusion.count_ref, ...), custom_call_target="tpu_custom_call" | custom-call | flops 48000000000 | bytes 32000000 | tf_op jit(solution)/shard_map/pallas_call | solution.py:440
  127.8 4.4 %collective-permute-done.9 = bf16[2,2,2,2,16,4608]{5,4,3,2,1,0:T(8,128)(2,1)S(1)} collective-permute-done((bf16[2,2,2,2,16,4608]{5,4,3,2,1,0:T(8,128)(2,1)}, bf16[2,2,2,2,16,4608]{5,4,3,2,1,0:T(8,128)(2,1)S(1)}, u32[]{:S(2)}, u32[]{:S(2)}) %collective-permute-start.9) | collective-permute-done | bytes 2359328 | tf_op jit(solution)/shard_map/ppermute | solution.py:527
  132.2 2.4 add_convert_fusion.1
  134.6 1.2 collective-permute-start.10
  135.8 30.9 %shard_map.319 = (bf16[1664,1536]{1,0:T(8,128)(2,1)}, f32[16,208,208]{2,1,0:T(8,128)}, bf16[16,16,1536]{2,1,0:T(8,128)(2,1)}, bf16[16,16,1536]{2,1,0:T(8,128)(2,1)}) custom-call(s32[1]{0:T(128)} %bitcast.1.core_ref, bf16[1664,1536]{1,0:T(8,128)(2,1)} %get-tuple-element.113.packed_ref, bf16[8,16,208,208]{3,2,1,0:T(8,128)(2,1)} %get-tuple-element.114.soft_ref, ...), custom_call_target="tpu_custom_call" | custom-call | flops 48000000000 | bytes 48000000 | tf_op jit(solution)/shard_map/pallas_call | solution.py:479
  167.5 2.5 %collective-permute-start.11 = (bf16[2,2,16,4608]{3,2,1,0:T(8,128)(2,1)S(1)}, bf16[2,2,16,4608]{3,2,1,0:T(8,128)(2,1)S(1)}, u32[]{:S(2)}, u32[]{:S(2)}) collective-permute-start(bf16[2,2,16,4608]{3,2,1,0:T(8,128)(2,1)S(1)} %get-tuple-element.119), channel_id=1, source_target_pairs={{0,4},{4,0},{8,12},{12,8},{16,20},{20,16},{24,28},{28,24},{1,5},{5... | collective-permute-start | bytes 1769480 | tf_op jit(solution)/shard_map/ppermute | solution.py:527
  170.0 6.4 %shard_map.320 = f32[16,176]{1,0:T(8,128)} custom-call(f32[16,208,208]{2,1,0:T(8,128)} %get-tuple-element.123.sums_ref, s32[49,208]{1,0:T(8,128)} %pad.17.index_ref), custom_call_target="tpu_custom_call" | custom-call | flops 2000000000 | bytes 4000000 | tf_op jit(solution)/shard_map/pallas_call | solution.py:384
  176.7 0.9 collective-permute-start.13
  177.6 12.5 %shard_map.321 = (f32[8,14,14,512]{3,2,1,0:T(8,128)}, f32[8,512]{1,0:T(8,128)}, f32[1,1536]{1,0:T(1,128)}) custom-call(bf16[1664,1536]{1,0:T(8,128)(2,1)} %get-tuple-element.125.d_packed_ref, bf16[1664,512]{1,0:T(8,128)(2,1)} %get-tuple-element.106.win_ref, f32[1664,512]{1,0:T(8,128)} %get-tuple-element.126.d_res_ref, ...), custom_call_target="tpu_custom_call" | custom-call | flops 8000000000 | bytes 16000000 | tf_op jit(solution)/shard_map/pallas_call | solution.py:503
  190.3 0.8 fusion.17
  191.6 0.7 collective-permute-start.14
  192.8 5.1 %collective-permute-done.15 = bf16[2,2,16,1536]{3,2,1,0:T(8,128)(2,1)S(1)} collective-permute-done((bf16[2,2,16,1536]{3,2,1,0:T(8,128)(2,1)S(1)}, bf16[2,2,16,1536]{3,2,1,0:T(8,128)(2,1)S(1)}, u32[]{:S(2)}, u32[]{:S(2)}) %collective-permute-start.15) | collective-permute-done | bytes 196640 | tf_op jit(solution)/shard_map/ppermute | solution.py:527
  198.1 1.2 collective-permute-start.17
  199.5 4.1 %collective-permute-start.20 = (bf16[16,1536]{1,0:T(8,128)(2,1)S(1)}, bf16[16,1536]{1,0:T(8,128)(2,1)S(1)}, u32[]{:S(2)}, u32[]{:S(2)}) collective-permute-start(bf16[16,1536]{1,0:T(8,128)(2,1)S(1)} %get-tuple-element.160), channel_id=1, source_target_pairs={{0,24},{4,28},{8,16},{12,20},{16,8},{20,12},{24,0},{28,4},{1,25},{... | collective-permute-start | bytes 147464 | tf_op jit(solution)/shard_map/ppermute | solution.py:527
  203.7 6.7 %collective-permute-done.14 = bf16[2,16,4608]{2,1,0:T(8,128)(2,1)S(1)} collective-permute-done((bf16[2,16,4608]{2,1,0:T(8,128)(2,1)S(1)}, bf16[2,16,4608]{2,1,0:T(8,128)(2,1)S(1)}, u32[]{:S(2)}, u32[]{:S(2)}) %collective-permute-start.14) | collective-permute-done | bytes 294944 | tf_op jit(solution)/shard_map/ppermute | solution.py:527
  210.4 1.4 collective-permute-start.22
  212.0 2.4 collective-permute-done.22
  214.3 3.0 %collective-permute-done.21 = bf16[16,4608]{1,0:T(8,128)(2,1)S(1)} collective-permute-done((bf16[16,4608]{1,0:T(8,128)(2,1)S(1)}, bf16[16,4608]{1,0:T(8,128)(2,1)S(1)}, u32[]{:S(2)}, u32[]{:S(2)}) %collective-permute-start.21) | collective-permute-done | bytes 147488 | tf_op jit(solution)/shard_map/ppermute | solution.py:527
  218.6 0.9 collective-permute-start.26
  219.5 3.3 %collective-permute-done.27 = f32[72,128]{1,0:T(8,128)S(1)} collective-permute-done((f32[72,128]{1,0:T(8,128)S(1)}, f32[72,128]{1,0:T(8,128)S(1)}, u32[]{:S(2)}, u32[]{:S(2)}) %collective-permute-start.27) | collective-permute-done | bytes 36896 | tf_op jit(solution)/shard_map/ppermute | solution.py:527
  222.9 0.8 collective-permute-start.29
  223.7 1.2 collective-permute-start.28
  225.5 6.4 %copy.61 = f32[8,14,14,512]{3,0,2,1:T(8,128)} copy(f32[8,14,14,512]{3,2,1,0:T(8,128)} %get-tuple-element.154) | data formatting | bytes 6422528
  231.9 2.2 copy.60
  234.9 0.7 copy-done.8
  235.6 2.3 shard_map.322
  (142 shorter events, 10.6 us)
Async XLA Ops:
  7.2 1.0 copy-start
  7.2 23.0 %copy-start.14 = (s32[49,49]{1,0:T(8,128)S(1)}, s32[49,49]{1,0:T(8,128)}, u32[]{:S(2)}) copy-start(s32[49,49]{1,0:T(8,128)} %param.25) | copy-start | bytes 28816
  7.2 23.9 %copy-start.16 = (bf16[169,16]{0,1:T(8,128)(2,1)S(1)}, bf16[169,16]{0,1:T(8,128)(2,1)}, u32[]{:S(2)}) copy-start(bf16[169,16]{0,1:T(8,128)(2,1)} %param.30) | copy-start | bytes 16228
  7.2 70.6 %all-gather.2.cloned.1.call-start = ((), (), s32[]{:S(2)}) async-start(), calls=%async_computation | async-start | bytes 4866048 | tf_op jit(solution)/shard_map/all_gather | solution.py:573
  11.3 16.3 %collective-permute-start = (bf16[32,1536]{1,0:T(8,128)(2,1)S(1)}, bf16[32,1536]{1,0:T(8,128)(2,1)S(1)}, u32[]{:S(2)}, u32[]{:S(2)}) collective-permute-start(bf16[32,1536]{1,0:T(8,128)(2,1)S(1)} %constant_dynamic-slice_fusion.3), channel_id=1, source_target_pairs={{0,8},{4,12},{8,0},{12,4},{16,24},{20,28},{24,16},{28,20},{1,9},{5... | collective-permute-start | bytes 294920 | tf_op jit(solution)/shard_map/ppermute | solution.py:527
  14.3 13.3 %collective-permute-start.1 = (bf16[32,1536]{1,0:T(8,128)(2,1)S(1)}, bf16[32,1536]{1,0:T(8,128)(2,1)S(1)}, u32[]{:S(2)}, u32[]{:S(2)}) collective-permute-start(bf16[32,1536]{1,0:T(8,128)(2,1)S(1)} %constant_dynamic-slice_fusion.3), channel_id=1, source_target_pairs={{0,16},{4,20},{8,24},{12,28},{16,0},{20,4},{24,8},{28,12},{1,17},{... | collective-permute-start | bytes 294920 | tf_op jit(solution)/shard_map/ppermute | solution.py:527
  16.9 10.7 %collective-permute-start.2 = (bf16[32,1536]{1,0:T(8,128)(2,1)S(1)}, bf16[32,1536]{1,0:T(8,128)(2,1)S(1)}, u32[]{:S(2)}, u32[]{:S(2)}) collective-permute-start(bf16[32,1536]{1,0:T(8,128)(2,1)S(1)} %constant_dynamic-slice_fusion.3), channel_id=1, source_target_pairs={{0,24},{4,28},{8,16},{12,20},{16,8},{20,12},{24,0},{28,4},{1,25},{... | collective-permute-start | bytes 294920 | tf_op jit(solution)/shard_map/ppermute | solution.py:527
  22.4 5.2 %collective-permute-start.3 = (bf16[1,6,128]{2,1,0:T(8,128)(2,1)S(1)}, bf16[1,6,128]{2,1,0:T(8,128)(2,1)S(1)}, u32[]{:S(2)}, u32[]{:S(2)}) collective-permute-start(bf16[1,6,128]{2,1,0:T(8,128)(2,1)S(1)} %bitcast.129), channel_id=1, source_target_pairs={{0,16},{4,20},{8,24},{12,28},{16,0},{20,4},{24,8},{28,12},{1,17},{... | collective-permute-start | bytes 4616 | tf_op jit(solution)/shard_map/ppermute | solution.py:527
  27.7 12.0 %copy-start.7 = (bf16[128,1536]{1,0:T(8,128)(2,1)}, bf16[128,1536]{1,0:T(8,128)(2,1)S(1)}, u32[]{:S(2)}) copy-start(bf16[128,1536]{1,0:T(8,128)(2,1)S(1)} %pad_maximum_fusion.rest_0_) | copy-start | bytes 1179652
  27.7 6.2 %collective-permute-start.5 = (bf16[2,6,128]{2,1,0:T(8,128)(2,1)S(1)}, bf16[2,6,128]{2,1,0:T(8,128)(2,1)S(1)}, u32[]{:S(2)}, u32[]{:S(2)}) collective-permute-start(bf16[2,6,128]{2,1,0:T(8,128)(2,1)S(1)} %pad_maximum_fusion.5), channel_id=1, source_target_pairs={{0,8},{4,12},{8,0},{12,4},{16,24},{20,28},{24,16},{28,20},{1,9},{5... | collective-permute-start | bytes 9224 | tf_op jit(solution)/shard_map/ppermute | solution.py:527
  32.4 12.4 %collective-permute-start.4 = (bf16[128,1536]{1,0:T(8,128)(2,1)S(1)}, bf16[128,1536]{1,0:T(8,128)(2,1)S(1)}, u32[]{:S(2)}, u32[]{:S(2)}) collective-permute-start(bf16[128,1536]{1,0:T(8,128)(2,1)S(1)} %pad_maximum_fusion.rest_0_), channel_id=1, source_target_pairs={{0,4},{4,0},{8,12},{12,8},{16,20},{20,16},{24,28},{28,24},{1,5},{5... | collective-permute-start | bytes 1179656 | tf_op jit(solution)/shard_map/ppermute | solution.py:527
  33.9 13.1 %collective-permute-start.7 = (bf16[128,1536]{1,0:T(8,128)(2,1)S(1)}, bf16[128,1536]{1,0:T(8,128)(2,1)S(1)}, u32[]{:S(2)}, u32[]{:S(2)}) collective-permute-start(bf16[128,1536]{1,0:T(8,128)(2,1)S(1)} %pad_maximum_fusion.rest_0_), channel_id=1, source_target_pairs={{0,1},{1,0},{2,3},{3,2},{4,5},{5,4},{6,7},{7,6},{8,9},{9,8},{10,11... | collective-permute-start | bytes 1179656 | tf_op jit(solution)/shard_map/ppermute | solution.py:527
  33.9 10.8 %collective-permute-start.6 = (bf16[4,6,128]{2,1,0:T(8,128)(2,1)S(1)}, bf16[4,6,128]{2,1,0:T(8,128)(2,1)S(1)}, u32[]{:S(2)}, u32[]{:S(2)}) collective-permute-start(bf16[4,6,128]{2,1,0:T(8,128)(2,1)S(1)} %pad_maximum_fusion.4), channel_id=1, source_target_pairs={{0,4},{4,0},{8,12},{12,8},{16,20},{20,16},{24,28},{28,24},{1,5},{5... | collective-permute-start | bytes 18440 | tf_op jit(solution)/shard_map/ppermute | solution.py:527
  34.5 5.1 %copy-start.3 = (bf16[8,14,14,512]{3,0,2,1:T(8,128)(2,1)S(1)}, bf16[8,14,14,512]{3,0,2,1:T(8,128)(2,1)}, u32[]{:S(2)}) copy-start(bf16[8,14,14,512]{3,0,2,1:T(8,128)(2,1)} %param.21) | copy-start | bytes 4816900
  39.6 1.8 copy-start.4
  44.7 2.3 copy-start.19
  44.9 2.1 collective-permute-start.8
  127.3 4.9 %collective-permute-start.9 = (bf16[2,2,2,2,16,4608]{5,4,3,2,1,0:T(8,128)(2,1)}, bf16[2,2,2,2,16,4608]{5,4,3,2,1,0:T(8,128)(2,1)S(1)}, u32[]{:S(2)}, u32[]{:S(2)}) collective-permute-start(bf16[2,2,2,2,16,4608]{5,4,3,2,1,0:T(8,128)(2,1)} %bitcast.140), channel_id=1, source_target_pairs={{0,1},{1,0},{2,3},{3,2},{4,5},{5,4},{6,7},{7,6},{8,9},{9,8},{10,11... | collective-permute-start | bytes 7077896 | tf_op jit(solution)/shard_map/ppermute | solution.py:527
  134.6 32.2 %collective-permute-start.10 = (bf16[2,2,2,16,4608]{4,3,2,1,0:T(8,128)(2,1)S(1)}, bf16[2,2,2,16,4608]{4,3,2,1,0:T(8,128)(2,1)S(1)}, u32[]{:S(2)}, u32[]{:S(2)}) collective-permute-start(bf16[2,2,2,16,4608]{4,3,2,1,0:T(8,128)(2,1)S(1)} %get-tuple-element.112), channel_id=1, source_target_pairs={{0,2},{1,3},{2,0},{3,1},{4,6},{5,7},{6,4},{7,5},{8,10},{9,11},{10,... | collective-permute-start | bytes 3538952 | tf_op jit(solution)/shard_map/ppermute | solution.py:527
  167.1 9.4 %collective-permute-start.12 = (bf16[2,2,2,2,16,1536]{5,4,3,2,1,0:T(8,128)(2,1)}, bf16[2,2,2,2,16,1536]{5,4,3,2,1,0:T(8,128)(2,1)S(1)}, u32[]{:S(2)}, u32[]{:S(2)}) collective-permute-start(bf16[2,2,2,2,16,1536]{5,4,3,2,1,0:T(8,128)(2,1)} %bitcast.34), channel_id=1, source_target_pairs={{0,1},{1,0},{2,3},{3,2},{4,5},{5,4},{6,7},{7,6},{8,9},{9,8},{10,11... | collective-permute-start | bytes 2359304 | tf_op jit(solution)/shard_map/ppermute | solution.py:527
  167.5 8.9 %copy-start.6 = (bf16[16,16,1536]{2,1,0:T(8,128)(2,1)S(1)}, bf16[16,16,1536]{2,1,0:T(8,128)(2,1)}, u32[]{:S(2)}) copy-start(bf16[16,16,1536]{2,1,0:T(8,128)(2,1)} %get-tuple-element.120) | copy-start | bytes 2359300
  167.5 23.6 %collective-permute-start.11 = (bf16[2,2,16,4608]{3,2,1,0:T(8,128)(2,1)S(1)}, bf16[2,2,16,4608]{3,2,1,0:T(8,128)(2,1)S(1)}, u32[]{:S(2)}, u32[]{:S(2)}) collective-permute-start(bf16[2,2,16,4608]{3,2,1,0:T(8,128)(2,1)S(1)} %get-tuple-element.119), channel_id=1, source_target_pairs={{0,4},{4,0},{8,12},{12,8},{16,20},{20,16},{24,28},{28,24},{1,5},{5... | collective-permute-start | bytes 1769480 | tf_op jit(solution)/shard_map/ppermute | solution.py:527
  176.7 14.4 %collective-permute-start.13 = (bf16[2,2,2,16,1536]{4,3,2,1,0:T(8,128)(2,1)S(1)}, bf16[2,2,2,16,1536]{4,3,2,1,0:T(8,128)(2,1)S(1)}, u32[]{:S(2)}, u32[]{:S(2)}) collective-permute-start(bf16[2,2,2,16,1536]{4,3,2,1,0:T(8,128)(2,1)S(1)} %get-tuple-element.124), channel_id=1, source_target_pairs={{0,2},{1,3},{2,0},{3,1},{4,6},{5,7},{6,4},{7,5},{8,10},{9,11},{10,... | collective-permute-start | bytes 1179656 | tf_op jit(solution)/shard_map/ppermute | solution.py:527
  177.6 12.5 %copy-start.15 = (f32[16,176]{1,0:T(8,128)S(1)}, f32[16,176]{1,0:T(8,128)}, u32[]{:S(2)}) copy-start(f32[16,176]{1,0:T(8,128)} %shard_map.320) | copy-start | bytes 33796
  177.6 13.5 %copy-start.17 = (f32[1,2048]{1,0:T(1,128)S(1)}, f32[1,2048]{1,0:T(1,128)}, u32[]{:S(2)}) copy-start(f32[1,2048]{1,0:T(1,128)} %get-tuple-element.131) | copy-start | bytes 24580
  191.4 6.5 %collective-permute-start.15 = (bf16[2,2,16,1536]{3,2,1,0:T(8,128)(2,1)S(1)}, bf16[2,2,16,1536]{3,2,1,0:T(8,128)(2,1)S(1)}, u32[]{:S(2)}, u32[]{:S(2)}) collective-permute-start(bf16[2,2,16,1536]{3,2,1,0:T(8,128)(2,1)S(1)} %fusion.11), channel_id=1, source_target_pairs={{0,4},{4,0},{8,12},{12,8},{16,20},{20,16},{24,28},{28,24},{1,5},{5... | collective-permute-start | bytes 589832 | tf_op jit(solution)/shard_map/ppermute | solution.py:527
  191.6 1.2 collective-permute-start.16
  191.6 18.7 %collective-permute-start.14 = (bf16[2,16,4608]{2,1,0:T(8,128)(2,1)S(1)}, bf16[2,16,4608]{2,1,0:T(8,128)(2,1)S(1)}, u32[]{:S(2)}, u32[]{:S(2)}) collective-permute-start(bf16[2,16,4608]{2,1,0:T(8,128)(2,1)S(1)} %get-tuple-element.147), channel_id=1, source_target_pairs={{0,16},{4,20},{8,24},{12,28},{16,0},{20,4},{24,8},{28,12},{1,17},{... | collective-permute-start | bytes 884744 | tf_op jit(solution)/shard_map/ppermute | solution.py:527
  198.1 5.6 %collective-permute-start.17 = (f32[72,128]{1,0:T(8,128)S(1)}, f32[72,128]{1,0:T(8,128)S(1)}, u32[]{:S(2)}, u32[]{:S(2)}) collective-permute-start(f32[72,128]{1,0:T(8,128)S(1)} %add.275), channel_id=1, source_target_pairs={{0,2},{1,3},{2,0},{3,1},{4,6},{5,7},{6,4},{7,5},{8,10},{9,11},{10,... | collective-permute-start | bytes 110600 | tf_op jit(solution)/shard_map/ppermute | solution.py:527
  199.3 12.6 %collective-permute-start.18 = (bf16[16,1536]{1,0:T(8,128)(2,1)S(1)}, bf16[16,1536]{1,0:T(8,128)(2,1)S(1)}, u32[]{:S(2)}, u32[]{:S(2)}) collective-permute-start(bf16[16,1536]{1,0:T(8,128)(2,1)S(1)} %get-tuple-element.158), channel_id=1, source_target_pairs={{0,8},{4,12},{8,0},{12,4},{16,24},{20,28},{24,16},{28,20},{1,9},{5... | collective-permute-start | bytes 147464 | tf_op jit(solution)/shard_map/ppermute | solution.py:527
  199.3 12.6 %collective-permute-start.19 = (bf16[16,1536]{1,0:T(8,128)(2,1)S(1)}, bf16[16,1536]{1,0:T(8,128)(2,1)S(1)}, u32[]{:S(2)}, u32[]{:S(2)}) collective-permute-start(bf16[16,1536]{1,0:T(8,128)(2,1)S(1)} %get-tuple-element.159), channel_id=1, source_target_pairs={{0,16},{4,20},{8,24},{12,28},{16,0},{20,4},{24,8},{28,12},{1,17},{... | collective-permute-start | bytes 147464 | tf_op jit(solution)/shard_map/ppermute | solution.py:527
  199.5 12.4 %collective-permute-start.20 = (bf16[16,1536]{1,0:T(8,128)(2,1)S(1)}, bf16[16,1536]{1,0:T(8,128)(2,1)S(1)}, u32[]{:S(2)}, u32[]{:S(2)}) collective-permute-start(bf16[16,1536]{1,0:T(8,128)(2,1)S(1)} %get-tuple-element.160), channel_id=1, source_target_pairs={{0,24},{4,28},{8,16},{12,20},{16,8},{20,12},{24,0},{28,4},{1,25},{... | collective-permute-start | bytes 147464 | tf_op jit(solution)/shard_map/ppermute | solution.py:527
  210.4 4.0 %collective-permute-start.22 = (f32[72,128]{1,0:T(8,128)S(1)}, f32[72,128]{1,0:T(8,128)S(1)}, u32[]{:S(2)}, u32[]{:S(2)}) collective-permute-start(f32[72,128]{1,0:T(8,128)S(1)} %add.276), channel_id=1, source_target_pairs={{0,4},{4,0},{8,12},{12,8},{16,20},{20,16},{24,28},{28,24},{1,5},{5... | collective-permute-start | bytes 110600 | tf_op jit(solution)/shard_map/ppermute | solution.py:527
  211.8 5.6 %collective-permute-start.21 = (bf16[16,4608]{1,0:T(8,128)(2,1)S(1)}, bf16[16,4608]{1,0:T(8,128)(2,1)S(1)}, u32[]{:S(2)}, u32[]{:S(2)}) collective-permute-start(bf16[16,4608]{1,0:T(8,128)(2,1)S(1)} %fusion.14), channel_id=1, source_target_pairs={{0,8},{4,12},{8,0},{12,4},{16,24},{20,28},{24,16},{28,20},{1,9},{5... | collective-permute-start | bytes 442376 | tf_op jit(solution)/shard_map/ppermute | solution.py:527
  211.9 19.9 %copy-start.10 = (bf16[16,1536]{1,0:T(8,128)(2,1)}, bf16[16,1536]{1,0:T(8,128)(2,1)S(1)}, u32[]{:S(2)}) copy-start(bf16[16,1536]{1,0:T(8,128)(2,1)S(1)} %add_convert_fusion.10.refs_0_) | copy-start | bytes 147460
  217.4 5.4 %collective-permute-start.23 = (bf16[16,4608]{1,0:T(8,128)(2,1)S(1)}, bf16[16,4608]{1,0:T(8,128)(2,1)S(1)}, u32[]{:S(2)}, u32[]{:S(2)}) collective-permute-start(bf16[16,4608]{1,0:T(8,128)(2,1)S(1)} %fusion.10), channel_id=1, source_target_pairs={{0,1},{1,0},{2,3},{3,2},{4,5},{5,4},{6,7},{7,6},{8,9},{9,8},{10,11... | collective-permute-start | bytes 442376 | tf_op jit(solution)/shard_map/ppermute | solution.py:527
  217.5 5.3 %collective-permute-start.27 = (f32[72,128]{1,0:T(8,128)S(1)}, f32[72,128]{1,0:T(8,128)S(1)}, u32[]{:S(2)}, u32[]{:S(2)}) collective-permute-start(f32[72,128]{1,0:T(8,128)S(1)} %add.286), channel_id=1, source_target_pairs={{0,16},{4,20},{8,24},{12,28},{16,0},{20,4},{24,8},{28,12},{1,17},{... | collective-permute-start | bytes 110600 | tf_op jit(solution)/shard_map/ppermute | solution.py:527
  217.6 5.3 %collective-permute-start.24 = (bf16[16,1536]{1,0:T(8,128)(2,1)S(1)}, bf16[16,1536]{1,0:T(8,128)(2,1)S(1)}, u32[]{:S(2)}, u32[]{:S(2)}) collective-permute-start(bf16[16,1536]{1,0:T(8,128)(2,1)S(1)} %add_convert_fusion.10.refs_0_), channel_id=1, source_target_pairs={{0,1},{1,0},{2,3},{3,2},{4,5},{5,4},{6,7},{7,6},{8,9},{9,8},{10,11... | collective-permute-start | bytes 147464 | tf_op jit(solution)/shard_map/ppermute | solution.py:527
  218.0 4.9 %collective-permute-start.25 = (bf16[16,1536]{1,0:T(8,128)(2,1)S(1)}, bf16[16,1536]{1,0:T(8,128)(2,1)S(1)}, u32[]{:S(2)}, u32[]{:S(2)}) collective-permute-start(bf16[16,1536]{1,0:T(8,128)(2,1)S(1)} %add_convert_fusion.10.refs_0_), channel_id=1, source_target_pairs={{0,2},{1,3},{2,0},{3,1},{4,6},{5,7},{6,4},{7,5},{8,10},{9,11},{10,... | collective-permute-start | bytes 147464 | tf_op jit(solution)/shard_map/ppermute | solution.py:527
  218.6 4.3 %collective-permute-start.26 = (bf16[16,1536]{1,0:T(8,128)(2,1)S(1)}, bf16[16,1536]{1,0:T(8,128)(2,1)S(1)}, u32[]{:S(2)}, u32[]{:S(2)}) collective-permute-start(bf16[16,1536]{1,0:T(8,128)(2,1)S(1)} %add_convert_fusion.10.refs_0_), channel_id=1, source_target_pairs={{0,3},{1,2},{2,1},{3,0},{4,7},{5,6},{6,5},{7,4},{8,11},{9,10},{10,... | collective-permute-start | bytes 147464 | tf_op jit(solution)/shard_map/ppermute | solution.py:527
  222.9 9.0 %copy-start.5 = (bf16[2,16,4608]{2,1,0:T(8,128)(2,1)}, bf16[2,16,4608]{2,1,0:T(8,128)(2,1)S(1)}, u32[]{:S(2)}) copy-start(bf16[2,16,4608]{2,1,0:T(8,128)(2,1)S(1)} %pad_maximum_fusion.1.both_ref) | copy-start | bytes 884740
  222.9 9.0 %copy-start.11 = (bf16[16,1536]{1,0:T(8,128)(2,1)}, bf16[16,1536]{1,0:T(8,128)(2,1)S(1)}, u32[]{:S(2)}) copy-start(bf16[16,1536]{1,0:T(8,128)(2,1)S(1)} %collective-permute-done.24.refs_1_) | copy-start | bytes 147460
  222.9 9.0 %copy-start.12 = (bf16[16,1536]{1,0:T(8,128)(2,1)}, bf16[16,1536]{1,0:T(8,128)(2,1)S(1)}, u32[]{:S(2)}) copy-start(bf16[16,1536]{1,0:T(8,128)(2,1)S(1)} %collective-permute-done.25.refs_2_) | copy-start | bytes 147460
  222.9 9.0 %copy-start.13 = (bf16[16,1536]{1,0:T(8,128)(2,1)}, bf16[16,1536]{1,0:T(8,128)(2,1)S(1)}, u32[]{:S(2)}) copy-start(bf16[16,1536]{1,0:T(8,128)(2,1)S(1)} %collective-permute-done.26.refs_3_) | copy-start | bytes 147460
  222.9 11.2 %collective-permute-start.29 = (f32[72,128]{1,0:T(8,128)S(1)}, f32[72,128]{1,0:T(8,128)S(1)}, u32[]{:S(2)}, u32[]{:S(2)}) collective-permute-start(f32[72,128]{1,0:T(8,128)S(1)} %add.287), channel_id=1, source_target_pairs={{0,8},{4,12},{8,0},{12,4},{16,24},{20,28},{24,16},{28,20},{1,9},{5... | collective-permute-start | bytes 110600 | tf_op jit(solution)/shard_map/ppermute | solution.py:527
  223.7 11.1 %collective-permute-start.28 = (bf16[2,16,4608]{2,1,0:T(8,128)(2,1)S(1)}, bf16[2,16,4608]{2,1,0:T(8,128)(2,1)S(1)}, u32[]{:S(2)}, u32[]{:S(2)}) collective-permute-start(bf16[2,16,4608]{2,1,0:T(8,128)(2,1)S(1)} %pad_maximum_fusion.1.both_ref), channel_id=1, source_target_pairs={{0,2},{1,3},{2,0},{3,1},{4,6},{5,7},{6,4},{7,5},{8,10},{9,11},{10,... | collective-permute-start | bytes 884744 | tf_op jit(solution)/shard_map/ppermute | solution.py:527
  225.5 6.4 %copy-start.2 = (bf16[8,14,14,512]{3,2,1,0:T(8,128)(2,1)S(1)}, bf16[8,14,14,512]{3,2,1,0:T(8,128)(2,1)}, u32[]{:S(2)}) copy-start(bf16[8,14,14,512]{3,2,1,0:T(8,128)(2,1)} %get-tuple-element.153) | copy-start | bytes 4816900
  231.9 6.0 %copy-start.1 = (bf16[64,2048]{1,0:T(8,128)(2,1)S(1)}, bf16[64,2048]{1,0:T(8,128)(2,1)}, u32[]{:S(2)}) copy-start(bf16[64,2048]{1,0:T(8,128)(2,1)} %param.35) | copy-start | bytes 786436
  (5 other events, 3.6 us)
Sparse Core Ops, SparseCore 0:
  11.0 66.3 all-gather.1

commit v4 on v3

--- a/solution.py
+++ b/solution.py
@@ -3,6 +3,7 @@
 import numpy as np
 from jax import lax
 from jax.experimental import pallas as pl
+from jax.experimental.layout import Layout, with_layout_constraint
 from jax.experimental.pallas import tpu as pltpu
 from jax.sharding import PartitionSpec as P
 
@@ -523,6 +524,10 @@
     return lax.all_gather(shard, "fsdp", axis=0, tiled=True)
 
 
+def images_last(grids):
+    return with_layout_constraint(grids.transpose(1, 2, 0, 3), Layout((0, 1, 2, 3)))
+
+
 def swap(value, axis, bits):
     return lax.ppermute(value, axis, [(i, i ^ bits) for i in range(lax.axis_size(axis))])
 
@@ -589,6 +594,14 @@
 def scatter_bits():
     mine, replica = lax.axis_index("fsdp"), lax.axis_index("rep")
     return mine // 4, mine // 2 % 2, mine % 2, replica // 2, replica % 2
+
+
+def scatter_plane(kept, got, row, side):
+    parts = []
+    for far_row, far_side in ((0, 0), (1, 0), (0, 1), (1, 1)):
+        at = [pick(pick(part, row ^ far_row, 0), side ^ far_side, 0) for part in (kept, got)]
+        parts.append(added(*at))
+    return parts
 
 
 def scatter_step(kept, got, bit):
@@ -644,47 +657,39 @@
     return outs[:4], [out.reshape(-1) for out in outs[4:]]
 
 
-def finish(kept_mlp, got_mlp, kept, got, vector, results):
-    far, near, side, _, _ = scatter_bits()
+def finish(kept_mlp, got_mlp, kept, got, vector, result):
+    _, near, side, _, _ = scatter_bits()
     line = lax.axis_index("fsdp") // 2
     tie = lax.optimization_barrier
     kept_mlp, got_mlp, kept, got, vector = tie((kept_mlp, got_mlp, kept, got, vector))
-    kept_mlp, away_mlp = scatter_step(kept_mlp, got_mlp, far)
+    kept_mlp, away_mlp = scatter_step(kept_mlp, got_mlp, near)
     kept, away = scatter_step(kept, got, side)
     rows = jnp.pad(jnp.concatenate(vector), (0, -sum(v.shape[0] for v in vector) % 1024))
     rows = rows.reshape(-1, 128)
 
     away_mlp, away, rows = tie((away_mlp, away, rows))
-    got_mlp = swap(away_mlp, "fsdp", 4)
+    total_mlp = added(kept_mlp, swap(away_mlp, "fsdp", 2))
     total = added(kept, swap(away, "fsdp", 1)).reshape(4, kept.shape[-2], kept.shape[-1])
     own = pick(total, line, 0)
     pieces = [pick(total, line ^ d, 0) for d in (1, 2, 3)]
     rows = rows + swap(rows, "rep", 1)
 
-    own, pieces, rows, results = tie((own, pieces, rows, results))
-    results = tuple(result.transpose(1, 2, 0, 3) for result in results)
-    got_pieces = [swap(pieces[d - 1], "fsdp", 2 * d) for d in (1, 2, 3)]
+    own, pieces, total_mlp, rows = tie((own, pieces, total_mlp, rows))
+    result = images_last(result)
+    total = own.astype(F32)
+    for d in (1, 2, 3):
+        total = total + swap(pieces[d - 1], "fsdp", 2 * d).astype(F32)
+    total = total.astype(BF16)
+    both_mlp = jnp.stack([total_mlp, swap(total_mlp, "rep", 1)])
     rows = rows + swap(rows, "rep", 2)
-
-    got_mlp, kept_mlp, rows, results = tie((got_mlp, kept_mlp, rows, results))
-    kept_mlp, away_mlp = scatter_step(kept_mlp, got_mlp, near)
-    total_mlp = added(kept_mlp, swap(away_mlp, "fsdp", 2))
     rows = rows + swap(rows, "fsdp", 1)
-    total = own.astype(F32)
-    for piece in got_pieces:
-        total = total + piece.astype(F32)
-    total = total.astype(BF16)
-
-    total, total_mlp, rows = tie((total, total_mlp, rows))
+
+    total, both_mlp, rows, result = tie((total, both_mlp, rows, result))
     parts = [total] + [swap(total, "rep", e) for e in (1, 2, 3)]
-    both_mlp = jnp.stack([total_mlp, swap(total_mlp, "rep", 1)])
+    rest_mlp = swap(both_mlp, "rep", 2)
     rows = rows + swap(rows, "fsdp", 4)
-
-    both_mlp, parts, rows = tie((both_mlp, parts, rows))
-    rest_mlp = swap(both_mlp, "rep", 2)
     rows = rows + swap(rows, "fsdp", 2)
-    results = tuple(result.transpose(2, 0, 1, 3) for result in results)
-    return [both_mlp, rest_mlp], parts, rows, results
+    return [both_mlp, rest_mlp], parts, rows, result.transpose(2, 0, 1, 3)
 
 
 def reduce_weight_grad(partial):
@@ -763,18 +768,28 @@
         jnp.stack([image_counts[0, 0], core]), win, merged, cotangent, order, back,
         (six, bias_exp, joined_weights),
     )
+    tie = lax.optimization_barrier
     if paired:
         split = (2, 2, 2, 2, 16, -1)
-        kept_mlp, away = kept_mlp.reshape(split), away_mlp.reshape(split)
-        kept_mlp, away = scatter_step(kept_mlp, swap(away, "rep", 1), row)
-        d_att, away = lax.optimization_barrier((d_att, away))
-        got = swap(away, "rep", 2)
+        got = swap(away_mlp.reshape(split), "rep", 1)
+        plane = scatter_plane(kept_mlp.reshape(split), got, row, side)
+        d_att, plane, block_output = tie((d_att, plane, images_last(block_output)))
+        block_output = block_output.transpose(2, 0, 1, 3)
+        plane = [
+            plane[0],
+            swap(plane[1], "rep", 2),
+            swap(plane[2], "fsdp", 1),
+            swap(plane[3], ("fsdp", "rep"), lax.axis_size("rep") + 2),
+        ]
     d_packed, pairs, kept, away = run_attend_back(core[None], packed, soft, d_att, attend_in)
     if paired:
-        kept_mlp, away_mlp = scatter_step(kept_mlp, got, side)
-        pairs, away, away_mlp = lax.optimization_barrier((pairs, away, away_mlp))
+        halved = [halves(part, far, 0) for part in plane]
+        kept_mlp, away_mlp = (
+            sum(half[at].astype(F32) for half in halved).astype(BF16) for at in (0, 1)
+        )
+        pairs, away, away_mlp = tie((pairs, away, away_mlp))
         kept, away = kept.reshape(split), away.reshape(split)
-        got, got_mlp = swap(away, "rep", 1), swap(away_mlp, "fsdp", 1)
+        got, got_mlp = swap(away, "rep", 1), swap(away_mlp, "fsdp", 4)
     table_part = run_table(pairs, index_rows)
     if paired:
         kept, away = scatter_step(kept, got, row)
@@ -788,8 +803,8 @@
         d_packed_bias[0, :C], d_packed_bias[0, 2 * C :], d_exp_bias[0], table_part.reshape(-1),
     )
     if paired:
-        mlp_pieces, part_pieces, rows, (block_output, input_grad) = finish(
-            kept_mlp, got_mlp, kept, got, small, (block_output, input_grad)
+        mlp_pieces, part_pieces, rows, input_grad = finish(
+            kept_mlp, got_mlp, kept, got, small, input_grad
         )
         (output_grad, expand_grad, reduce_grad, attend_grad), owned = run_join(
             mlp_pieces, part_pieces, rows,

time: 246 us -> 238 us (0.967)
  waiting for transfers between devices: 27 us -> 16.1 us
  starting transfers between devices: 29.6 us -> 32.3 us
    ppermute x30 -> x31, waiting for transfers between devices: 27 us -> 16.1 us  [swap(): lax.ppermute(value, axis, [(i, i ^ bits) for i in range(lax.axis_size(axi...]
    pallas_call x0 -> x2, local copies, waits for them, and re-layouts: none -> 10.1 us  [the longest x1 6.26 us: run_input(): pl.pallas_call(input_kernel, grid=(shape[0],), out_shape=(struct(shape, F...]
    unnamed x58 -> x56, local copies, waits for them, and re-layouts: 12.7 us -> 4.6 us
    ppermute x30 -> x31, starting transfers between devices: 29.6 us -> 32.2 us  [swap(): lax.ppermute(value, axis, [(i, i ^ bits) for i in range(lax.axis_size(axi...]
  transfers between devices with their start and end apart: 31 -> 32, of which waited for: 8 -> 10; matrix products, arithmetic and copies ran while one was open for 11% -> 12% of each run, Pallas kernels for 34% -> 36%
where the time goes in v4:
time: 238 us; the launch traced here: 237 us
  Pallas kernels  136 us (57%)
  starting transfers between devices  32.3 us (14%)
  local copies, waits for them, and re-layouts  31.3 us (13%)
  waiting for transfers between devices  16.1 us (7%)
  between operations  15.3 us (6%)
  other arithmetic  5.59 us (2%)
    pallas_call x1, Pallas kernels, run_mlp(): pl.pallas_call(mlp_kernel, grid=(images // per,), out_shape=(struct(cotan...  49.7 us
    ppermute x31, starting transfers between devices, swap(): lax.ppermute(value, axis, [(i, i ^ bits) for i in range(lax.axis_size(axi...  32.2 us
    pallas_call x1, Pallas kernels, run_attend_back(): pl.pallas_call(attend_back_kernel, grid=(images,), out_shape=(struct(pack...  30.9 us
    pallas_call x1, Pallas kernels, run_attend(): pl.pallas_call(attend_kernel, grid=(images,), out_shape=(struct((rows, C)...  29.4 us
    ppermute x31, waiting for transfers between devices, swap(): lax.ppermute(value, axis, [(i, i ^ bits) for i in range(lax.axis_size(axi...  16.1 us
    pallas_call x1, Pallas kernels, run_input(): pl.pallas_call(input_kernel, grid=(shape[0],), out_shape=(struct(shape, F...  12.6 us
    pallas_call x1, Pallas kernels, run_table(): pl.pallas_call(table_kernel, out_shape=struct((HEADS, TABLE_PAD), F32), i...  6.38 us
    pallas_call x1, local copies, waits for them, and re-layouts, run_input(): pl.pallas_call(input_kernel, grid=(shape[0],), out_shape=(struct(shape, F...  6.26 us
  transfers between devices with their start and end apart: 32, of which 10 were waited for; matrix products, arithmetic and copies ran while one was open for 12% of the time, Pallas kernels for 36%

profile of v4, /device:TPU:0, one launch (start us, length us, event | category | flops | bytes accessed | tf_op | source)
XLA Modules:
  0.0 236.9 jit_solution(14307881572168189976)
XLA Ops:
  7.3 0.9 copy-done
  8.1 0.7 constant_dynamic-slice_fusion.2
  8.9 0.8 constant_dynamic-slice_fusion
  10.4 0.9 constant_dynamic-slice_fusion.3
  11.3 3.0 %collective-permute-start = (bf16[32,1536]{1,0:T(8,128)(2,1)S(1)}, bf16[32,1536]{1,0:T(8,128)(2,1)S(1)}, u32[]{:S(2)}, u32[]{:S(2)}) collective-permute-start(bf16[32,1536]{1,0:T(8,128)(2,1)S(1)} %constant_dynamic-slice_fusion.3), channel_id=1, source_target_pairs={{0,8},{4,12},{8,0},{12,4},{16,24},{20,28},{24,16},{28,20},{1,9},{5... | collective-permute-start | bytes 294920 | tf_op jit(solution)/shard_map/ppermute | solution.py:532
  14.4 2.6 %collective-permute-start.1 = (bf16[32,1536]{1,0:T(8,128)(2,1)S(1)}, bf16[32,1536]{1,0:T(8,128)(2,1)S(1)}, u32[]{:S(2)}, u32[]{:S(2)}) collective-permute-start(bf16[32,1536]{1,0:T(8,128)(2,1)S(1)} %constant_dynamic-slice_fusion.3), channel_id=1, source_target_pairs={{0,16},{4,20},{8,24},{12,28},{16,0},{20,4},{24,8},{28,12},{1,17},{... | collective-permute-start | bytes 294920 | tf_op jit(solution)/shard_map/ppermute | solution.py:532
  16.9 5.4 %concatenate.26 = bf16[768]{0:T(1024)(128)(2,1)S(1)} concatenate(bf16[64]{0:T(256)(128)(2,1)} %param.26, bf16[64]{0:T(256)(128)(2,1)} %param.27, bf16[64]{0:T(256)(128)(2,1)} %param.32, bf16[64]{0:T(256)(128)(2,1)} %param.33, bf16[64]{0:T(256)(128)(2,1)} %param.34, bf16[64]{0:T(256)(128)(2,1)} %param.38, bf16[128]{0:T(256)(128)(2,1)} %param.29, bf16[256]{0:T(256)(128)(2,1)} %param.36), dimensions={0} | concatenate | bytes 3072 | tf_op jit(solution)/shard_map/concatenate | solution.py:741
  22.4 1.9 collective-permute-start.3
  24.9 0.7 xor_compare_fusion
  25.6 0.8 broadcast_add_fusion
  27.7 2.5 %collective-permute-start.5 = (bf16[2,6,128]{2,1,0:T(8,128)(2,1)S(1)}, bf16[2,6,128]{2,1,0:T(8,128)(2,1)S(1)}, u32[]{:S(2)}, u32[]{:S(2)}) collective-permute-start(bf16[2,6,128]{2,1,0:T(8,128)(2,1)S(1)} %pad_maximum_fusion.5), channel_id=1, source_target_pairs={{0,8},{4,12},{8,0},{12,4},{16,24},{20,28},{24,16},{28,20},{1,9},{5... | collective-permute-start | bytes 9224 | tf_op jit(solution)/shard_map/ppermute | solution.py:532
  32.3 1.5 collective-permute-start.4
  34.4 5.1 %shard_map.316.pair_ref = f32[16,208,208]{2,1,0:T(8,128)} custom-call(s32[208]{0:T(256)} %pad.16.code_ref, s32[1,208]{1,0:T(1,128)} %bitcast.139, s32[49,208]{1,0:T(8,128)} %pad.17.index_ref, bf16[16,176]{1,0:T(8,128)(2,1)} %pad.18.table_ref), custom_call_target="tpu_custom_call" | custom-call | flops 2000000000 | bytes 4000000 | tf_op jit(solution)/shard_map/pallas_call | solution.py:374
  39.6 1.8 copy.57.grid_ref
  41.4 1.8 copy.59.grid_ref
  43.1 1.4 collective-permute-done.6
  45.0 0.7 reshape.221.rows_in_ref.six_ref
  46.9 0.7 copy-done.20
  47.6 0.7 copy-done.21
  48.3 29.4 %shard_map.317 = (bf16[1664,512]{1,0:T(8,128)(2,1)}, bf16[1664,512]{1,0:T(8,128)(2,1)}, bf16[1664,1536]{1,0:T(8,128)(2,1)}, bf16[8,16,208,208]{3,2,1,0:T(8,128)(...) custom-call(s32[16]{0:T(128)} %stack.93.starts_ref, bf16[8,14,14,512]{3,2,1,0:T(8,128)(2,1)} %copy.57.grid_ref, ...), custom_call_target="tpu_custom_call" | custom-call | flops 40000000000 | bytes 48000000 | tf_op jit(solution)/shard_map/pallas_call | solution.py:399
  77.7 49.7 %shard_map.318 = (bf16[8,14,14,512]{3,2,1,0:T(8,128)(2,1)}, f32[1664,512]{1,0:T(8,128)}, bf16[1664,512]{1,0:T(8,128)(2,1)}, bf16[16,16,4608]{2,1,0:T(8,128)(2,1)...) custom-call(s32[2]{0:T(128)} %pad_add_fusion.count_ref, ...), custom_call_target="tpu_custom_call" | custom-call | flops 48000000000 | bytes 32000000 | tf_op jit(solution)/shard_map/pallas_call | solution.py:441
  128.0 3.8 %copy.69 = bf16[8,14,14,512]{3,0,2,1:T(8,128)(2,1)} copy(bf16[8,14,14,512]{3,2,1,0:T(8,128)(2,1)} %get-tuple-element.105) | data formatting | bytes 3211264 | tf_op jit(solution)/shard_map/pallas_call | solution.py:441
  132.3 0.7 fusion.3
  133.0 1.2 collective-permute-start.10
  134.3 2.5 %collective-permute-start.11 = (bf16[2,2,16,4608]{3,2,1,0:T(8,128)(2,1)S(1)}, bf16[2,2,16,4608]{3,2,1,0:T(8,128)(2,1)S(1)}, u32[]{:S(2)}, u32[]{:S(2)}) collective-permute-start(bf16[2,2,16,4608]{3,2,1,0:T(8,128)(2,1)S(1)} %get-tuple-element.109), channel_id=1, source_target_pairs={{0,4},{4,0},{8,12},{12,8},{16,20},{20,16},{24,28},{28,24},{1,5},{5... | collective-permute-start | bytes 1769480 | tf_op jit(solution)/shard_map/ppermute | solution.py:532
  137.1 30.9 %shard_map.319 = (bf16[1664,1536]{1,0:T(8,128)(2,1)}, f32[16,208,208]{2,1,0:T(8,128)}, bf16[16,16,1536]{2,1,0:T(8,128)(2,1)}, bf16[16,16,1536]{2,1,0:T(8,128)(2,1)}) custom-call(s32[1]{0:T(128)} %bitcast.1.core_ref, bf16[1664,1536]{1,0:T(8,128)(2,1)} %get-tuple-element.111.packed_ref, bf16[8,16,208,208]{3,2,1,0:T(8,128)(2,1)} %get-tuple-element.112.soft_ref, ...), custom_call_target="tpu_custom_call" | custom-call | flops 48000000000 | bytes 48000000 | tf_op jit(solution)/shard_map/pallas_call | solution.py:480
  168.7 1.0 collective-permute-start.13
  169.7 6.4 %shard_map.320 = f32[16,176]{1,0:T(8,128)} custom-call(f32[16,208,208]{2,1,0:T(8,128)} %get-tuple-element.121.sums_ref, s32[49,208]{1,0:T(8,128)} %pad.17.index_ref), custom_call_target="tpu_custom_call" | custom-call | flops 2000000000 | bytes 4000000 | tf_op jit(solution)/shard_map/pallas_call | solution.py:385
  176.3 1.5 collective-permute-start.15
  177.9 12.6 %shard_map.321 = (f32[8,14,14,512]{3,2,1,0:T(8,128)}, f32[8,512]{1,0:T(8,128)}, f32[1,1536]{1,0:T(1,128)}) custom-call(bf16[1664,1536]{1,0:T(8,128)(2,1)} %get-tuple-element.123.d_packed_ref, bf16[1664,512]{1,0:T(8,128)(2,1)} %get-tuple-element.99.win_ref, f32[1664,512]{1,0:T(8,128)} %get-tuple-element.124.d_res_ref, f32[6,512]{1,0:T(8,128)} %reshape.221.rows_in_ref.six_ref, ...), custom_call_target="tpu_custom_call" | custom-call | flops 8000000000 | bytes 16000000 | tf_op jit(solution)/shard_map/pallas_call | solution.py:504
  190.5 0.8 fusion.16
  193.5 3.6 %collective-permute-done.17 = bf16[16,4608]{1,0:T(8,128)(2,1)S(1)} collective-permute-done((bf16[16,4608]{1,0:T(8,128)(2,1)S(1)}, bf16[16,4608]{1,0:T(8,128)(2,1)S(1)}, u32[]{:S(2)}, u32[]{:S(2)}) %collective-permute-start.17) | collective-permute-done | bytes 147488 | tf_op jit(solution)/shard_map/ppermute | solution.py:532
  197.1 2.5 %collective-permute-done.16 = bf16[2,2,16,1536]{3,2,1,0:T(8,128)(2,1)S(1)} collective-permute-done((bf16[2,2,16,1536]{3,2,1,0:T(8,128)(2,1)S(1)}, bf16[2,2,16,1536]{3,2,1,0:T(8,128)(2,1)S(1)}, u32[]{:S(2)}, u32[]{:S(2)}) %collective-permute-start.16) | collective-permute-done | bytes 196640 | tf_op jit(solution)/shard_map/ppermute | solution.py:532
  199.7 1.5 collective-permute-start.19
  201.2 2.0 collective-permute-start.20
  203.2 1.0 collective-permute-start.21
  204.7 6.3 %copy.68 = f32[8,14,14,512]{3,0,2,1:T(8,128)} copy(f32[8,14,14,512]{3,2,1,0:T(8,128)} %get-tuple-element.154) | data formatting | bytes 6422528 | tf_op jit(solution)/shard_map/pallas_call | solution.py:504
  211.0 1.5 collective-permute-start.24
  212.5 2.5 %collective-permute-done.24 = f32[72,128]{1,0:T(8,128)S(1)} collective-permute-done((f32[72,128]{1,0:T(8,128)S(1)}, f32[72,128]{1,0:T(8,128)S(1)}, u32[]{:S(2)}, u32[]{:S(2)}) %collective-permute-start.24) | collective-permute-done | bytes 36896 | tf_op jit(solution)/shard_map/ppermute | solution.py:532
  215.1 1.3 collective-permute-start.29
  216.3 1.5 collective-permute-start.25
  217.8 2.5 %collective-permute-done.29 = f32[72,128]{1,0:T(8,128)S(1)} collective-permute-done((f32[72,128]{1,0:T(8,128)S(1)}, f32[72,128]{1,0:T(8,128)S(1)}, u32[]{:S(2)}, u32[]{:S(2)}) %collective-permute-start.29) | collective-permute-done | bytes 36896 | tf_op jit(solution)/shard_map/ppermute | solution.py:532
  221.5 1.1 collective-permute-start.27
  222.6 0.7 collective-permute-start.28
  223.3 1.0 collective-permute-done.30
  225.7 0.7 collective-permute-done.28.refs_3_
  227.0 0.7 copy-done.8
  227.7 2.3 shard_map.322
  (143 shorter events, 14.5 us)
Async XLA Ops:
  7.2 1.0 copy-start
  7.2 23.0 %copy-start.14 = (s32[49,49]{1,0:T(8,128)S(1)}, s32[49,49]{1,0:T(8,128)}, u32[]{:S(2)}) copy-start(s32[49,49]{1,0:T(8,128)} %param.25) | copy-start | bytes 28816
  7.2 23.9 %copy-start.16 = (bf16[169,16]{0,1:T(8,128)(2,1)S(1)}, bf16[169,16]{0,1:T(8,128)(2,1)}, u32[]{:S(2)}) copy-start(bf16[169,16]{0,1:T(8,128)(2,1)} %param.30) | copy-start | bytes 16228
  7.2 70.5 %all-gather.2.cloned.1.call-start = ((), (), s32[]{:S(2)}) async-start(), calls=%async_computation | async-start | bytes 4866048 | tf_op jit(solution)/shard_map/all_gather | solution.py:578
  11.3 16.3 %collective-permute-start = (bf16[32,1536]{1,0:T(8,128)(2,1)S(1)}, bf16[32,1536]{1,0:T(8,128)(2,1)S(1)}, u32[]{:S(2)}, u32[]{:S(2)}) collective-permute-start(bf16[32,1536]{1,0:T(8,128)(2,1)S(1)} %constant_dynamic-slice_fusion.3), channel_id=1, source_target_pairs={{0,8},{4,12},{8,0},{12,4},{16,24},{20,28},{24,16},{28,20},{1,9},{5... | collective-permute-start | bytes 294920 | tf_op jit(solution)/shard_map/ppermute | solution.py:532
  14.4 13.3 %collective-permute-start.1 = (bf16[32,1536]{1,0:T(8,128)(2,1)S(1)}, bf16[32,1536]{1,0:T(8,128)(2,1)S(1)}, u32[]{:S(2)}, u32[]{:S(2)}) collective-permute-start(bf16[32,1536]{1,0:T(8,128)(2,1)S(1)} %constant_dynamic-slice_fusion.3), channel_id=1, source_target_pairs={{0,16},{4,20},{8,24},{12,28},{16,0},{20,4},{24,8},{28,12},{1,17},{... | collective-permute-start | bytes 294920 | tf_op jit(solution)/shard_map/ppermute | solution.py:532
  16.9 10.7 %collective-permute-start.2 = (bf16[32,1536]{1,0:T(8,128)(2,1)S(1)}, bf16[32,1536]{1,0:T(8,128)(2,1)S(1)}, u32[]{:S(2)}, u32[]{:S(2)}) collective-permute-start(bf16[32,1536]{1,0:T(8,128)(2,1)S(1)} %constant_dynamic-slice_fusion.3), channel_id=1, source_target_pairs={{0,24},{4,28},{8,16},{12,20},{16,8},{20,12},{24,0},{28,4},{1,25},{... | collective-permute-start | bytes 294920 | tf_op jit(solution)/shard_map/ppermute | solution.py:532
  22.4 5.2 %collective-permute-start.3 = (bf16[1,6,128]{2,1,0:T(8,128)(2,1)S(1)}, bf16[1,6,128]{2,1,0:T(8,128)(2,1)S(1)}, u32[]{:S(2)}, u32[]{:S(2)}) collective-permute-start(bf16[1,6,128]{2,1,0:T(8,128)(2,1)S(1)} %bitcast.129), channel_id=1, source_target_pairs={{0,16},{4,20},{8,24},{12,28},{16,0},{20,4},{24,8},{28,12},{1,17},{... | collective-permute-start | bytes 4616 | tf_op jit(solution)/shard_map/ppermute | solution.py:532
  27.7 11.9 %copy-start.7 = (bf16[128,1536]{1,0:T(8,128)(2,1)}, bf16[128,1536]{1,0:T(8,128)(2,1)S(1)}, u32[]{:S(2)}) copy-start(bf16[128,1536]{1,0:T(8,128)(2,1)S(1)} %pad_maximum_fusion.rest_0_) | copy-start | bytes 1179652
  27.7 6.1 %collective-permute-start.5 = (bf16[2,6,128]{2,1,0:T(8,128)(2,1)S(1)}, bf16[2,6,128]{2,1,0:T(8,128)(2,1)S(1)}, u32[]{:S(2)}, u32[]{:S(2)}) collective-permute-start(bf16[2,6,128]{2,1,0:T(8,128)(2,1)S(1)} %pad_maximum_fusion.5), channel_id=1, source_target_pairs={{0,8},{4,12},{8,0},{12,4},{16,24},{20,28},{24,16},{28,20},{1,9},{5... | collective-permute-start | bytes 9224 | tf_op jit(solution)/shard_map/ppermute | solution.py:532
  32.3 12.3 %collective-permute-start.4 = (bf16[128,1536]{1,0:T(8,128)(2,1)S(1)}, bf16[128,1536]{1,0:T(8,128)(2,1)S(1)}, u32[]{:S(2)}, u32[]{:S(2)}) collective-permute-start(bf16[128,1536]{1,0:T(8,128)(2,1)S(1)} %pad_maximum_fusion.rest_0_), channel_id=1, source_target_pairs={{0,4},{4,0},{8,12},{12,8},{16,20},{20,16},{24,28},{28,24},{1,5},{5... | collective-permute-start | bytes 1179656 | tf_op jit(solution)/shard_map/ppermute | solution.py:532
  33.8 13.0 %collective-permute-start.7 = (bf16[128,1536]{1,0:T(8,128)(2,1)S(1)}, bf16[128,1536]{1,0:T(8,128)(2,1)S(1)}, u32[]{:S(2)}, u32[]{:S(2)}) collective-permute-start(bf16[128,1536]{1,0:T(8,128)(2,1)S(1)} %pad_maximum_fusion.rest_0_), channel_id=1, source_target_pairs={{0,1},{1,0},{2,3},{3,2},{4,5},{5,4},{6,7},{7,6},{8,9},{9,8},{10,11... | collective-permute-start | bytes 1179656 | tf_op jit(solution)/shard_map/ppermute | solution.py:532
  33.8 10.8 %collective-permute-start.6 = (bf16[4,6,128]{2,1,0:T(8,128)(2,1)S(1)}, bf16[4,6,128]{2,1,0:T(8,128)(2,1)S(1)}, u32[]{:S(2)}, u32[]{:S(2)}) collective-permute-start(bf16[4,6,128]{2,1,0:T(8,128)(2,1)S(1)} %pad_maximum_fusion.4), channel_id=1, source_target_pairs={{0,4},{4,0},{8,12},{12,8},{16,20},{20,16},{24,28},{28,24},{1,5},{5... | collective-permute-start | bytes 18440 | tf_op jit(solution)/shard_map/ppermute | solution.py:532
  34.4 5.1 %copy-start.3 = (bf16[8,14,14,512]{3,0,2,1:T(8,128)(2,1)S(1)}, bf16[8,14,14,512]{3,0,2,1:T(8,128)(2,1)}, u32[]{:S(2)}) copy-start(bf16[8,14,14,512]{3,0,2,1:T(8,128)(2,1)} %param.21) | copy-start | bytes 4816900
  39.6 1.8 copy-start.4
  44.6 2.3 copy-start.19
  44.8 2.1 collective-permute-start.8
  127.4 4.9 %collective-permute-start.9 = (bf16[2,2,2,2,16,4608]{5,4,3,2,1,0:T(8,128)(2,1)}, bf16[2,2,2,2,16,4608]{5,4,3,2,1,0:T(8,128)(2,1)S(1)}, u32[]{:S(2)}, u32[]{:S(2)}) collective-permute-start(bf16[2,2,2,2,16,4608]{5,4,3,2,1,0:T(8,128)(2,1)} %bitcast.140), channel_id=1, source_target_pairs={{0,1},{1,0},{2,3},{3,2},{4,5},{5,4},{6,7},{7,6},{8,9},{9,8},{10,11... | collective-permute-start | bytes 7077896 | tf_op jit(solution)/shard_map/ppermute | solution.py:532
  128.0 4.4 %copy-start.2 = (bf16[16,16,4608]{2,1,0:T(8,128)(2,1)S(1)}, bf16[16,16,4608]{2,1,0:T(8,128)(2,1)}, u32[]{:S(2)}) copy-start(bf16[16,16,4608]{2,1,0:T(8,128)(2,1)} %get-tuple-element.103) | copy-start | bytes 7077892
  133.0 35.0 %collective-permute-start.10 = (bf16[2,2,16,4608]{3,2,1,0:T(8,128)(2,1)S(1)}, bf16[2,2,16,4608]{3,2,1,0:T(8,128)(2,1)S(1)}, u32[]{:S(2)}, u32[]{:S(2)}) collective-permute-start(bf16[2,2,16,4608]{3,2,1,0:T(8,128)(2,1)S(1)} %get-tuple-element.108), channel_id=1, source_target_pairs={{0,2},{1,3},{2,0},{3,1},{4,6},{5,7},{6,4},{7,5},{8,10},{9,11},{10,... | collective-permute-start | bytes 1769480 | tf_op jit(solution)/shard_map/ppermute | solution.py:532
  134.3 33.8 %collective-permute-start.11 = (bf16[2,2,16,4608]{3,2,1,0:T(8,128)(2,1)S(1)}, bf16[2,2,16,4608]{3,2,1,0:T(8,128)(2,1)S(1)}, u32[]{:S(2)}, u32[]{:S(2)}) collective-permute-start(bf16[2,2,16,4608]{3,2,1,0:T(8,128)(2,1)S(1)} %get-tuple-element.109), channel_id=1, source_target_pairs={{0,4},{4,0},{8,12},{12,8},{16,20},{20,16},{24,28},{28,24},{1,5},{5... | collective-permute-start | bytes 1769480 | tf_op jit(solution)/shard_map/ppermute | solution.py:532
  136.8 31.3 %collective-permute-start.12 = (bf16[2,2,16,4608]{3,2,1,0:T(8,128)(2,1)S(1)}, bf16[2,2,16,4608]{3,2,1,0:T(8,128)(2,1)S(1)}, u32[]{:S(2)}, u32[]{:S(2)}) collective-permute-start(bf16[2,2,16,4608]{3,2,1,0:T(8,128)(2,1)S(1)} %get-tuple-element.110), channel_id=1, source_target_pairs={{0,6},{1,7},{2,4},{3,5},{4,2},{5,3},{6,0},{7,1},{8,14},{9,15},{10,... | collective-permute-start | bytes 1769480 | tf_op jit(solution)/shard_map/ppermute | solution.py:532
  168.3 7.7 %collective-permute-start.14 = (bf16[2,2,2,2,16,1536]{5,4,3,2,1,0:T(8,128)(2,1)}, bf16[2,2,2,2,16,1536]{5,4,3,2,1,0:T(8,128)(2,1)S(1)}, u32[]{:S(2)}, u32[]{:S(2)}) collective-permute-start(bf16[2,2,2,2,16,1536]{5,4,3,2,1,0:T(8,128)(2,1)} %bitcast.37), channel_id=1, source_target_pairs={{0,1},{1,0},{2,3},{3,2},{4,5},{5,4},{6,7},{7,6},{8,9},{9,8},{10,11... | collective-permute-start | bytes 2359304 | tf_op jit(solution)/shard_map/ppermute | solution.py:532
  168.7 7.4 %copy-start.6 = (bf16[16,16,1536]{2,1,0:T(8,128)(2,1)S(1)}, bf16[16,16,1536]{2,1,0:T(8,128)(2,1)}, u32[]{:S(2)}) copy-start(bf16[16,16,1536]{2,1,0:T(8,128)(2,1)} %get-tuple-element.118) | copy-start | bytes 2359300
  168.7 22.6 %collective-permute-start.13 = (bf16[2,16,4608]{2,1,0:T(8,128)(2,1)S(1)}, bf16[2,16,4608]{2,1,0:T(8,128)(2,1)S(1)}, u32[]{:S(2)}, u32[]{:S(2)}) collective-permute-start(bf16[2,16,4608]{2,1,0:T(8,128)(2,1)S(1)} %get-tuple-element.117), channel_id=1, source_target_pairs={{0,16},{4,20},{8,24},{12,28},{16,0},{20,4},{24,8},{28,12},{1,17},{... | collective-permute-start | bytes 884744 | tf_op jit(solution)/shard_map/ppermute | solution.py:532
  176.3 15.0 %collective-permute-start.15 = (bf16[2,2,2,16,1536]{4,3,2,1,0:T(8,128)(2,1)S(1)}, bf16[2,2,2,16,1536]{4,3,2,1,0:T(8,128)(2,1)S(1)}, u32[]{:S(2)}, u32[]{:S(2)}) collective-permute-start(bf16[2,2,2,16,1536]{4,3,2,1,0:T(8,128)(2,1)S(1)} %get-tuple-element.122), channel_id=1, source_target_pairs={{0,2},{1,3},{2,0},{3,1},{4,6},{5,7},{6,4},{7,5},{8,10},{9,11},{10,... | collective-permute-start | bytes 1179656 | tf_op jit(solution)/shard_map/ppermute | solution.py:532
  177.9 12.6 %copy-start.15 = (f32[16,176]{1,0:T(8,128)S(1)}, f32[16,176]{1,0:T(8,128)}, u32[]{:S(2)}) copy-start(f32[16,176]{1,0:T(8,128)} %shard_map.320) | copy-start | bytes 33796
  177.9 13.6 %copy-start.17 = (f32[1,2048]{1,0:T(1,128)S(1)}, f32[1,2048]{1,0:T(1,128)}, u32[]{:S(2)}) copy-start(f32[1,2048]{1,0:T(1,128)} %get-tuple-element.129) | copy-start | bytes 24580
  191.6 5.4 %collective-permute-start.17 = (bf16[16,4608]{1,0:T(8,128)(2,1)S(1)}, bf16[16,4608]{1,0:T(8,128)(2,1)S(1)}, u32[]{:S(2)}, u32[]{:S(2)}) collective-permute-start(bf16[16,4608]{1,0:T(8,128)(2,1)S(1)} %fusion.12), channel_id=1, source_target_pairs={{0,8},{4,12},{8,0},{12,4},{16,24},{20,28},{24,16},{28,20},{1,9},{5... | collective-permute-start | bytes 442376 | tf_op jit(solution)/shard_map/ppermute | solution.py:532
  192.3 1.2 collective-permute-start.18
  192.3 7.3 %collective-permute-start.16 = (bf16[2,2,16,1536]{3,2,1,0:T(8,128)(2,1)S(1)}, bf16[2,2,16,1536]{3,2,1,0:T(8,128)(2,1)S(1)}, u32[]{:S(2)}, u32[]{:S(2)}) collective-permute-start(bf16[2,2,16,1536]{3,2,1,0:T(8,128)(2,1)S(1)} %fusion.11), channel_id=1, source_target_pairs={{0,4},{4,0},{8,12},{12,8},{16,20},{20,16},{24,28},{28,24},{1,5},{5... | collective-permute-start | bytes 589832 | tf_op jit(solution)/shard_map/ppermute | solution.py:532
  199.7 12.7 %collective-permute-start.19 = (bf16[16,1536]{1,0:T(8,128)(2,1)S(1)}, bf16[16,1536]{1,0:T(8,128)(2,1)S(1)}, u32[]{:S(2)}, u32[]{:S(2)}) collective-permute-start(bf16[16,1536]{1,0:T(8,128)(2,1)S(1)} %get-tuple-element.149), channel_id=1, source_target_pairs={{0,8},{4,12},{8,0},{12,4},{16,24},{20,28},{24,16},{28,20},{1,9},{5... | collective-permute-start | bytes 147464 | tf_op jit(solution)/shard_map/ppermute | solution.py:532
  201.2 11.2 %collective-permute-start.20 = (bf16[16,1536]{1,0:T(8,128)(2,1)S(1)}, bf16[16,1536]{1,0:T(8,128)(2,1)S(1)}, u32[]{:S(2)}, u32[]{:S(2)}) collective-permute-start(bf16[16,1536]{1,0:T(8,128)(2,1)S(1)} %get-tuple-element.150), channel_id=1, source_target_pairs={{0,16},{4,20},{8,24},{12,28},{16,0},{20,4},{24,8},{28,12},{1,17},{... | collective-permute-start | bytes 147464 | tf_op jit(solution)/shard_map/ppermute | solution.py:532
  203.2 9.3 %collective-permute-start.21 = (bf16[16,1536]{1,0:T(8,128)(2,1)S(1)}, bf16[16,1536]{1,0:T(8,128)(2,1)S(1)}, u32[]{:S(2)}, u32[]{:S(2)}) collective-permute-start(bf16[16,1536]{1,0:T(8,128)(2,1)S(1)} %get-tuple-element.151), channel_id=1, source_target_pairs={{0,24},{4,28},{8,16},{12,20},{16,8},{20,12},{24,0},{28,4},{1,25},{... | collective-permute-start | bytes 147464 | tf_op jit(solution)/shard_map/ppermute | solution.py:532
  204.2 6.8 %collective-permute-start.23 = (f32[72,128]{1,0:T(8,128)S(1)}, f32[72,128]{1,0:T(8,128)S(1)}, u32[]{:S(2)}, u32[]{:S(2)}) collective-permute-start(f32[72,128]{1,0:T(8,128)S(1)} %add.373), channel_id=1, source_target_pairs={{0,2},{1,3},{2,0},{3,1},{4,6},{5,7},{6,4},{7,5},{8,10},{9,11},{10,... | collective-permute-start | bytes 110600 | tf_op jit(solution)/shard_map/ppermute | solution.py:532
  204.7 25.4 %copy-start.1 = (bf16[64,2048]{1,0:T(8,128)(2,1)S(1)}, bf16[64,2048]{1,0:T(8,128)(2,1)}, u32[]{:S(2)}) copy-start(bf16[64,2048]{1,0:T(8,128)(2,1)} %param.35) | copy-start | bytes 786436
  211.0 4.0 %collective-permute-start.22 = (bf16[16,4608]{1,0:T(8,128)(2,1)S(1)}, bf16[16,4608]{1,0:T(8,128)(2,1)S(1)}, u32[]{:S(2)}, u32[]{:S(2)}) collective-permute-start(bf16[16,4608]{1,0:T(8,128)(2,1)S(1)} %fusion.9), channel_id=1, source_target_pairs={{0,1},{1,0},{2,3},{3,2},{4,5},{5,4},{6,7},{7,6},{8,9},{9,8},{10,11... | collective-permute-start | bytes 442376 | tf_op jit(solution)/shard_map/ppermute | solution.py:532
  211.0 4.0 %collective-permute-start.24 = (f32[72,128]{1,0:T(8,128)S(1)}, f32[72,128]{1,0:T(8,128)S(1)}, u32[]{:S(2)}, u32[]{:S(2)}) collective-permute-start(f32[72,128]{1,0:T(8,128)S(1)} %add.377), channel_id=1, source_target_pairs={{0,4},{4,0},{8,12},{12,8},{16,20},{20,16},{24,28},{28,24},{1,5},{5... | collective-permute-start | bytes 110600 | tf_op jit(solution)/shard_map/ppermute | solution.py:532
  212.5 13.9 %copy-start.10 = (bf16[16,1536]{1,0:T(8,128)(2,1)}, bf16[16,1536]{1,0:T(8,128)(2,1)S(1)}, u32[]{:S(2)}) copy-start(bf16[16,1536]{1,0:T(8,128)(2,1)S(1)} %add_convert_fusion.12.refs_0_) | copy-start | bytes 147460
  215.1 11.3 %copy-start.5 = (bf16[2,16,4608]{2,1,0:T(8,128)(2,1)}, bf16[2,16,4608]{2,1,0:T(8,128)(2,1)S(1)}, u32[]{:S(2)}) copy-start(bf16[2,16,4608]{2,1,0:T(8,128)(2,1)S(1)} %pad_maximum_fusion.1.both_ref) | copy-start | bytes 884740
  215.1 5.3 %collective-permute-start.29 = (f32[72,128]{1,0:T(8,128)S(1)}, f32[72,128]{1,0:T(8,128)S(1)}, u32[]{:S(2)}, u32[]{:S(2)}) collective-permute-start(f32[72,128]{1,0:T(8,128)S(1)} %add.378), channel_id=1, source_target_pairs={{0,16},{4,20},{8,24},{12,28},{16,0},{20,4},{24,8},{28,12},{1,17},{... | collective-permute-start | bytes 110600 | tf_op jit(solution)/shard_map/ppermute | solution.py:532
  216.3 10.1 %collective-permute-start.25 = (bf16[2,16,4608]{2,1,0:T(8,128)(2,1)S(1)}, bf16[2,16,4608]{2,1,0:T(8,128)(2,1)S(1)}, u32[]{:S(2)}, u32[]{:S(2)}) collective-permute-start(bf16[2,16,4608]{2,1,0:T(8,128)(2,1)S(1)} %pad_maximum_fusion.1.both_ref), channel_id=1, source_target_pairs={{0,2},{1,3},{2,0},{3,1},{4,6},{5,7},{6,4},{7,5},{8,10},{9,11},{10,... | collective-permute-start | bytes 884744 | tf_op jit(solution)/shard_map/ppermute | solution.py:532
  220.4 4.0 %collective-permute-start.30 = (f32[72,128]{1,0:T(8,128)S(1)}, f32[72,128]{1,0:T(8,128)S(1)}, u32[]{:S(2)}, u32[]{:S(2)}) collective-permute-start(f32[72,128]{1,0:T(8,128)S(1)} %add.379), channel_id=1, source_target_pairs={{0,8},{4,12},{8,0},{12,4},{16,24},{20,28},{24,16},{28,20},{1,9},{5... | collective-permute-start | bytes 110600 | tf_op jit(solution)/shard_map/ppermute | solution.py:532
  221.5 3.6 %collective-permute-start.26 = (bf16[16,1536]{1,0:T(8,128)(2,1)S(1)}, bf16[16,1536]{1,0:T(8,128)(2,1)S(1)}, u32[]{:S(2)}, u32[]{:S(2)}) collective-permute-start(bf16[16,1536]{1,0:T(8,128)(2,1)S(1)} %add_convert_fusion.12.refs_0_), channel_id=1, source_target_pairs={{0,1},{1,0},{2,3},{3,2},{4,5},{5,4},{6,7},{7,6},{8,9},{9,8},{10,11... | collective-permute-start | bytes 147464 | tf_op jit(solution)/shard_map/ppermute | solution.py:532
  221.5 4.2 %collective-permute-start.27 = (bf16[16,1536]{1,0:T(8,128)(2,1)S(1)}, bf16[16,1536]{1,0:T(8,128)(2,1)S(1)}, u32[]{:S(2)}, u32[]{:S(2)}) collective-permute-start(bf16[16,1536]{1,0:T(8,128)(2,1)S(1)} %add_convert_fusion.12.refs_0_), channel_id=1, source_target_pairs={{0,2},{1,3},{2,0},{3,1},{4,6},{5,7},{6,4},{7,5},{8,10},{9,11},{10,... | collective-permute-start | bytes 147464 | tf_op jit(solution)/shard_map/ppermute | solution.py:532
  222.6 3.8 %collective-permute-start.28 = (bf16[16,1536]{1,0:T(8,128)(2,1)S(1)}, bf16[16,1536]{1,0:T(8,128)(2,1)S(1)}, u32[]{:S(2)}, u32[]{:S(2)}) collective-permute-start(bf16[16,1536]{1,0:T(8,128)(2,1)S(1)} %add_convert_fusion.12.refs_0_), channel_id=1, source_target_pairs={{0,3},{1,2},{2,1},{3,0},{4,7},{5,6},{6,5},{7,4},{8,11},{9,10},{10,... | collective-permute-start | bytes 147464 | tf_op jit(solution)/shard_map/ppermute | solution.py:532
  224.4 2.1 copy-start.9
  225.1 1.4 copy-start.11
  (6 other events, 4.3 us)
Sparse Core Ops, SparseCore 0:
  11.0 66.3 all-gather.1
